TPU v7x, 32 devices: a whole 2x2x4 slice. The times are simulated.
32 devices in a mesh: sx: 4 (over y, x), sy: 4 (over z), par: 2 (over core).
Axes of the slice: x: 2, y: 2, z: 4, core: 2. Of those that a mesh axis runs over, the one named last changes fastest.
Arguments:
- initial_state: float32 [64, 64, 64, 128], P('par', 'sx', 'sy'), may hold values from -6 to 6
- conductivity: float32 [64, 64, 64, 128], P('par', 'sx', 'sy'), may hold values from 0.1 to 1
- omega: bfloat16 [64, 64], replicated, may hold values from -0.75 to 0.75
- psi: bfloat16 [64, 64, 64, 128], P(None, 'sx', 'sy'), may hold values from -0.01171875 to 0.01171875
- range_prev: bfloat16 [64, 64, 64, 128], P('par', 'sx', 'sy'), may hold values from -3 to 3
- corange_prev: float32 [64, 64], P(None, 'par'), may hold values from -3 to 3
Outputs:
- final_state: float32 [64, 64, 64, 128], P('par', 'sx', 'sy')
- range_sketch: bfloat16 [64, 64, 64, 128], P('par', 'sx', 'sy')
- corange_sketch: float32 [64, 64], P(None, 'par')
All inputs are finite; a program needn't handle non-finite values.
Results may differ from a plain program's by a relative error of at most 0.0033.
Values may be sent and summed in bfloat16 or wider, within the bound.
No kernel may reach another device: no remote copies, remote signals or barrier semaphores. Data moves between devices by JAX's collectives and lax.ppermute only.
A program may use at most 192 MiB of HBM per device.

v0:
```python
import jax
import jax.numpy as jnp
from jax import lax
from jax.sharding import PartitionSpec as P

STEPS = 4


def extended(block, sides, width):
    for axis, dim in sides:
        count = lax.axis_size(axis)
        forward = [(i, i + 1) for i in range(count - 1)]
        backward = [(target, source) for source, target in forward]
        low = lax.ppermute(
            lax.slice_in_dim(block, block.shape[dim] - width, None, axis=dim), axis, forward
        )
        high = lax.ppermute(lax.slice_in_dim(block, 0, width, axis=dim), axis, backward)
        block = jnp.concatenate([low, block, high], axis=dim)
    return block


def advance(field, kpad):
    center = field[:, 1:-1, 1:-1, :]
    kcen = kpad[:, 1:-1, 1:-1, :]
    width_x = center.shape[1]
    width_y = center.shape[2]
    zfield = jnp.pad(center, ((0, 0), (0, 0), (0, 0), (1, 1)))
    zcond = jnp.pad(kcen, ((0, 0), (0, 0), (0, 0), (1, 1)))
    length = center.shape[3]
    pairs = [
        (field[:, 2:, 1:-1, :], kpad[:, 2:, 1:-1, :]),
        (field[:, :width_x, 1:-1, :], kpad[:, :width_x, 1:-1, :]),
        (field[:, 1:-1, 2:, :], kpad[:, 1:-1, 2:, :]),
        (field[:, 1:-1, :width_y, :], kpad[:, 1:-1, :width_y, :]),
        (zfield[:, :, :, 2:], zcond[:, :, :, 2:]),
        (zfield[:, :, :, :length], zcond[:, :, :, :length]),
    ]
    total = jnp.zeros_like(center)
    for unb, knb in pairs:
        total = total + 0.5 * (kcen + knb) * (unb - center)
    return center + 0.16 * total


def per_device(initial_state, conductivity, omega, psi, range_prev, corange_prev):
    samples, cells_x, cells_y, length = initial_state.shape
    kpad = extended(conductivity, (("sx", 1), ("sy", 2)), 1)
    state = initial_state
    for step in range(STEPS):
        field = extended(state, (("sx", 1), ("sy", 2)), 1)
        state = advance(field, kpad)
    snapshot = state.astype(jnp.bfloat16)
    flat_snap = snapshot.reshape(samples, cells_x * cells_y * length)
    rank = omega.shape[1]
    rank_dev = range_prev.shape[0]
    own_cols = lax.dynamic_slice_in_dim(omega, lax.axis_index("par") * rank_dev, rank_dev, 1)
    start_sum = range_prev.astype(jnp.float32)
    piece = lax.all_gather(snapshot, "par", axis=0, tiled=True)
    rows = piece.shape[0]
    term = lax.dot_general(
        own_cols,
        piece.reshape(rows, -1),
        (((0,), (0,)), ((), ())),
        preferred_element_type=jnp.float32,
    )
    range_sum = start_sum + term.reshape(start_sum.shape)
    range_sketch = range_sum.astype(jnp.bfloat16)
    flat_psi = psi.reshape(rank, cells_x * cells_y * length)
    partial_value = lax.dot_general(
        flat_psi, flat_snap, (((1,), (1,)), ((), ())), preferred_element_type=jnp.float32
    )
    corange_sketch = corange_prev + lax.psum(partial_value, ("sx", "sy"))
    return (state, range_sketch, corange_sketch)


def solution(mesh):
    in_specs = (
        P("par", "sx", "sy", None),
        P("par", "sx", "sy", None),
        P(),
        P(None, "sx", "sy", None),
        P("par", "sx", "sy", None),
        P(None, "par"),
    )
    out_specs = (P("par", "sx", "sy", None), P("par", "sx", "sy", None), P(None, "par"))
    return jax.shard_map(
        per_device, mesh=mesh, in_specs=in_specs, out_specs=out_specs, check_vma=False
    )
```

profile of v0, /device:TPU:0, one launch (start us, length us, event | category | flops | bytes accessed | tf_op | source)
XLA Modules:
  0.0 271.4 jit_solution(11380879610806708669)
XLA Ops:
  7.2 4.8 %copy.22 = f32[32,16,16,128]{3,0,2,1:T(8,128)S(1)} copy(f32[32,16,16,128]{3,2,1,0:T(8,128)} %param.7) | data formatting | bytes 8388608 | tf_op args[1]
  12.0 4.9 %collective-permute-start.2 = (f32[32,1,16,128]{3,0,2,1:T(8,128)S(1)}, f32[32,1,16,128]{3,0,2,1:T(8,128)S(1)}, u32[]{:S(2)}, u32[]{:S(2)}) collective-permute-start(f32[32,1,16,128]{3,0,2,1:T(8,128)S(1)} %get-tuple-element.30), channel_id=1, source_target_pairs={{0,8},{8,16},{16,24},{1,9},{9,17},{17,25},{2,10},{10,18},{18,26},{... | collective-permute-start | bytes 786440 | tf_op jit(solution)/shard_map/ppermute | solution.py:14
  16.9 1.6 collective-permute-start
  18.5 2.4 copy.44
  21.0 4.6 %collective-permute-start.3 = (f32[32,1,16,128]{3,0,2,1:T(8,128)S(1)}, f32[32,1,16,128]{3,0,2,1:T(8,128)S(1)}, u32[]{:S(2)}, u32[]{:S(2)}) collective-permute-start(f32[32,1,16,128]{3,0,2,1:T(8,128)S(1)} %get-tuple-element.33), channel_id=1, source_target_pairs={{0,8},{8,16},{16,24},{1,9},{9,17},{17,25},{2,10},{10,18},{18,26},{... | collective-permute-start | bytes 786440 | tf_op jit(solution)/shard_map/ppermute | solution.py:14
  25.6 1.3 collective-permute-start.1
  26.9 2.4 constant_dynamic-update-slice_fusion.1
  29.3 1.8 collective-permute-done
  31.2 1.3 collective-permute-start.4
  32.5 4.6 %collective-permute-start.6 = (f32[32,18,1,128]{3,0,2,1:T(8,128)S(1)}, f32[32,18,1,128]{3,0,2,1:T(8,128)S(1)}, u32[]{:S(2)}, u32[]{:S(2)}) collective-permute-start(f32[32,18,1,128]{3,0,2,1:T(8,128)S(1)} %get-tuple-element.20), channel_id=1, source_target_pairs={{0,2},{2,4},{4,6},{1,3},{3,5},{5,7},{8,10},{10,12},{12,14},{9,11},... | collective-permute-start | bytes 884744 | tf_op jit(solution)/shard_map/ppermute | solution.py:14
  37.8 4.4 %constant_dynamic-update-slice_fusion.4 = f32[32,18,16,128]{3,0,2,1:T(8,128)} fusion(f32[32,18,16,128]{3,0,2,1:T(8,128)} %constant_dynamic-update-slice_fusion.5, f32[32,16,16,128]{3,2,1,0:T(8,128)S(1)} %copy-done.2), kind=kLoop, calls=%fused_computation.152 | loop fusion | bytes 8388608
  44.1 1.3 collective-permute-start.5
  45.4 4.7 %collective-permute-start.7 = (f32[32,18,1,128]{3,0,2,1:T(8,128)S(1)}, f32[32,18,1,128]{3,0,2,1:T(8,128)S(1)}, u32[]{:S(2)}, u32[]{:S(2)}) collective-permute-start(f32[32,18,1,128]{3,0,2,1:T(8,128)S(1)} %get-tuple-element.23), channel_id=1, source_target_pairs={{0,2},{2,4},{4,6},{1,3},{3,5},{5,7},{8,10},{10,12},{12,14},{9,11},... | collective-permute-start | bytes 884744 | tf_op jit(solution)/shard_map/ppermute | solution.py:14
  50.1 2.7 %collective-permute-done.5 = f32[32,18,1,128]{3,0,2,1:T(8,128)S(1)} collective-permute-done((f32[32,18,1,128]{3,0,2,1:T(8,128)S(1)}, f32[32,18,1,128]{3,0,2,1:T(8,128)S(1)}, u32[]{:S(2)}, u32[]{:S(2)}) %collective-permute-start.5) | collective-permute-done | bytes 294944 | tf_op jit(solution)/shard_map/ppermute | solution.py:17
  52.8 1.3 collective-permute-done.7
  54.1 10.3 %fusion.9 = f32[32,16,16,128]{3,0,2,1:T(8,128)S(1)} fusion(f32[32,16,16,128]{3,0,2,1:T(8,128)S(1)} %copy.44, f32[32,18,16,128]{3,0,2,1:T(8,128)} %constant_dynamic-update-slice_fusion.3, f32[32,18,1,128]{3,0,2,1:T(8,128)S(1)} %collective-permute-done.7, f32[32,18,1,128]{3,0,2,1:T(8,128)S(1)} %collective-permute-done.5, ...), kind=kLoop, calls=%fused_computation.19 | loop fusion | flops 40894464 | bytes 24248320 | tf_op jit(solution)/shard_map/add | solution.py:41
  64.5 1.3 collective-permute-start.8
  65.8 4.6 %collective-permute-start.9 = (f32[32,1,16,128]{3,0,2,1:T(8,128)S(1)}, f32[32,1,16,128]{3,0,2,1:T(8,128)S(1)}, u32[]{:S(2)}, u32[]{:S(2)}) collective-permute-start(f32[32,1,16,128]{3,0,2,1:T(8,128)S(1)} %get-tuple-element.28), channel_id=1, source_target_pairs={{0,8},{8,16},{16,24},{1,9},{9,17},{17,25},{2,10},{10,18},{18,26},{... | collective-permute-start | bytes 786440 | tf_op jit(solution)/shard_map/ppermute | solution.py:14
  70.3 5.1 %collective-permute-done.8 = f32[32,1,16,128]{3,0,2,1:T(8,128)S(1)} collective-permute-done((f32[32,1,16,128]{3,0,2,1:T(8,128)S(1)}, f32[32,1,16,128]{3,0,2,1:T(8,128)S(1)}, u32[]{:S(2)}, u32[]{:S(2)}) %collective-permute-start.8) | collective-permute-done | bytes 262176 | tf_op jit(solution)/shard_map/ppermute | solution.py:17
  75.5 1.3 collective-permute-start.10
  76.8 5.0 %collective-permute-start.11 = (f32[32,18,1,128]{3,0,2,1:T(8,128)S(1)}, f32[32,18,1,128]{3,0,2,1:T(8,128)S(1)}, u32[]{:S(2)}, u32[]{:S(2)}) collective-permute-start(f32[32,18,1,128]{3,0,2,1:T(8,128)S(1)} %get-tuple-element.19), channel_id=1, source_target_pairs={{0,2},{2,4},{4,6},{1,3},{3,5},{5,7},{8,10},{10,12},{12,14},{9,11},... | collective-permute-start | bytes 884744 | tf_op jit(solution)/shard_map/ppermute | solution.py:14
  81.9 2.7 %collective-permute-done.10 = f32[32,18,1,128]{3,0,2,1:T(8,128)S(1)} collective-permute-done((f32[32,18,1,128]{3,0,2,1:T(8,128)S(1)}, f32[32,18,1,128]{3,0,2,1:T(8,128)S(1)}, u32[]{:S(2)}, u32[]{:S(2)}) %collective-permute-start.10) | collective-permute-done | bytes 294944 | tf_op jit(solution)/shard_map/ppermute | solution.py:17
  84.6 1.5 collective-permute-done.11
  86.1 8.1 %fusion.17 = f32[32,16,16,128]{3,0,2,1:T(8,128)S(1)} fusion(f32[32,16,16,128]{3,0,2,1:T(8,128)S(1)} %fusion.9, f32[32,18,1,128]{3,0,2,1:T(8,128)S(1)} %collective-permute-done.11, f32[32,1,16,128]{3,0,2,1:T(8,128)S(1)} %collective-permute-done.8, f32[32,1,16,128]{3,0,2,1:T(8,128)S(1)} %collective-permute-done.9, ...), kind=kLoop, calls=%fused_computation.27 | loop fusion | flops 45088768 | bytes 19529728 | tf_op jit(solution)/shard_map/add | solution.py:41
  94.2 1.3 collective-permute-start.12
  95.5 5.0 %collective-permute-start.13 = (f32[32,1,16,128]{3,0,2,1:T(8,128)S(1)}, f32[32,1,16,128]{3,0,2,1:T(8,128)S(1)}, u32[]{:S(2)}, u32[]{:S(2)}) collective-permute-start(f32[32,1,16,128]{3,0,2,1:T(8,128)S(1)} %get-tuple-element.26), channel_id=1, source_target_pairs={{0,8},{8,16},{16,24},{1,9},{9,17},{17,25},{2,10},{10,18},{18,26},{... | collective-permute-start | bytes 786440 | tf_op jit(solution)/shard_map/ppermute | solution.py:14
  100.5 4.4 %collective-permute-done.12 = f32[32,1,16,128]{3,0,2,1:T(8,128)S(1)} collective-permute-done((f32[32,1,16,128]{3,0,2,1:T(8,128)S(1)}, f32[32,1,16,128]{3,0,2,1:T(8,128)S(1)}, u32[]{:S(2)}, u32[]{:S(2)}) %collective-permute-start.12) | collective-permute-done | bytes 262176 | tf_op jit(solution)/shard_map/ppermute | solution.py:17
  104.9 1.3 collective-permute-start.14
  106.2 5.0 %collective-permute-start.15 = (f32[32,18,1,128]{3,0,2,1:T(8,128)S(1)}, f32[32,18,1,128]{3,0,2,1:T(8,128)S(1)}, u32[]{:S(2)}, u32[]{:S(2)}) collective-permute-start(f32[32,18,1,128]{3,0,2,1:T(8,128)S(1)} %get-tuple-element.17), channel_id=1, source_target_pairs={{0,2},{2,4},{4,6},{1,3},{3,5},{5,7},{8,10},{10,12},{12,14},{9,11},... | collective-permute-start | bytes 884744 | tf_op jit(solution)/shard_map/ppermute | solution.py:14
  111.3 2.7 %collective-permute-done.14 = f32[32,18,1,128]{3,0,2,1:T(8,128)S(1)} collective-permute-done((f32[32,18,1,128]{3,0,2,1:T(8,128)S(1)}, f32[32,18,1,128]{3,0,2,1:T(8,128)S(1)}, u32[]{:S(2)}, u32[]{:S(2)}) %collective-permute-start.14) | collective-permute-done | bytes 294944 | tf_op jit(solution)/shard_map/ppermute | solution.py:17
  114.0 1.5 collective-permute-done.15
  115.5 8.1 %fusion.25 = f32[32,16,16,128]{3,0,2,1:T(8,128)S(1)} fusion(f32[32,16,16,128]{3,0,2,1:T(8,128)S(1)} %fusion.17, f32[32,18,1,128]{3,0,2,1:T(8,128)S(1)} %collective-permute-done.15, f32[32,1,16,128]{3,0,2,1:T(8,128)S(1)} %collective-permute-done.12, f32[32,1,16,128]{3,0,2,1:T(8,128)S(1)} %collective-permute-done.13, ...), kind=kLoop, calls=%fused_computation.35 | loop fusion | flops 45088768 | bytes 19529728 | tf_op jit(solution)/shard_map/add | solution.py:41
  123.6 1.3 collective-permute-start.16
  124.9 5.9 %collective-permute-start.17 = (f32[32,1,16,128]{3,0,2,1:T(8,128)S(1)}, f32[32,1,16,128]{3,0,2,1:T(8,128)S(1)}, u32[]{:S(2)}, u32[]{:S(2)}) collective-permute-start(f32[32,1,16,128]{3,0,2,1:T(8,128)S(1)} %get-tuple-element.24), channel_id=1, source_target_pairs={{0,8},{8,16},{16,24},{1,9},{9,17},{17,25},{2,10},{10,18},{18,26},{... | collective-permute-start | bytes 786440 | tf_op jit(solution)/shard_map/ppermute | solution.py:14
  130.9 4.4 %collective-permute-done.16 = f32[32,1,16,128]{3,0,2,1:T(8,128)S(1)} collective-permute-done((f32[32,1,16,128]{3,0,2,1:T(8,128)S(1)}, f32[32,1,16,128]{3,0,2,1:T(8,128)S(1)}, u32[]{:S(2)}, u32[]{:S(2)}) %collective-permute-start.16) | collective-permute-done | bytes 262176 | tf_op jit(solution)/shard_map/ppermute | solution.py:17
  135.4 1.3 collective-permute-start.18
  136.7 5.0 %collective-permute-start.19 = (f32[32,18,1,128]{3,0,2,1:T(8,128)S(1)}, f32[32,18,1,128]{3,0,2,1:T(8,128)S(1)}, u32[]{:S(2)}, u32[]{:S(2)}) collective-permute-start(f32[32,18,1,128]{3,0,2,1:T(8,128)S(1)} %get-tuple-element.15), channel_id=1, source_target_pairs={{0,2},{2,4},{4,6},{1,3},{3,5},{5,7},{8,10},{10,12},{12,14},{9,11},... | collective-permute-start | bytes 884744 | tf_op jit(solution)/shard_map/ppermute | solution.py:14
  141.7 2.7 %collective-permute-done.18 = f32[32,18,1,128]{3,0,2,1:T(8,128)S(1)} collective-permute-done((f32[32,18,1,128]{3,0,2,1:T(8,128)S(1)}, f32[32,18,1,128]{3,0,2,1:T(8,128)S(1)}, u32[]{:S(2)}, u32[]{:S(2)}) %collective-permute-start.18) | collective-permute-done | bytes 294944 | tf_op jit(solution)/shard_map/ppermute | solution.py:17
  144.4 1.5 collective-permute-done.19
  145.9 9.7 %fusion.100 = (bf16[32,16,16,128]{3,0,2,1:T(8,128)(2,1)S(1)}, f32[32,16,16,128]{3,0,2,1:T(8,128)}) fusion(f32[32,16,16,128]{3,0,2,1:T(8,128)S(1)} %fusion.25, f32[32,16,16,128]{3,0,2,1:T(8,128)S(1)} %copy.22, f32[32,1,16,128]{3,0,2,1:T(8,128)S(1)} %collective-permute-done.16, f32[32,1,16,128]{3,0,2,1:T(8,128)S(1)} %collective-permute-done.17, ...), kind=kLoop, calls=%fused_computation.155 | loop fusion | flops 46137344 | bytes 21626880 | tf_op jit(solution)/shard_map/convert_element_type | solution.py:51
  155.6 2.1 copy.47
  157.8 6.8 %copy.50 = f32[32,16,16,128]{3,2,1,0:T(8,128)} copy(f32[32,16,16,128]{3,0,2,1:T(8,128)} %get-tuple-element.13) | data formatting | bytes 8388608
  164.6 3.8 %fusion.94 = f32[64,32]{0,1:T(8,128)S(1)} fusion(bf16[32,16,16,128]{3,0,2,1:T(8,128)(2,1)S(1)} %get-tuple-element.12, bf16[64,16,16,128]{3,2,1,0:T(8,128)(2,1)S(1)} %copy-done.5), kind=kOutput, calls=%fused_computation.136 | convolution fusion | flops 134217728 | bytes 6299648 | tf_op jit(solution)/shard_map/dot_general | solution.py:68
  168.3 82.9 %psum.7 = f32[64,32]{0,1:T(8,128)S(1)} all-reduce(f32[64,32]{0,1:T(8,128)S(1)} %fusion.94), channel_id=1, replica_groups=mesh['sx'=4,'sy'=4,'par'=2] {'sx','sy'}, use_global_device_ids=true, to_apply=%region_0.1 | all-reduce | flops 2048 | bytes 16384 | tf_op jit(solution)/shard_map/psum | solution.py:71
  251.9 4.9 %copy.69 = bf16[8,8,256,128]{3,1,2,0:T(8,128)(2,1)S(1)} copy(bf16[8,8,256,128]{3,2,1,0:T(8,128)(2,1)} %bitcast.27) | data formatting | bytes 8388608
  256.8 1.2 copy.56
  258.4 4.1 %add_convert_fusion = bf16[32,16,16,128]{3,0,2,1:T(8,128)(2,1)S(1)} fusion(bf16[16,16,128,64]{2,1,0,3:T(8,128)(2,1)S(1)} %bitcast.26, bf16[32,16,16,128]{3,2,1,0:T(8,128)(2,1)S(1)} %copy-done.3, bf16[64,64]{1,0:T(8,128)(2,1)S(1)} %copy-done, s32[]{:T(128)S(6)} %select_n.3), kind=kOutput, calls=%fused_computation.135 | convolution fusion | flops 137363456 | bytes 8396804 | tf_op jit(solution)/shard_map/dot_general | solution.py:59
  262.5 2.1 copy.51
  (38 shorter events, 4.0 us)
Async XLA Ops:
  7.2 250.8 %copy-start = (bf16[64,64]{1,0:T(8,128)(2,1)S(1)}, bf16[64,64]{1,0:T(8,128)(2,1)}, u32[]{:S(2)}) copy-start(bf16[64,64]{1,0:T(8,128)(2,1)} %param.8) | copy-start | bytes 24580
  7.2 244.7 %all-gather.2.cloned.1.call-start = ((), (), s32[]{:S(2)}) async-start(), calls=%async_computation | async-start | bytes 6291456 | tf_op jit(solution)/shard_map/all_gather | solution.py:57
  7.2 11.3 %copy-start.2 = (f32[32,16,16,128]{3,2,1,0:T(8,128)S(1)}, f32[32,16,16,128]{3,2,1,0:T(8,128)}, u32[]{:S(2)}) copy-start(f32[32,16,16,128]{3,2,1,0:T(8,128)} %param.6) | copy-start | bytes 12582916
  12.0 14.8 %collective-permute-start.2 = (f32[32,1,16,128]{3,0,2,1:T(8,128)S(1)}, f32[32,1,16,128]{3,0,2,1:T(8,128)S(1)}, u32[]{:S(2)}, u32[]{:S(2)}) collective-permute-start(f32[32,1,16,128]{3,0,2,1:T(8,128)S(1)} %get-tuple-element.30), channel_id=1, source_target_pairs={{0,8},{8,16},{16,24},{1,9},{9,17},{17,25},{2,10},{10,18},{18,26},{... | collective-permute-start | bytes 786440 | tf_op jit(solution)/shard_map/ppermute | solution.py:14
  16.9 10.0 %copy-start.1 = (f32[32,16,16,128]{3,2,1,0:T(8,128)S(1)}, f32[32,16,16,128]{3,2,1,0:T(8,128)}, u32[]{:S(2)}) copy-start(f32[32,16,16,128]{3,2,1,0:T(8,128)} %param.7) | copy-start | bytes 12582916
  16.9 14.2 %collective-permute-start = (f32[32,1,16,128]{3,0,2,1:T(8,128)S(1)}, f32[32,1,16,128]{3,0,2,1:T(8,128)S(1)}, u32[]{:S(2)}, u32[]{:S(2)}) collective-permute-start(f32[32,1,16,128]{3,0,2,1:T(8,128)S(1)} %get-tuple-element.31), channel_id=1, source_target_pairs={{8,0},{16,8},{24,16},{9,1},{17,9},{25,17},{10,2},{18,10},{26,18},{... | collective-permute-start | bytes 786440 | tf_op jit(solution)/shard_map/ppermute | solution.py:17
  21.0 16.1 %collective-permute-start.3 = (f32[32,1,16,128]{3,0,2,1:T(8,128)S(1)}, f32[32,1,16,128]{3,0,2,1:T(8,128)S(1)}, u32[]{:S(2)}, u32[]{:S(2)}) collective-permute-start(f32[32,1,16,128]{3,0,2,1:T(8,128)S(1)} %get-tuple-element.33), channel_id=1, source_target_pairs={{0,8},{8,16},{16,24},{1,9},{9,17},{17,25},{2,10},{10,18},{18,26},{... | collective-permute-start | bytes 786440 | tf_op jit(solution)/shard_map/ppermute | solution.py:14
  25.6 16.7 %collective-permute-start.1 = (f32[32,1,16,128]{3,0,2,1:T(8,128)S(1)}, f32[32,1,16,128]{3,0,2,1:T(8,128)S(1)}, u32[]{:S(2)}, u32[]{:S(2)}) collective-permute-start(f32[32,1,16,128]{3,0,2,1:T(8,128)S(1)} %get-tuple-element.32), channel_id=1, source_target_pairs={{8,0},{16,8},{24,16},{9,1},{17,9},{25,17},{10,2},{18,10},{26,18},{... | collective-permute-start | bytes 786440 | tf_op jit(solution)/shard_map/ppermute | solution.py:17
  31.2 18.9 %collective-permute-start.4 = (f32[32,18,1,128]{3,0,2,1:T(8,128)S(1)}, f32[32,18,1,128]{3,0,2,1:T(8,128)S(1)}, u32[]{:S(2)}, u32[]{:S(2)}) collective-permute-start(f32[32,18,1,128]{3,0,2,1:T(8,128)S(1)} %get-tuple-element.21), channel_id=1, source_target_pairs={{2,0},{4,2},{6,4},{3,1},{5,3},{7,5},{10,8},{12,10},{14,12},{11,9},... | collective-permute-start | bytes 884744 | tf_op jit(solution)/shard_map/ppermute | solution.py:17
  32.5 17.6 %collective-permute-start.6 = (f32[32,18,1,128]{3,0,2,1:T(8,128)S(1)}, f32[32,18,1,128]{3,0,2,1:T(8,128)S(1)}, u32[]{:S(2)}, u32[]{:S(2)}) collective-permute-start(f32[32,18,1,128]{3,0,2,1:T(8,128)S(1)} %get-tuple-element.20), channel_id=1, source_target_pairs={{0,2},{2,4},{4,6},{1,3},{3,5},{5,7},{8,10},{10,12},{12,14},{9,11},... | collective-permute-start | bytes 884744 | tf_op jit(solution)/shard_map/ppermute | solution.py:14
  44.1 8.8 %collective-permute-start.5 = (f32[32,18,1,128]{3,0,2,1:T(8,128)S(1)}, f32[32,18,1,128]{3,0,2,1:T(8,128)S(1)}, u32[]{:S(2)}, u32[]{:S(2)}) collective-permute-start(f32[32,18,1,128]{3,0,2,1:T(8,128)S(1)} %get-tuple-element.22), channel_id=1, source_target_pairs={{2,0},{4,2},{6,4},{3,1},{5,3},{7,5},{10,8},{12,10},{14,12},{11,9},... | collective-permute-start | bytes 884744 | tf_op jit(solution)/shard_map/ppermute | solution.py:17
  45.4 8.8 %collective-permute-start.7 = (f32[32,18,1,128]{3,0,2,1:T(8,128)S(1)}, f32[32,18,1,128]{3,0,2,1:T(8,128)S(1)}, u32[]{:S(2)}, u32[]{:S(2)}) collective-permute-start(f32[32,18,1,128]{3,0,2,1:T(8,128)S(1)} %get-tuple-element.23), channel_id=1, source_target_pairs={{0,2},{2,4},{4,6},{1,3},{3,5},{5,7},{8,10},{10,12},{12,14},{9,11},... | collective-permute-start | bytes 884744 | tf_op jit(solution)/shard_map/ppermute | solution.py:14
  64.5 11.0 %collective-permute-start.8 = (f32[32,1,16,128]{3,0,2,1:T(8,128)S(1)}, f32[32,1,16,128]{3,0,2,1:T(8,128)S(1)}, u32[]{:S(2)}, u32[]{:S(2)}) collective-permute-start(f32[32,1,16,128]{3,0,2,1:T(8,128)S(1)} %get-tuple-element.29), channel_id=1, source_target_pairs={{8,0},{16,8},{24,16},{9,1},{17,9},{25,17},{10,2},{18,10},{26,18},{... | collective-permute-start | bytes 786440 | tf_op jit(solution)/shard_map/ppermute | solution.py:17
  65.8 9.7 %collective-permute-start.9 = (f32[32,1,16,128]{3,0,2,1:T(8,128)S(1)}, f32[32,1,16,128]{3,0,2,1:T(8,128)S(1)}, u32[]{:S(2)}, u32[]{:S(2)}) collective-permute-start(f32[32,1,16,128]{3,0,2,1:T(8,128)S(1)} %get-tuple-element.28), channel_id=1, source_target_pairs={{0,8},{8,16},{16,24},{1,9},{9,17},{17,25},{2,10},{10,18},{18,26},{... | collective-permute-start | bytes 786440 | tf_op jit(solution)/shard_map/ppermute | solution.py:14
  75.5 9.1 %collective-permute-start.10 = (f32[32,18,1,128]{3,0,2,1:T(8,128)S(1)}, f32[32,18,1,128]{3,0,2,1:T(8,128)S(1)}, u32[]{:S(2)}, u32[]{:S(2)}) collective-permute-start(f32[32,18,1,128]{3,0,2,1:T(8,128)S(1)} %get-tuple-element.18), channel_id=1, source_target_pairs={{2,0},{4,2},{6,4},{3,1},{5,3},{7,5},{10,8},{12,10},{14,12},{11,9},... | collective-permute-start | bytes 884744 | tf_op jit(solution)/shard_map/ppermute | solution.py:17
  76.8 9.2 %collective-permute-start.11 = (f32[32,18,1,128]{3,0,2,1:T(8,128)S(1)}, f32[32,18,1,128]{3,0,2,1:T(8,128)S(1)}, u32[]{:S(2)}, u32[]{:S(2)}) collective-permute-start(f32[32,18,1,128]{3,0,2,1:T(8,128)S(1)} %get-tuple-element.19), channel_id=1, source_target_pairs={{0,2},{2,4},{4,6},{1,3},{3,5},{5,7},{8,10},{10,12},{12,14},{9,11},... | collective-permute-start | bytes 884744 | tf_op jit(solution)/shard_map/ppermute | solution.py:14
  94.2 10.7 %collective-permute-start.12 = (f32[32,1,16,128]{3,0,2,1:T(8,128)S(1)}, f32[32,1,16,128]{3,0,2,1:T(8,128)S(1)}, u32[]{:S(2)}, u32[]{:S(2)}) collective-permute-start(f32[32,1,16,128]{3,0,2,1:T(8,128)S(1)} %get-tuple-element.27), channel_id=1, source_target_pairs={{8,0},{16,8},{24,16},{9,1},{17,9},{25,17},{10,2},{18,10},{26,18},{... | collective-permute-start | bytes 786440 | tf_op jit(solution)/shard_map/ppermute | solution.py:17
  95.5 9.4 %collective-permute-start.13 = (f32[32,1,16,128]{3,0,2,1:T(8,128)S(1)}, f32[32,1,16,128]{3,0,2,1:T(8,128)S(1)}, u32[]{:S(2)}, u32[]{:S(2)}) collective-permute-start(f32[32,1,16,128]{3,0,2,1:T(8,128)S(1)} %get-tuple-element.26), channel_id=1, source_target_pairs={{0,8},{8,16},{16,24},{1,9},{9,17},{17,25},{2,10},{10,18},{18,26},{... | collective-permute-start | bytes 786440 | tf_op jit(solution)/shard_map/ppermute | solution.py:14
  104.9 9.1 %collective-permute-start.14 = (f32[32,18,1,128]{3,0,2,1:T(8,128)S(1)}, f32[32,18,1,128]{3,0,2,1:T(8,128)S(1)}, u32[]{:S(2)}, u32[]{:S(2)}) collective-permute-start(f32[32,18,1,128]{3,0,2,1:T(8,128)S(1)} %get-tuple-element.16), channel_id=1, source_target_pairs={{2,0},{4,2},{6,4},{3,1},{5,3},{7,5},{10,8},{12,10},{14,12},{11,9},... | collective-permute-start | bytes 884744 | tf_op jit(solution)/shard_map/ppermute | solution.py:17
  106.2 9.3 %collective-permute-start.15 = (f32[32,18,1,128]{3,0,2,1:T(8,128)S(1)}, f32[32,18,1,128]{3,0,2,1:T(8,128)S(1)}, u32[]{:S(2)}, u32[]{:S(2)}) collective-permute-start(f32[32,18,1,128]{3,0,2,1:T(8,128)S(1)} %get-tuple-element.17), channel_id=1, source_target_pairs={{0,2},{2,4},{4,6},{1,3},{3,5},{5,7},{8,10},{10,12},{12,14},{9,11},... | collective-permute-start | bytes 884744 | tf_op jit(solution)/shard_map/ppermute | solution.py:14
  123.6 11.7 %collective-permute-start.16 = (f32[32,1,16,128]{3,0,2,1:T(8,128)S(1)}, f32[32,1,16,128]{3,0,2,1:T(8,128)S(1)}, u32[]{:S(2)}, u32[]{:S(2)}) collective-permute-start(f32[32,1,16,128]{3,0,2,1:T(8,128)S(1)} %get-tuple-element.25), channel_id=1, source_target_pairs={{8,0},{16,8},{24,16},{9,1},{17,9},{25,17},{10,2},{18,10},{26,18},{... | collective-permute-start | bytes 786440 | tf_op jit(solution)/shard_map/ppermute | solution.py:17
  124.9 10.4 %collective-permute-start.17 = (f32[32,1,16,128]{3,0,2,1:T(8,128)S(1)}, f32[32,1,16,128]{3,0,2,1:T(8,128)S(1)}, u32[]{:S(2)}, u32[]{:S(2)}) collective-permute-start(f32[32,1,16,128]{3,0,2,1:T(8,128)S(1)} %get-tuple-element.24), channel_id=1, source_target_pairs={{0,8},{8,16},{16,24},{1,9},{9,17},{17,25},{2,10},{10,18},{18,26},{... | collective-permute-start | bytes 786440 | tf_op jit(solution)/shard_map/ppermute | solution.py:14
  135.4 9.1 %collective-permute-start.18 = (f32[32,18,1,128]{3,0,2,1:T(8,128)S(1)}, f32[32,18,1,128]{3,0,2,1:T(8,128)S(1)}, u32[]{:S(2)}, u32[]{:S(2)}) collective-permute-start(f32[32,18,1,128]{3,0,2,1:T(8,128)S(1)} %get-tuple-element.14), channel_id=1, source_target_pairs={{2,0},{4,2},{6,4},{3,1},{5,3},{7,5},{10,8},{12,10},{14,12},{11,9},... | collective-permute-start | bytes 884744 | tf_op jit(solution)/shard_map/ppermute | solution.py:17
  136.7 9.2 %collective-permute-start.19 = (f32[32,18,1,128]{3,0,2,1:T(8,128)S(1)}, f32[32,18,1,128]{3,0,2,1:T(8,128)S(1)}, u32[]{:S(2)}, u32[]{:S(2)}) collective-permute-start(f32[32,18,1,128]{3,0,2,1:T(8,128)S(1)} %get-tuple-element.15), channel_id=1, source_target_pairs={{0,2},{2,4},{4,6},{1,3},{3,5},{5,7},{8,10},{10,12},{12,14},{9,11},... | collective-permute-start | bytes 884744 | tf_op jit(solution)/shard_map/ppermute | solution.py:14
  157.8 6.8 %copy-start.5 = (bf16[64,16,16,128]{3,2,1,0:T(8,128)(2,1)S(1)}, bf16[64,16,16,128]{3,2,1,0:T(8,128)(2,1)}, u32[]{:S(2)}) copy-start(bf16[64,16,16,128]{3,2,1,0:T(8,128)(2,1)} %param.9) | copy-start | bytes 12582916
  164.6 86.7 %copy-start.4 = (f32[64,32]{0,1:T(8,128)S(1)}, f32[64,32]{0,1:T(8,128)}, u32[]{:S(2)}) copy-start(f32[64,32]{0,1:T(8,128)} %param.11) | copy-start | bytes 24580
  256.8 1.6 copy-start.3
Sparse Core Ops, SparseCore 0:
  157.9 20.3 all-gather.1
where the time goes:
time: 272 us; the launch traced here: 271 us
  blocking collectives  82.9 us (30%)
  starting transfers between devices  62.5 us (23%)
  other arithmetic  36.9 us (14%)
  local copies, waits for them, and re-layouts  34.4 us (13%)
  waiting for transfers between devices  32.4 us (12%)
  between operations  14.4 us (5%)
  matrix products  7.86 us (3%)
    psum x1, blocking collectives, per_device(): corange_sketch = corange_prev + lax.psum(partial_value, ('sx', 'sy'))  82.9 us
    ppermute x10, starting transfers between devices, extended(): lax.ppermute(lax.slice_in_dim(block, block.shape[dim] - width, None, axis...  49.3 us
    unnamed x22, local copies, waits for them, and re-layouts  30.2 us
    ppermute x10, waiting for transfers between devices, extended(): lax.ppermute(lax.slice_in_dim(block, 0, width, axis=dim), axis, backward)  26.7 us
    add x3, other arithmetic, advance(): return center + 0.16 * total  26.5 us
    ppermute x10, starting transfers between devices, extended(): lax.ppermute(lax.slice_in_dim(block, 0, width, axis=dim), axis, backward)  13.2 us
    convert_element_type x1, other arithmetic, per_device(): snapshot = state.astype(jnp.bfloat16)  9.73 us
    ppermute x10, waiting for transfers between devices, extended(): lax.ppermute(lax.slice_in_dim(block, block.shape[dim] - width, None, axis...  5.68 us
  transfers between devices with their start and end apart: 21, of which 12 were waited for; matrix products, arithmetic and copies ran while one was open for 8% of the time, Pallas kernels for 0%

commit v1 on v0

v1 whole, which is shorter than its diff:
```python
import functools

import jax
import jax.numpy as jnp
from jax import lax
from jax.experimental import pallas as pl
from jax.experimental.pallas import tpu as pltpu
from jax.sharding import PartitionSpec as P

STEPS = 4
BF = jnp.bfloat16
F32 = jnp.float32
HALF = 0.16 * 0.5


def vmem_call(kernel, outs, name, limit=8 << 20, scratch=(), hbm_in=(), hbm_out=(), flops=0, nbytes=0):
    def call(*args):
        in_specs = []
        ready = []
        for i, arg in enumerate(args):
            if i in hbm_in:
                in_specs.append(pl.BlockSpec(memory_space=pl.ANY))
                ready.append(arg)
            else:
                in_specs.append(pl.BlockSpec(memory_space=pltpu.VMEM))
                ready.append(pltpu.with_memory_space_constraint(arg, pltpu.VMEM))
        out_shape = []
        out_specs = []
        for i, (shape, dtype) in enumerate(outs):
            if i in hbm_out:
                out_shape.append(jax.ShapeDtypeStruct(shape, dtype))
                out_specs.append(pl.BlockSpec(memory_space=pl.ANY))
            else:
                out_shape.append(pltpu.VMEM(shape, dtype))
                out_specs.append(pl.BlockSpec(memory_space=pltpu.VMEM))
        return pl.pallas_call(
            kernel,
            out_shape=out_shape,
            in_specs=in_specs,
            out_specs=out_specs,
            scratch_shapes=list(scratch),
            name=name,
            compiler_params=pltpu.CompilerParams(vmem_limit_bytes=limit),
            cost_estimate=pl.CostEstimate(flops=flops, bytes_accessed=nbytes, transcendentals=0),
        )(*ready)

    return call


def row_of(ref, s, x):
    return ref[s, pl.ds(x, 1), :]


def merged(u_ref, faces, s, x, row):
    if faces is None:
        return u_ref[s, x]
    fx0, fx1, fy0, fy1 = faces
    last = u_ref.shape[1] - 1
    if x == 0:
        return fx0[s]
    if x == last:
        return fx1[s]
    value = u_ref[s, x]
    value = jnp.where(row == 0, row_of(fy0, s, x), value)
    return jnp.where(row == u_ref.shape[2] - 1, row_of(fy1, s, x), value)


def step_body(u_ref, k_ref, faces, w_ref, wfx0, wfx1, wfy0, wfy1):
    samples, nx, ny, nz = u_ref.shape
    row = lax.broadcasted_iota(jnp.int32, (ny, nz), 0)
    lane = lax.broadcasted_iota(jnp.int32, (ny, nz), 1)
    y_open = row < ny - 1
    z_open = lane < nz - 1
    z_edge = (lane == 0) | (lane == nz - 1)

    def body(s, carry):
        u = merged(u_ref, faces, s, 0, row)
        k = k_ref[s, 0] * HALF
        flux_low = None
        for x in range(nx):
            total = u
            if x + 1 < nx:
                u_next = merged(u_ref, faces, s, x + 1, row)
                k_next = k_ref[s, x + 1] * HALF
                flux = (k + k_next) * (u_next - u)
                total = total + flux
            if flux_low is not None:
                total = total - flux_low
            fy = (k + pltpu.roll(k, ny - 1, 0)) * (pltpu.roll(u, ny - 1, 0) - u)
            fy = jnp.where(y_open, fy, 0.0)
            total = total + fy - pltpu.roll(fy, 1, 0)
            fz = (k + pltpu.roll(k, nz - 1, 1)) * (pltpu.roll(u, nz - 1, 1) - u)
            fz = jnp.where(z_open, fz, 0.0)
            total = total + fz - pltpu.roll(fz, 1, 1)
            total = total - jnp.where(z_edge, k * u, 0.0)
            w_ref[s, x] = total
            if x == 0:
                wfx0[s] = total
            if x == nx - 1:
                wfx1[s] = total
            wfy0[s, pl.ds(x, 1), :] = total[0:1]
            wfy1[s, pl.ds(x, 1), :] = total[ny - 1 : ny]
            if x + 1 < nx:
                u, k, flux_low = u_next, k_next, flux
        return carry

    lax.fori_loop(0, samples, body, 0)


def first_kernel(u_ref, k_ref, w_ref, wfx0, wfx1, wfy0, wfy1):
    step_body(u_ref, k_ref, None, w_ref, wfx0, wfx1, wfy0, wfy1)


def step_kernel(u_ref, k_ref, fx0, fx1, fy0, fy1, w_ref, wfx0, wfx1, wfy0, wfy1):
    step_body(u_ref, k_ref, (fx0, fx1, fy0, fy1), w_ref, wfx0, wfx1, wfy0, wfy1)


def final_kernel(w_ref, fx0, fx1, fy0, fy1, out_ref, snap_ref, buf, sem):
    samples, nx, ny, nz = w_ref.shape
    row = lax.broadcasted_iota(jnp.int32, (ny, nz), 0)

    def copy_of(s):
        return pltpu.make_async_copy(buf.at[s], out_ref.at[s], sem.at[s])

    def body(s, carry):
        for x in range(nx):
            value = merged(w_ref, (fx0, fx1, fy0, fy1), s, x, row)
            buf[s, x] = value
            snap_ref[s, x] = value.astype(BF)
        copy_of(s).start()
        return carry

    lax.fori_loop(0, samples, body, 0)

    def finish(s, carry):
        copy_of(s).wait()
        return carry

    lax.fori_loop(0, samples, finish, 0)


def columns(ref, x, width):
    samples, _, ny, nz = ref.shape
    parts = [ref[:, x + i].reshape(samples * ny, nz) for i in range(width)]
    return jnp.concatenate(parts, axis=1)


def range_kernel(w_own_ref, w_other_ref, own_ref, other_ref, prev_ref, out_ref):
    ranks, nx, ny, nz = prev_ref.shape
    for x in range(0, nx, 2):
        value = jnp.dot(w_own_ref[...], columns(own_ref, x, 2), preferred_element_type=F32)
        value += jnp.dot(w_other_ref[...], columns(other_ref, x, 2), preferred_element_type=F32)
        for i in range(2):
            part = value[:, i * nz : (i + 1) * nz].reshape(ranks, ny, nz)
            out_ref[:, x + i] = (part + prev_ref[:, x + i].astype(F32)).astype(BF)


def corange_kernel(psi_ref, snap_ref, out_ref, acc):
    ranks, nx, ny, nz = psi_ref.shape
    samples = snap_ref.shape[0]
    cols = samples * ny
    acc[...] = jnp.zeros_like(acc)
    for x in range(0, nx, 2):
        left = columns(psi_ref, x, 2)
        right = columns(snap_ref, x, 2)
        acc[...] += lax.dot_general(left, right, (((1,), (1,)), ((), ())), preferred_element_type=F32)
    row = lax.broadcasted_iota(jnp.int32, (ny, cols), 0)
    col = lax.broadcasted_iota(jnp.int32, (ny, cols), 1) % ny
    same = row == col
    fold = (
        lax.broadcasted_iota(jnp.int32, (cols, samples), 0) // ny
        == lax.broadcasted_iota(jnp.int32, (cols, samples), 1)
    ).astype(F32)
    picked = jnp.where(same[None], acc[...].reshape(ranks, ny, cols), 0.0).sum(1)
    out_ref[...] = jnp.dot(picked, fold, precision=lax.Precision.HIGHEST, preferred_element_type=F32)


def swap_pairs(count, parity, par):
    partner = {}
    for i in range(parity, count - 1, 2):
        partner[i] = i + 1
        partner[i + 1] = i
    pairs = []
    for i in range(count):
        for p in range(par):
            source = i * par + p
            if i in partner:
                pairs.append((source, partner[i] * par + p))
            else:
                pairs.append((source, i * par + (p + 1) % par))
    return pairs


def exchange(low, high, axis):
    count, par = lax.axis_size(axis), lax.axis_size("par")
    index = lax.axis_index(axis)
    odd = index % 2 == 1
    first = lax.ppermute(jnp.where(odd, low, high), (axis, "par"), swap_pairs(count, 0, par))
    second = lax.ppermute(jnp.where(odd, high, low), (axis, "par"), swap_pairs(count, 1, par))
    zero = jnp.zeros_like(first)
    below = jnp.where(index == 0, zero, jnp.where(odd, first, second))
    above = jnp.where(index == count - 1, zero, jnp.where(odd, second, first))
    return below, above


def add_fluxes(base, state, coefs, halos):
    dx0, dx1, dy0, dy1 = (c * (h.astype(F32) - u) for c, h, u in zip(coefs, halos, state))
    fx0, fx1, fy0, fy1 = base
    ny, nx = fx0.shape[1], fy0.shape[1]
    yrow = lax.broadcasted_iota(jnp.int32, fx0.shape, 1)
    xrow = lax.broadcasted_iota(jnp.int32, fy0.shape, 1)

    def at_ends(index, count, low, high):
        return jnp.where(index == 0, low, 0.0) + jnp.where(index == count - 1, high, 0.0)

    return (
        fx0 + dx0 + at_ends(yrow, ny, dy0[:, :1], dy1[:, :1]),
        fx1 + dx1 + at_ends(yrow, ny, dy0[:, -1:], dy1[:, -1:]),
        fy0 + dy0 + at_ends(xrow, nx, dx0[:, :1], dx1[:, :1]),
        fy1 + dy1 + at_ends(xrow, nx, dx0[:, -1:], dx1[:, -1:]),
    )


def faces_of(block):
    return block[:, 0], block[:, -1], block[:, :, 0], block[:, :, -1]


def spread(block, ny):
    rows, cols = block.shape
    up = (jnp.arange(rows * ny)[:, None] // ny == jnp.arange(rows)[None, :]).astype(BF)
    across = (jnp.arange(cols)[:, None] == jnp.arange(cols * ny)[None, :] // ny).astype(BF)
    full = jnp.dot(jnp.dot(up, block), across)
    same = jnp.arange(rows * ny)[:, None] % ny == jnp.arange(cols * ny)[None, :] % ny
    return jnp.where(same, full, jnp.zeros_like(full))


def total_of(value, axis):
    count = lax.axis_size(axis)
    stride = 1
    while stride < count:
        value = value + lax.ppermute(value, axis, [(i, i ^ stride) for i in range(count)])
        stride *= 2
    return value


def per_device(initial_state, conductivity, omega, psi, range_prev, corange_prev):
    samples, nx, ny, nz = initial_state.shape
    ranks = psi.shape[0]
    cells = samples * nx * ny * nz
    par = lax.axis_index("par")
    par_size = lax.axis_size("par")

    kfaces = faces_of(conductivity)
    ufaces = faces_of(initial_state)
    sent = [jnp.concatenate([k.astype(BF), u.astype(BF)], axis=0) for k, u in zip(kfaces, ufaces)]
    got = exchange(sent[0], sent[1], "sx") + exchange(sent[2], sent[3], "sy")
    coefs = tuple(HALF * (k + g[:samples].astype(F32)) for k, g in zip(kfaces, got))
    halos = tuple(g[samples:] for g in got)

    face_shape_x, face_shape_y = (samples, ny, nz), (samples, nx, nz)
    step_outs = [((samples, nx, ny, nz), F32)] + [(face_shape_x, F32)] * 2 + [(face_shape_y, F32)] * 2
    cost = dict(flops=24 * cells, nbytes=12 * cells)
    state = initial_state
    faces = None
    for step in range(STEPS):
        if step == 0:
            out = vmem_call(first_kernel, step_outs, "first_step", **cost)(state, conductivity)
        else:
            sent = [f.astype(BF) for f in faces]
            halos = exchange(sent[0], sent[1], "sx") + exchange(sent[2], sent[3], "sy")
            out = vmem_call(step_kernel, step_outs, "later_step", **cost)(state, conductivity, *faces)
        state = out[0]
        old = ufaces if faces is None else faces
        faces = add_fluxes(out[1:], old, coefs, halos)

    final_state, snapshot = vmem_call(
        final_kernel,
        [((samples, nx, ny, nz), F32), ((samples, nx, ny, nz), BF)],
        "final",
        scratch=[pltpu.VMEM((samples, nx, ny, nz), F32), pltpu.SemaphoreType.DMA((samples,))],
        limit=16 << 20,
        hbm_out=(0,),
        flops=cells,
        nbytes=10 * cells,
    )(state, *faces)

    other = lax.ppermute(snapshot, "par", [(i, (i + 1) % par_size) for i in range(par_size)])
    own_ranks = range_prev.shape[0]
    own_cols = lax.dynamic_slice_in_dim(omega, par * own_ranks, own_ranks, 1)
    own_rows = lax.dynamic_slice_in_dim(own_cols, par * samples, samples, 0)
    source = (par + par_size - 1) % par_size
    other_rows = lax.dynamic_slice_in_dim(own_cols, source * samples, samples, 0)
    w_own, w_other = spread(own_rows.T, ny), spread(other_rows.T, ny)

    partial_sum = vmem_call(
        corange_kernel,
        [((ranks, samples), F32)],
        "corange",
        scratch=[pltpu.VMEM((ranks * ny, samples * ny), F32)],
        limit=32 << 20,
        flops=2 * ranks * cells * ny,
        nbytes=4 * cells,
    )(psi, snapshot)[0]
    corange = corange_prev + total_of(total_of(partial_sum, "sx"), "sy")

    range_sketch = vmem_call(
        range_kernel,
        [(range_prev.shape, BF)],
        "range",
        limit=32 << 20,
        flops=4 * ranks * cells * ny,
        nbytes=8 * cells,
    )(w_own, w_other, snapshot, other, range_prev)[0]
    return final_state, range_sketch, corange


def solution(mesh):
    in_specs = (
        P("par", "sx", "sy", None),
        P("par", "sx", "sy", None),
        P(),
        P(None, "sx", "sy", None),
        P("par", "sx", "sy", None),
        P(None, "par"),
    )
    out_specs = (P("par", "sx", "sy", None), P("par", "sx", "sy", None), P(None, "par"))
    return jax.shard_map(
        per_device, mesh=mesh, in_specs=in_specs, out_specs=out_specs, check_vma=False
    )
```

time: 272 us -> 95 us (0.35)
  blocking collectives: 82.9 us -> 0 us
  Pallas kernels: 0 us -> 41.3 us
  starting transfers between devices: 62.5 us -> 23.3 us
  other arithmetic: 36.9 us -> 2.92 us
  local copies, waits for them, and re-layouts: 34.4 us -> 13.5 us
  waiting for transfers between devices: 32.4 us -> 11.5 us
  between operations: 14.4 us -> 1.25 us
  matrix products: 7.86 us -> 0.95 us
    psum x1 -> x0, blocking collectives: 82.9 us -> none  [per_device(): corange_sketch = corange_prev + lax.psum(partial_value, ('sx', 'sy'))]
    pallas_call x0 -> x7, Pallas kernels: none -> 41.3 us  [call(): pl.pallas_call(kernel, out_shape=out_shape, in_specs=in_specs, out_specs=...]
    ppermute x20 -> x21, starting transfers between devices: 62.5 us -> 23.3 us  [the longest x8 16.8 us: exchange(): lax.ppermute(jnp.where(odd, low, high), (axis, 'par'), swap_pairs(count,...]
    add x4 -> x6, other arithmetic: 27.1 us -> 0.46 us  [the longest x1 0.26 us: add_fluxes(): fy0 + dy0 + at_ends(xrow, nx, dx0[:, :1], dx1[:, :1])]
    unnamed x22 -> x17, local copies, waits for them, and re-layouts: 30.2 us -> 6.49 us
    ppermute x20 -> x21, waiting for transfers between devices: 32.4 us -> 11.5 us  [the longest x4 11.4 us: total_of(): lax.ppermute(value, axis, [(i, i ^ stride) for i in range(count)])]
    convert_element_type x1 -> x4, other arithmetic: 9.73 us -> 0.08 us  [the longest x2 0.04 us: per_device(): u.astype(BF)]
    dot_general x2, matrix products: 7.86 us -> 0.95 us  [spread(): full = jnp.dot(jnp.dot(up, block), across)]
  transfers between devices with their start and end apart: 21 -> 21, of which waited for: 12 -> 4; matrix products, arithmetic and copies ran while one was open for 8% -> 9% of each run, Pallas kernels for 0% -> 35%
where the time goes in v1:
time: 95 us; the launch traced here: 94.8 us
  Pallas kernels  41.3 us (43%)
  starting transfers between devices  23.3 us (25%)
  local copies, waits for them, and re-layouts  13.5 us (14%)
  waiting for transfers between devices  11.5 us (12%)
  other arithmetic  2.92 us (3%)
  between operations  1.25 us (1%)
    pallas_call x7, Pallas kernels, call(): pl.pallas_call(kernel, out_shape=out_shape, in_specs=in_specs, out_specs=...  41.3 us
    ppermute x8, starting transfers between devices, exchange(): lax.ppermute(jnp.where(odd, low, high), (axis, 'par'), swap_pairs(count,...  16.8 us
    ppermute x4, waiting for transfers between devices, total_of(): lax.ppermute(value, axis, [(i, i ^ stride) for i in range(count)])  11.4 us
    unnamed x17, local copies, waits for them, and re-layouts  6.49 us
    slice x2, local copies, waits for them, and re-layouts, faces_of(): return (block[:, 0], block[:, -1], block[:, :, 0], block[:, :, -1])  5.33 us
    ppermute x4, starting transfers between devices, total_of(): lax.ppermute(value, axis, [(i, i ^ stride) for i in range(count)])  4.08 us
  transfers between devices with their start and end apart: 21, of which 4 were waited for; matrix products, arithmetic and copies ran while one was open for 9% of the time, Pallas kernels for 35%

profile of v1, /device:TPU:0, one launch (start us, length us, event | category | flops | bytes accessed | tf_op | source)
XLA Modules:
  0.0 94.8 jit_solution(12470501198509917560)
XLA Ops:
  0.7 1.3 %bitcast_convert_fusion.2 = (bf16[32,16,128]{2,1,0:T(8,128)(2,1)S(1)}, bf16[32,16,128]{2,1,0:T(8,128)(2,1)S(1)}, bf16[32,16,128]{2,1,0:T(8,128)(2,1)S(1)}, bf16[32,16,128]{2,1,0:T(8,128)(2,1)S(1)}) fusion(f32[32,16,16,128]{3,2,1,0:T(8,128)} %u_ref.1, f32[32,16,16,128]{3,2,1,0:T(8,128)} %k_ref.7), kind=kLoop, calls=%fused_computation.15 | loop fusion | bytes 1048576 | tf_op jit(solution)/shard_map/convert_element_type | solution.py:255
  2.0 3.0 %collective-permute-start = (bf16[64,16,128]{2,1,0:T(8,128)(2,1)S(1)}, bf16[64,16,128]{2,1,0:T(8,128)(2,1)S(1)}, u32[]{:S(2)}, u32[]{:S(2)}) collective-permute-start(bf16[64,16,128]{2,1,0:T(8,128)(2,1)S(1)} %get-tuple-element.100), channel_id=1, source_target_pairs={{0,8},{1,9},{8,0},{9,1},{16,24},{17,25},{24,16},{25,17},{2,10},{3,... | collective-permute-start | bytes 786440 | tf_op jit(solution)/shard_map/ppermute | solution.py:198
  5.0 2.7 %fusion.24 = (f32[32,16,1,128]{3,2,1,0:T(1,128)S(1)}, f32[32,16,1,128]{3,2,1,0:T(1,128)S(1)}) fusion(f32[32,16,16,128]{3,2,1,0:T(8,128)} %u_ref.1), kind=kLoop, calls=%fused_computation.94 | loop fusion | bytes 1048576 | tf_op jit(solution)/shard_map/slice | solution.py:225
  7.7 2.7 %fusion.23 = (f32[32,16,1,128]{3,2,1,0:T(1,128)S(1)}, f32[32,16,1,128]{3,2,1,0:T(1,128)S(1)}) fusion(f32[32,16,16,128]{3,2,1,0:T(8,128)} %k_ref.7), kind=kLoop, calls=%fused_computation.93 | loop fusion | bytes 1048576 | tf_op jit(solution)/shard_map/slice | solution.py:225
  10.5 0.6 collective-permute-start.3
  11.1 2.6 %collective-permute-start.2 = (bf16[64,16,128]{2,1,0:T(8,128)(2,1)S(1)}, bf16[64,16,128]{2,1,0:T(8,128)(2,1)S(1)}, u32[]{:S(2)}, u32[]{:S(2)}) collective-permute-start(bf16[64,16,128]{2,1,0:T(8,128)(2,1)S(1)} %get-tuple-element.97), channel_id=1, source_target_pairs={{0,2},{1,3},{2,0},{3,1},{4,6},{5,7},{6,4},{7,5},{8,10},{9,11},{10,... | collective-permute-start | bytes 786440 | tf_op jit(solution)/shard_map/ppermute | solution.py:198
  13.8 2.2 %copy-done.1 = f32[32,16,16,128]{3,2,1,0:T(8,128)S(1)} copy-done((f32[32,16,16,128]{3,2,1,0:T(8,128)S(1)}, f32[32,16,16,128]{3,2,1,0:T(8,128)}, u32[]{:S(2)}) %copy-start.1) | copy-done | bytes 4194328
  16.0 2.2 %copy-done.3 = f32[32,16,16,128]{3,2,1,0:T(8,128)S(1)} copy-done((f32[32,16,16,128]{3,2,1,0:T(8,128)S(1)}, f32[32,16,16,128]{3,2,1,0:T(8,128)}, u32[]{:S(2)}) %copy-start.3) | copy-done | bytes 4194328
  18.1 7.1 %first_step.1 = (f32[32,16,16,128]{3,2,1,0:T(8,128)S(1)}, f32[32,16,128]{2,1,0:T(8,128)S(1)}, f32[32,16,128]{2,1,0:T(8,128)S(1)}, f32[32,16,128]{2,1,0:T(8,128)S(1)}, f32[32,16,128]{2,1,0:T(8,128)S(1)}) custom-call(f32[32,16,16,128]{3,2,1,0:T(8,128)S(1)} %copy-done.3, f32[32,16,16,128]{3,2,1,0:T(8,128)S(1)} %copy-done.1), custom_call_target="tpu_custom_call" | custom-call | flops 25165824 | bytes 12582912 | tf_op jit(solution)/shard_map/first_step/pallas_call | solution.py:36
  25.3 0.1 fusion.6
  25.6 0.3 broadcast_select_fusion.9
  26.0 0.2 broadcast_select_fusion.14
  26.2 3.0 %collective-permute-start.4 = (bf16[32,16,128]{2,1,0:T(8,128)(2,1)S(1)}, bf16[32,16,128]{2,1,0:T(8,128)(2,1)S(1)}, u32[]{:S(2)}, u32[]{:S(2)}) collective-permute-start(bf16[32,16,128]{2,1,0:T(8,128)(2,1)S(1)} %broadcast_select_fusion.15), channel_id=1, source_target_pairs={{0,8},{1,9},{8,0},{9,1},{16,24},{17,25},{24,16},{25,17},{2,10},{3,... | collective-permute-start | bytes 393224 | tf_op jit(solution)/shard_map/ppermute | solution.py:198
  29.3 0.6 collective-permute-start.7
  29.9 7.2 %later_step.3 = (f32[32,16,16,128]{3,2,1,0:T(8,128)S(1)}, f32[32,16,128]{2,1,0:T(8,128)S(1)}, f32[32,16,128]{2,1,0:T(8,128)S(1)}, f32[32,16,128]{2,1,0:T(8,128)S(1)}, f32[32,16,128]{2,1,0:T(8,128)S(1)}) custom-call(f32[32,16,16,128]{3,2,1,0:T(8,128)S(1)} %get-tuple-element.25.u_ref, f32[32,16,16,128]{3,2,1,0:T(8,128)S(1)} %copy-done.2, ...), custom_call_target="tpu_custom_call" | custom-call | flops 25165824 | bytes 12582912 | tf_op jit(solution)/shard_map/later_step/pallas_call | solution.py:36
  37.1 0.2 subtract_multiply_fusion.11
  37.3 0.3 broadcast_select_fusion.7
  37.7 0.2 broadcast_select_fusion.12
  37.9 0.9 collective-permute-start.8
  38.8 1.7 %collective-permute-start.10 = (bf16[32,16,128]{2,1,0:T(8,128)(2,1)S(1)}, bf16[32,16,128]{2,1,0:T(8,128)(2,1)S(1)}, u32[]{:S(2)}, u32[]{:S(2)}) collective-permute-start(bf16[32,16,128]{2,1,0:T(8,128)(2,1)S(1)} %get-tuple-element.62), channel_id=1, source_target_pairs={{0,2},{1,3},{2,0},{3,1},{4,6},{5,7},{6,4},{7,5},{8,10},{9,11},{10,... | collective-permute-start | bytes 393224 | tf_op jit(solution)/shard_map/ppermute | solution.py:198
  40.5 0.3 collective-permute-start.11
  40.8 7.2 %later_step.4 = (f32[32,16,16,128]{3,2,1,0:T(8,128)S(1)}, f32[32,16,128]{2,1,0:T(8,128)S(1)}, f32[32,16,128]{2,1,0:T(8,128)S(1)}, f32[32,16,128]{2,1,0:T(8,128)S(1)}, f32[32,16,128]{2,1,0:T(8,128)S(1)}) custom-call(f32[32,16,16,128]{3,2,1,0:T(8,128)S(1)} %get-tuple-element.30.u_ref, f32[32,16,16,128]{3,2,1,0:T(8,128)S(1)} %copy-done.2, ...), custom_call_target="tpu_custom_call" | custom-call | flops 25165824 | bytes 12582912 | tf_op jit(solution)/shard_map/later_step/pallas_call | solution.py:36
  48.0 0.2 subtract_multiply_fusion.7
  48.3 0.3 broadcast_select_fusion.5
  48.6 0.2 broadcast_select_fusion.10
  48.8 0.3 collective-permute-start.13
  49.2 4.0 %collective-permute-start.12 = (bf16[32,16,128]{2,1,0:T(8,128)(2,1)S(1)}, bf16[32,16,128]{2,1,0:T(8,128)(2,1)S(1)}, u32[]{:S(2)}, u32[]{:S(2)}) collective-permute-start(bf16[32,16,128]{2,1,0:T(8,128)(2,1)S(1)} %broadcast_select_fusion.11), channel_id=1, source_target_pairs={{0,8},{1,9},{8,0},{9,1},{16,24},{17,25},{24,16},{25,17},{2,10},{3,... | collective-permute-start | bytes 393224 | tf_op jit(solution)/shard_map/ppermute | solution.py:198
  53.2 1.6 %collective-permute-start.14 = (bf16[32,16,128]{2,1,0:T(8,128)(2,1)S(1)}, bf16[32,16,128]{2,1,0:T(8,128)(2,1)S(1)}, u32[]{:S(2)}, u32[]{:S(2)}) collective-permute-start(bf16[32,16,128]{2,1,0:T(8,128)(2,1)S(1)} %get-tuple-element.54), channel_id=1, source_target_pairs={{0,2},{1,3},{2,0},{3,1},{4,6},{5,7},{6,4},{7,5},{8,10},{9,11},{10,... | collective-permute-start | bytes 393224 | tf_op jit(solution)/shard_map/ppermute | solution.py:198
  54.8 7.2 %later_step.5 = (f32[32,16,16,128]{3,2,1,0:T(8,128)S(1)}, f32[32,16,128]{2,1,0:T(8,128)S(1)}, f32[32,16,128]{2,1,0:T(8,128)S(1)}, f32[32,16,128]{2,1,0:T(8,128)S(1)}, f32[32,16,128]{2,1,0:T(8,128)S(1)}) custom-call(f32[32,16,16,128]{3,2,1,0:T(8,128)S(1)} %get-tuple-element.35.u_ref, f32[32,16,16,128]{3,2,1,0:T(8,128)S(1)} %copy-done.2, ...), custom_call_target="tpu_custom_call" | custom-call | flops 25165824 | bytes 12582912 | tf_op jit(solution)/shard_map/later_step/pallas_call | solution.py:36
  62.1 0.1 subtract_multiply_fusion
  62.3 0.3 add_add_fusion.1
  62.6 0.2 add_add_fusion.2
  62.8 3.7 %final.1 = (f32[32,16,16,128]{3,2,1,0:T(8,128)}, bf16[32,16,16,128]{3,2,1,0:T(8,128)(2,1)}) custom-call(f32[32,16,16,128]{3,2,1,0:T(8,128)S(1)} %get-tuple-element.40.w_ref, f32[32,16,128]{2,1,0:T(8,128)S(1)} %get-tuple-element.137.fx0, f32[32,16,128]{2,1,0:T(8,128)S(1)} %get-tuple-element.136.fx1, f32[32,16,128]{2,1,0:T(8,128)S(1)} %get-tuple-element.52.fy0, ...), custom_call_target="tpu_custom_call" | custom-call | flops 1048576 | bytes 10485760 | tf_op jit(solution)/shard_map/final/pallas_call | solution.py:36
  66.6 0.6 collective-permute-start.16
  67.2 4.4 %corange.1 = f32[64,32]{1,0:T(8,128)S(1)} custom-call(bf16[64,16,16,128]{3,2,1,0:T(8,128)(2,1)S(1)} %copy-done.4, bf16[32,16,16,128]{3,2,1,0:T(8,128)(2,1)} %get-tuple-element.46.own_ref.snap_ref), custom_call_target="tpu_custom_call" | custom-call | flops 2147483648 | bytes 4194304 | tf_op jit(solution)/shard_map/corange/pallas_call | solution.py:36
  71.5 0.1 collective-permute-start.17
  71.7 3.8 %collective-permute-done.17 = f32[64,32]{1,0:T(8,128)S(1)} collective-permute-done((f32[64,32]{1,0:T(8,128)S(1)}, f32[64,32]{1,0:T(8,128)S(1)}, u32[]{:S(2)}, u32[]{:S(2)}) %collective-permute-start.17) | collective-permute-done | bytes 8224 | tf_op jit(solution)/shard_map/ppermute | solution.py:241
  75.5 3.9 %collective-permute-done.18 = f32[64,32]{1,0:T(8,128)S(1)} collective-permute-done((f32[64,32]{1,0:T(8,128)S(1)}, f32[64,32]{1,0:T(8,128)S(1)}, u32[]{:S(2)}, u32[]{:S(2)}) %collective-permute-start.18) | collective-permute-done | bytes 8224 | tf_op jit(solution)/shard_map/ppermute | solution.py:241
  79.4 2.0 %collective-permute-start.19 = (f32[64,32]{1,0:T(8,128)S(1)}, f32[64,32]{1,0:T(8,128)S(1)}, u32[]{:S(2)}, u32[]{:S(2)}) collective-permute-start(f32[64,32]{1,0:T(8,128)S(1)} %add.299), channel_id=1, source_target_pairs={{0,2},{2,0},{4,6},{6,4},{1,3},{3,1},{5,7},{7,5},{8,10},{10,8},{12,... | collective-permute-start | bytes 24584 | tf_op jit(solution)/shard_map/ppermute | solution.py:241
  81.5 0.5 compare_select_fusion.1.w_own_ref
  82.0 1.4 %collective-permute-done.19 = f32[64,32]{1,0:T(8,128)S(1)} collective-permute-done((f32[64,32]{1,0:T(8,128)S(1)}, f32[64,32]{1,0:T(8,128)S(1)}, u32[]{:S(2)}, u32[]{:S(2)}) %collective-permute-start.19) | collective-permute-done | bytes 8224 | tf_op jit(solution)/shard_map/ppermute | solution.py:241
  83.4 1.9 %collective-permute-start.20 = (f32[64,32]{1,0:T(8,128)S(1)}, f32[64,32]{1,0:T(8,128)S(1)}, u32[]{:S(2)}, u32[]{:S(2)}) collective-permute-start(f32[64,32]{1,0:T(8,128)S(1)} %add.300), channel_id=1, source_target_pairs={{0,4},{2,6},{4,0},{6,2},{1,5},{3,7},{5,1},{7,3},{8,12},{10,14},{12... | collective-permute-start | bytes 24584 | tf_op jit(solution)/shard_map/ppermute | solution.py:241
  85.3 0.5 compare_select_fusion.w_other_ref
  85.8 0.1 copy.17
  85.8 2.3 %collective-permute-done.20 = f32[64,32]{1,0:T(8,128)S(1)} collective-permute-done((f32[64,32]{1,0:T(8,128)S(1)}, f32[64,32]{1,0:T(8,128)S(1)}, u32[]{:S(2)}, u32[]{:S(2)}) %collective-permute-start.20) | collective-permute-done | bytes 8224 | tf_op jit(solution)/shard_map/ppermute | solution.py:241
  88.2 0.7 copy.18
  88.9 4.6 %range.1 = bf16[32,16,16,128]{3,2,1,0:T(8,128)(2,1)S(1)} custom-call(bf16[512,512]{1,0:T(8,128)(2,1)S(1)} %compare_select_fusion.1.w_own_ref, bf16[512,512]{1,0:T(8,128)(2,1)S(1)} %compare_select_fusion.w_other_ref, bf16[32,16,16,128]{3,2,1,0:T(8,128)(2,1)} %get-tuple-element.46.own_ref.snap_ref, ...), custom_call_target="tpu_custom_call" | custom-call | flops 4294967296 | bytes 8388608 | tf_op jit(solution)/shard_map/range/pallas_call | solution.py:36
  93.4 1.3 %copy.27 = bf16[32,16,16,128]{3,2,1,0:T(8,128)(2,1)} copy(bf16[32,16,16,128]{3,2,1,0:T(8,128)(2,1)S(1)} %range.1) | data formatting | bytes 4194304
  (71 shorter events, 1.1 us)
Async XLA Ops:
  0.6 80.8 %copy-start = (bf16[64,64]{1,0:T(8,128)(2,1)S(1)}, bf16[64,64]{1,0:T(8,128)(2,1)}, u32[]{:S(2)}) copy-start(bf16[64,64]{1,0:T(8,128)(2,1)} %param.8) | copy-start | bytes 24580
  2.0 23.3 %collective-permute-start = (bf16[64,16,128]{2,1,0:T(8,128)(2,1)S(1)}, bf16[64,16,128]{2,1,0:T(8,128)(2,1)S(1)}, u32[]{:S(2)}, u32[]{:S(2)}) collective-permute-start(bf16[64,16,128]{2,1,0:T(8,128)(2,1)S(1)} %get-tuple-element.100), channel_id=1, source_target_pairs={{0,8},{1,9},{8,0},{9,1},{16,24},{17,25},{24,16},{25,17},{2,10},{3,... | collective-permute-start | bytes 786440 | tf_op jit(solution)/shard_map/ppermute | solution.py:198
  5.0 20.3 %collective-permute-start.1 = (bf16[64,16,128]{2,1,0:T(8,128)(2,1)S(1)}, bf16[64,16,128]{2,1,0:T(8,128)(2,1)S(1)}, u32[]{:S(2)}, u32[]{:S(2)}) collective-permute-start(bf16[64,16,128]{2,1,0:T(8,128)(2,1)S(1)} %get-tuple-element.101), channel_id=1, source_target_pairs={{0,1},{1,0},{8,16},{9,17},{16,8},{17,9},{24,25},{25,24},{2,3},{3,2... | collective-permute-start | bytes 786440 | tf_op jit(solution)/shard_map/ppermute | solution.py:199
  10.5 15.0 %collective-permute-start.3 = (bf16[64,16,128]{2,1,0:T(8,128)(2,1)S(1)}, bf16[64,16,128]{2,1,0:T(8,128)(2,1)S(1)}, u32[]{:S(2)}, u32[]{:S(2)}) collective-permute-start(bf16[64,16,128]{2,1,0:T(8,128)(2,1)S(1)} %get-tuple-element.96), channel_id=1, source_target_pairs={{0,1},{1,0},{2,4},{3,5},{4,2},{5,3},{6,7},{7,6},{8,9},{9,8},{10,12... | collective-permute-start | bytes 786440 | tf_op jit(solution)/shard_map/ppermute | solution.py:199
  11.1 14.4 %collective-permute-start.2 = (bf16[64,16,128]{2,1,0:T(8,128)(2,1)S(1)}, bf16[64,16,128]{2,1,0:T(8,128)(2,1)S(1)}, u32[]{:S(2)}, u32[]{:S(2)}) collective-permute-start(bf16[64,16,128]{2,1,0:T(8,128)(2,1)S(1)} %get-tuple-element.97), channel_id=1, source_target_pairs={{0,2},{1,3},{2,0},{3,1},{4,6},{5,7},{6,4},{7,5},{8,10},{9,11},{10,... | collective-permute-start | bytes 786440 | tf_op jit(solution)/shard_map/ppermute | solution.py:198
  13.8 2.2 %copy-start.1 = (f32[32,16,16,128]{3,2,1,0:T(8,128)S(1)}, f32[32,16,16,128]{3,2,1,0:T(8,128)}, u32[]{:S(2)}) copy-start(f32[32,16,16,128]{3,2,1,0:T(8,128)} %k_ref.7) | copy-start | bytes 12582916
  16.0 2.2 %copy-start.3 = (f32[32,16,16,128]{3,2,1,0:T(8,128)S(1)}, f32[32,16,16,128]{3,2,1,0:T(8,128)}, u32[]{:S(2)}) copy-start(f32[32,16,16,128]{3,2,1,0:T(8,128)} %u_ref.1) | copy-start | bytes 12582916
  25.5 4.4 %copy-start.2 = (f32[32,16,16,128]{3,2,1,0:T(8,128)S(1)}, f32[32,16,16,128]{3,2,1,0:T(8,128)}, u32[]{:S(2)}) copy-start(f32[32,16,16,128]{3,2,1,0:T(8,128)} %k_ref.7) | copy-start | bytes 12582916
  26.2 10.9 %collective-permute-start.4 = (bf16[32,16,128]{2,1,0:T(8,128)(2,1)S(1)}, bf16[32,16,128]{2,1,0:T(8,128)(2,1)S(1)}, u32[]{:S(2)}, u32[]{:S(2)}) collective-permute-start(bf16[32,16,128]{2,1,0:T(8,128)(2,1)S(1)} %broadcast_select_fusion.15), channel_id=1, source_target_pairs={{0,8},{1,9},{8,0},{9,1},{16,24},{17,25},{24,16},{25,17},{2,10},{3,... | collective-permute-start | bytes 393224 | tf_op jit(solution)/shard_map/ppermute | solution.py:198
  29.2 7.8 %collective-permute-start.5 = (bf16[32,16,128]{2,1,0:T(8,128)(2,1)S(1)}, bf16[32,16,128]{2,1,0:T(8,128)(2,1)S(1)}, u32[]{:S(2)}, u32[]{:S(2)}) collective-permute-start(bf16[32,16,128]{2,1,0:T(8,128)(2,1)S(1)} %get-tuple-element.75), channel_id=1, source_target_pairs={{0,1},{1,0},{8,16},{9,17},{16,8},{17,9},{24,25},{25,24},{2,3},{3,2... | collective-permute-start | bytes 393224 | tf_op jit(solution)/shard_map/ppermute | solution.py:199
  29.2 8.1 %collective-permute-start.6 = (bf16[32,16,128]{2,1,0:T(8,128)(2,1)S(1)}, bf16[32,16,128]{2,1,0:T(8,128)(2,1)S(1)}, u32[]{:S(2)}, u32[]{:S(2)}) collective-permute-start(bf16[32,16,128]{2,1,0:T(8,128)(2,1)S(1)} %get-tuple-element.70), channel_id=1, source_target_pairs={{0,2},{1,3},{2,0},{3,1},{4,6},{5,7},{6,4},{7,5},{8,10},{9,11},{10,... | collective-permute-start | bytes 393224 | tf_op jit(solution)/shard_map/ppermute | solution.py:198
  29.3 8.0 %collective-permute-start.7 = (bf16[32,16,128]{2,1,0:T(8,128)(2,1)S(1)}, bf16[32,16,128]{2,1,0:T(8,128)(2,1)S(1)}, u32[]{:S(2)}, u32[]{:S(2)}) collective-permute-start(bf16[32,16,128]{2,1,0:T(8,128)(2,1)S(1)} %broadcast_select_fusion.8), channel_id=1, source_target_pairs={{0,1},{1,0},{2,4},{3,5},{4,2},{5,3},{6,7},{7,6},{8,9},{9,8},{10,12... | collective-permute-start | bytes 393224 | tf_op jit(solution)/shard_map/ppermute | solution.py:199
  37.9 10.1 %collective-permute-start.8 = (bf16[32,16,128]{2,1,0:T(8,128)(2,1)S(1)}, bf16[32,16,128]{2,1,0:T(8,128)(2,1)S(1)}, u32[]{:S(2)}, u32[]{:S(2)}) collective-permute-start(bf16[32,16,128]{2,1,0:T(8,128)(2,1)S(1)} %broadcast_select_fusion.13), channel_id=1, source_target_pairs={{0,8},{1,9},{8,0},{9,1},{16,24},{17,25},{24,16},{25,17},{2,10},{3,... | collective-permute-start | bytes 393224 | tf_op jit(solution)/shard_map/ppermute | solution.py:198
  38.8 9.3 %collective-permute-start.9 = (bf16[32,16,128]{2,1,0:T(8,128)(2,1)S(1)}, bf16[32,16,128]{2,1,0:T(8,128)(2,1)S(1)}, u32[]{:S(2)}, u32[]{:S(2)}) collective-permute-start(bf16[32,16,128]{2,1,0:T(8,128)(2,1)S(1)} %get-tuple-element.67), channel_id=1, source_target_pairs={{0,1},{1,0},{8,16},{9,17},{16,8},{17,9},{24,25},{25,24},{2,3},{3,2... | collective-permute-start | bytes 393224 | tf_op jit(solution)/shard_map/ppermute | solution.py:199
  38.8 9.5 %collective-permute-start.10 = (bf16[32,16,128]{2,1,0:T(8,128)(2,1)S(1)}, bf16[32,16,128]{2,1,0:T(8,128)(2,1)S(1)}, u32[]{:S(2)}, u32[]{:S(2)}) collective-permute-start(bf16[32,16,128]{2,1,0:T(8,128)(2,1)S(1)} %get-tuple-element.62), channel_id=1, source_target_pairs={{0,2},{1,3},{2,0},{3,1},{4,6},{5,7},{6,4},{7,5},{8,10},{9,11},{10,... | collective-permute-start | bytes 393224 | tf_op jit(solution)/shard_map/ppermute | solution.py:198
  40.5 7.7 %collective-permute-start.11 = (bf16[32,16,128]{2,1,0:T(8,128)(2,1)S(1)}, bf16[32,16,128]{2,1,0:T(8,128)(2,1)S(1)}, u32[]{:S(2)}, u32[]{:S(2)}) collective-permute-start(bf16[32,16,128]{2,1,0:T(8,128)(2,1)S(1)} %broadcast_select_fusion.6), channel_id=1, source_target_pairs={{0,1},{1,0},{2,4},{3,5},{4,2},{5,3},{6,7},{7,6},{8,9},{9,8},{10,12... | collective-permute-start | bytes 393224 | tf_op jit(solution)/shard_map/ppermute | solution.py:199
  48.8 13.2 %collective-permute-start.13 = (bf16[32,16,128]{2,1,0:T(8,128)(2,1)S(1)}, bf16[32,16,128]{2,1,0:T(8,128)(2,1)S(1)}, u32[]{:S(2)}, u32[]{:S(2)}) collective-permute-start(bf16[32,16,128]{2,1,0:T(8,128)(2,1)S(1)} %get-tuple-element.59), channel_id=1, source_target_pairs={{0,1},{1,0},{8,16},{9,17},{16,8},{17,9},{24,25},{25,24},{2,3},{3,2... | collective-permute-start | bytes 393224 | tf_op jit(solution)/shard_map/ppermute | solution.py:199
  49.2 12.9 %collective-permute-start.12 = (bf16[32,16,128]{2,1,0:T(8,128)(2,1)S(1)}, bf16[32,16,128]{2,1,0:T(8,128)(2,1)S(1)}, u32[]{:S(2)}, u32[]{:S(2)}) collective-permute-start(bf16[32,16,128]{2,1,0:T(8,128)(2,1)S(1)} %broadcast_select_fusion.11), channel_id=1, source_target_pairs={{0,8},{1,9},{8,0},{9,1},{16,24},{17,25},{24,16},{25,17},{2,10},{3,... | collective-permute-start | bytes 393224 | tf_op jit(solution)/shard_map/ppermute | solution.py:198
  53.2 9.1 %collective-permute-start.14 = (bf16[32,16,128]{2,1,0:T(8,128)(2,1)S(1)}, bf16[32,16,128]{2,1,0:T(8,128)(2,1)S(1)}, u32[]{:S(2)}, u32[]{:S(2)}) collective-permute-start(bf16[32,16,128]{2,1,0:T(8,128)(2,1)S(1)} %get-tuple-element.54), channel_id=1, source_target_pairs={{0,2},{1,3},{2,0},{3,1},{4,6},{5,7},{6,4},{7,5},{8,10},{9,11},{10,... | collective-permute-start | bytes 393224 | tf_op jit(solution)/shard_map/ppermute | solution.py:198
  54.8 7.5 %collective-permute-start.15 = (bf16[32,16,128]{2,1,0:T(8,128)(2,1)S(1)}, bf16[32,16,128]{2,1,0:T(8,128)(2,1)S(1)}, u32[]{:S(2)}, u32[]{:S(2)}) collective-permute-start(bf16[32,16,128]{2,1,0:T(8,128)(2,1)S(1)} %broadcast_select_fusion.4), channel_id=1, source_target_pairs={{0,1},{1,0},{2,4},{3,5},{4,2},{5,3},{6,7},{7,6},{8,9},{9,8},{10,12... | collective-permute-start | bytes 393224 | tf_op jit(solution)/shard_map/ppermute | solution.py:199
  62.6 4.6 %copy-start.4 = (bf16[64,16,16,128]{3,2,1,0:T(8,128)(2,1)S(1)}, bf16[64,16,16,128]{3,2,1,0:T(8,128)(2,1)}, u32[]{:S(2)}) copy-start(bf16[64,16,16,128]{3,2,1,0:T(8,128)(2,1)} %psi_ref.1) | copy-start | bytes 12582916
  66.6 19.2 %copy-start.6 = (f32[64,32]{0,1:T(8,128)S(1)}, f32[64,32]{0,1:T(8,128)}, u32[]{:S(2)}) copy-start(f32[64,32]{0,1:T(8,128)} %param.11) | copy-start | bytes 24580
  66.6 22.3 %copy-start.5 = (bf16[32,16,16,128]{3,2,1,0:T(8,128)(2,1)S(1)}, bf16[32,16,16,128]{3,2,1,0:T(8,128)(2,1)}, u32[]{:S(2)}) copy-start(bf16[32,16,16,128]{3,2,1,0:T(8,128)(2,1)} %prev_ref.1) | copy-start | bytes 6291460
  66.6 22.3 %collective-permute-start.16 = (bf16[32,16,16,128]{3,2,1,0:T(8,128)(2,1)}, bf16[32,16,16,128]{3,2,1,0:T(8,128)(2,1)}, u32[]{:S(2)}, u32[]{:S(2)}) collective-permute-start(bf16[32,16,16,128]{3,2,1,0:T(8,128)(2,1)} %get-tuple-element.46.own_ref.snap_ref), channel_id=1, source_target_pairs={{0,1},{1,0},{2,3},{3,2},{4,5},{5,4},{6,7},{7,6},{8,9},{9,8},{10,11... | collective-permute-start | bytes 6291464 | tf_op jit(solution)/shard_map/ppermute | solution.py:287
  71.5 4.0 %collective-permute-start.17 = (f32[64,32]{1,0:T(8,128)S(1)}, f32[64,32]{1,0:T(8,128)S(1)}, u32[]{:S(2)}, u32[]{:S(2)}) collective-permute-start(f32[64,32]{1,0:T(8,128)S(1)} %corange.1), channel_id=1, source_target_pairs={{0,8},{8,0},{16,24},{24,16},{1,9},{9,1},{17,25},{25,17},{2,10},{10... | collective-permute-start | bytes 24584 | tf_op jit(solution)/shard_map/ppermute | solution.py:241
  75.5 3.9 %collective-permute-start.18 = (f32[64,32]{1,0:T(8,128)S(1)}, f32[64,32]{1,0:T(8,128)S(1)}, u32[]{:S(2)}, u32[]{:S(2)}) collective-permute-start(f32[64,32]{1,0:T(8,128)S(1)} %add.298), channel_id=1, source_target_pairs={{0,16},{8,24},{16,0},{24,8},{1,17},{9,25},{17,1},{25,9},{2,18},{10... | collective-permute-start | bytes 24584 | tf_op jit(solution)/shard_map/ppermute | solution.py:241
  79.4 3.9 %collective-permute-start.19 = (f32[64,32]{1,0:T(8,128)S(1)}, f32[64,32]{1,0:T(8,128)S(1)}, u32[]{:S(2)}, u32[]{:S(2)}) collective-permute-start(f32[64,32]{1,0:T(8,128)S(1)} %add.299), channel_id=1, source_target_pairs={{0,2},{2,0},{4,6},{6,4},{1,3},{3,1},{5,7},{7,5},{8,10},{10,8},{12,... | collective-permute-start | bytes 24584 | tf_op jit(solution)/shard_map/ppermute | solution.py:241
  83.4 4.8 %collective-permute-start.20 = (f32[64,32]{1,0:T(8,128)S(1)}, f32[64,32]{1,0:T(8,128)S(1)}, u32[]{:S(2)}, u32[]{:S(2)}) collective-permute-start(f32[64,32]{1,0:T(8,128)S(1)} %add.300), channel_id=1, source_target_pairs={{0,4},{2,6},{4,0},{6,2},{1,5},{3,7},{5,1},{7,3},{8,12},{10,14},{12... | collective-permute-start | bytes 24584 | tf_op jit(solution)/shard_map/ppermute | solution.py:241

commit v2 on v0

v2 whole, which is shorter than its diff:
```python
import functools

import jax
import jax.numpy as jnp
from jax import lax
from jax.experimental import pallas as pl
from jax.experimental.pallas import tpu as pltpu
from jax.sharding import PartitionSpec as P

STEPS = 4
BF = jnp.bfloat16
F32 = jnp.float32
HALF = 0.16 * 0.5
BLOCK = 8
ROWS = 8


def vmem_call(
    kernel, outs, name, limit=3 << 20, scratch=(), hbm_in=(), hbm_out=(), aliases=None, flops=0, nbytes=0
):
    def call(*args):
        in_specs = []
        ready = []
        for i, arg in enumerate(args):
            in_specs.append(pl.BlockSpec(memory_space=pltpu.HBM if i in hbm_in else pltpu.VMEM))
            ready.append(
                pltpu.with_memory_space_constraint(arg, pltpu.HBM if i in hbm_in else pltpu.VMEM)
            )
        out_shape = []
        out_specs = []
        for i, (shape, dtype) in enumerate(outs):
            out_shape.append((pltpu.HBM if i in hbm_out else pltpu.VMEM)(shape, dtype))
            out_specs.append(pl.BlockSpec(memory_space=pltpu.HBM if i in hbm_out else pltpu.VMEM))
        return pl.pallas_call(
            kernel,
            out_shape=out_shape,
            in_specs=in_specs,
            out_specs=out_specs,
            scratch_shapes=list(scratch),
            input_output_aliases=aliases or {},
            name=name,
            compiler_params=pltpu.CompilerParams(vmem_limit_bytes=limit),
            cost_estimate=pl.CostEstimate(flops=flops, bytes_accessed=nbytes, transcendentals=0),
        )(*ready)

    return call


def faces_kernel(u_ref, k_ref, lx, ux, ly, uy, xbuf, ybuf, sem):
    _, nx, ny, _ = u_ref.shape
    copies = []
    for i, (ref, end) in enumerate(((k_ref, 0), (u_ref, 0), (k_ref, 1), (u_ref, 1))):
        x, y = end * (nx - 1), end * (ny - 1)
        copies.append(pltpu.make_async_copy(ref.at[:, x], xbuf.at[i], sem.at[i]))
        copies.append(pltpu.make_async_copy(ref.at[:, :, y], ybuf.at[i], sem.at[4 + i]))
    for copy in copies:
        copy.start()
    for i in range(4):
        copies[2 * i].wait()
        copies[2 * i + 1].wait()
        (lx if i < 2 else ux)[i % 2] = xbuf[i].astype(BF)
        (ly if i < 2 else uy)[i % 2] = ybuf[i].astype(BF)


def y_line(ref, s, y):
    _, nx, ny, _ = ref.shape
    return pl.ds(s * (nx * ny) + y, nx, stride=ny)


def flat(ref):
    samples, nx, ny, nz = ref.shape
    return ref.reshape(samples * nx * ny, nz)


def coef_kernel(k_hbm, cx_ref, cy_ref, cup_ref, cdown_ref, kx0, kx1, ky0, ky1, buf, sem):
    samples, nx, ny, nz = k_hbm.shape
    shape = (BLOCK, ny, nz)
    groups = samples // BLOCK
    y_open = lax.broadcasted_iota(jnp.int32, shape, 1) < ny - 1
    lane = lax.broadcasted_iota(jnp.int32, shape, 2)

    def copy_of(g):
        part = pl.ds(g * BLOCK, BLOCK)
        return pltpu.make_async_copy(k_hbm.at[part], buf.at[part], sem.at[g])

    for g in range(groups):
        copy_of(g).start()
    rows = flat(buf)
    for g in range(groups):
        copy_of(g).wait()
        part = slice(g * BLOCK, (g + 1) * BLOCK)
        for s in range(g * BLOCK, (g + 1) * BLOCK):
            ky0[s] = rows[y_line(buf, s, 0), :] * HALF
            ky1[s] = rows[y_line(buf, s, ny - 1), :] * HALF
        k = buf[part, 0] * HALF
        kx0[part] = k
        for x in range(nx):
            if x + 1 < nx:
                k_next = buf[part, x + 1] * HALF
                cx_ref[part, x] = k + k_next
            cy_ref[part, x] = jnp.where(y_open, k + pltpu.roll(k, ny - 1, 1), 0.0)
            cup_ref[part, x] = k + jnp.where(lane < nz - 1, pltpu.roll(k, nz - 1, 2), 0.0)
            cdown_ref[part, x] = k + jnp.where(lane > 0, pltpu.roll(k, 1, 2), 0.0)
            if x + 1 < nx:
                k = k_next
        kx1[part] = k


def difference_matrix(nz):
    row = lax.broadcasted_iota(jnp.int32, (nz, nz), 0)
    col = lax.broadcasted_iota(jnp.int32, (nz, nz), 1)
    eye = (row == col).astype(F32)
    up = (row == col + 1).astype(F32) - eye
    down = (row + 1 == col).astype(F32) - eye
    both = jnp.concatenate([up, down], axis=1).astype(BF)
    return jnp.concatenate([both, both], axis=0)


def first_step_kernel(u_hbm, cx_ref, cy_ref, cup_ref, cdown_ref, u_ref, w_ref, sem):
    groups = u_ref.shape[0] // BLOCK

    def copy_of(g):
        part = pl.ds(g * BLOCK, BLOCK)
        return pltpu.make_async_copy(u_hbm.at[part], u_ref.at[part], sem.at[g])

    for g in range(groups):
        copy_of(g).start()
    step_body(u_ref, cx_ref, cy_ref, cup_ref, cdown_ref, w_ref, lambda g: copy_of(g).wait())


def step_kernel(u_ref, cx_ref, cy_ref, cup_ref, cdown_ref, *refs):
    step_body(u_ref, cx_ref, cy_ref, cup_ref, cdown_ref, refs[-1], lambda g: None)


def step_body(u_ref, cx_ref, cy_ref, cup_ref, cdown_ref, w_ref, before):
    samples, nx, ny, nz = u_ref.shape
    shape = (BLOCK, ny, nz)
    matrix = difference_matrix(nz)

    def body(g, carry):
        before(g)
        part = pl.ds(g * BLOCK, BLOCK)
        u = u_ref[part, 0]
        for x in range(nx):
            total = u
            if x + 1 < nx:
                u_next = u_ref[part, x + 1]
                flux = cx_ref[part, x] * (u_next - u)
                total = total + flux
            if x > 0:
                total = total - flux_low
            fy = cy_ref[part, x] * (pltpu.roll(u, ny - 1, 1) - u)
            total = total + (fy - pltpu.roll(fy, 1, 1))
            wide = u.reshape(BLOCK * ny, nz)
            coarse = wide.astype(BF)
            fine = (wide - coarse.astype(F32)).astype(BF)
            dz = jnp.dot(jnp.concatenate([coarse, fine], axis=1), matrix, preferred_element_type=F32)
            total = total + cup_ref[part, x] * dz[:, :nz].reshape(shape)
            total = total + cdown_ref[part, x] * dz[:, nz:].reshape(shape)
            w_ref[part, x] = total
            if x + 1 < nx:
                u, flux_low = u_next, flux
        return carry

    lax.fori_loop(0, samples // BLOCK, body, 0)


def edge_kernel(send, w_in, u_ref, cx0, cx1, cy0, cy1, hx0, hx1, hy0, hy1, *refs):
    del w_in
    w_ref, lx, ux, ly, uy = refs[-5:] if send else (refs[-1],) + (None,) * 4
    samples, nx, ny, nz = u_ref.shape
    w_rows, u_rows = flat(w_ref), flat(u_ref)

    def one(s):
        for y, coef, halo in ((0, cy0, hy0), (ny - 1, cy1, hy1)):
            line = y_line(u_ref, s, y)
            flux = coef[s] * (halo[s].astype(F32) - u_rows[line, :])
            w_rows[line, :] = w_rows[line, :] + flux
        for x, coef, halo, out in ((0, cx0, hx0, lx), (nx - 1, cx1, hx1, ux)):
            value = w_ref[s, x] + coef[s] * (halo[s].astype(F32) - u_ref[s, x])
            w_ref[s, x] = value
            if send:
                out[s] = value.astype(BF)
        if send:
            for y, out in ((0, ly), (ny - 1, uy)):
                out[s] = w_rows[y_line(u_ref, s, y), :].astype(BF)

    def body(i, carry):
        for j in range(4):
            one(i * 4 + j)
        return carry

    lax.fori_loop(0, samples // 4, body, 0)


def split_shape(shape):
    count, nx, ny, nz = shape
    return (nx, ny // ROWS, count * ROWS, nz)


def split_into(out_ref, x, value):
    count, ny, nz = value.shape
    for h in range(ny // ROWS):
        part = value[:, h * ROWS : (h + 1) * ROWS]
        out_ref[x, h] = part.reshape(count * ROWS, nz).astype(BF)


def one_hot(rows, cols, row_width, col_width):
    row = lax.broadcasted_iota(jnp.int32, (rows, cols), 0) // row_width
    col = lax.broadcasted_iota(jnp.int32, (rows, cols), 1) // col_width
    return (row == col).astype(BF)


def spread(block):
    rows, cols = block.shape
    tall = jnp.dot(one_hot(rows * ROWS, rows, ROWS, 1), block, preferred_element_type=F32).astype(BF)
    full = jnp.dot(tall, one_hot(cols, cols * ROWS, 1, ROWS), preferred_element_type=F32)
    row = lax.broadcasted_iota(jnp.int32, full.shape, 0) % ROWS
    col = lax.broadcasted_iota(jnp.int32, full.shape, 1) % ROWS
    return jnp.where(row == col, full, 0.0).astype(BF)


def psi_kernel(psi_hbm, omega_ref, out_ref, weight_ref, buf, sem):
    ranks, nx, ny, nz = psi_hbm.shape
    parts = 4

    def copy_of(i):
        part = pl.ds(i * (nx // parts), nx // parts)
        return pltpu.make_async_copy(psi_hbm.at[:, part], buf.at[:, part], sem.at[i])

    for i in range(parts):
        copy_of(i).start()
    for i in range(omega_ref.shape[0]):
        weight_ref[i] = spread(omega_ref[i])

    def body(x, carry):
        split_into(out_ref, x, buf[:, x].astype(F32))
        return carry

    for i in range(parts):
        copy_of(i).wait()
        lax.fori_loop(i * (nx // parts), (i + 1) * (nx // parts), body, 0)


def side_by_side(ref, x):
    return jnp.concatenate([ref[x, h] for h in range(ref.shape[1])], axis=1)


def range_kernel(weight_ref, own_ref, other_ref, prev_hbm, out_ref, done_ref, prev, buf, sem):
    ranks, nx, ny, nz = prev_hbm.shape
    parts = 4

    def prev_copy(i):
        part = pl.ds(i * (nx // parts), nx // parts)
        return pltpu.make_async_copy(prev_hbm.at[:, part], prev.at[:, part], sem.at[1, i])

    for i in range(parts):
        prev_copy(i).start()

    def copy_of(i):
        part = pl.ds(i * (nx // parts), nx // parts)
        return pltpu.make_async_copy(buf.at[:, part], out_ref.at[:, part], sem.at[0, i])

    done_ref[...] = jnp.zeros_like(done_ref)

    def body(x):
        value = jnp.dot(weight_ref[0], side_by_side(own_ref, x), preferred_element_type=F32)
        value += jnp.dot(weight_ref[1], side_by_side(other_ref, x), preferred_element_type=F32)
        halves = [
            value[:, h * nz : (h + 1) * nz].reshape(ranks, ROWS, nz) for h in range(ny // ROWS)
        ]
        total = jnp.concatenate(halves, axis=1) + prev[:, x].astype(F32)
        buf[:, x] = total.astype(BF)

    for i in range(parts):
        prev_copy(i).wait()
        for x in range(i * (nx // parts), (i + 1) * (nx // parts)):
            body(x)
        copy_of(i).start()
    for i in range(parts):
        copy_of(i).wait()


def corange_kernel(psi_ref, u_ref, snap_ref, out_ref, state_hbm, acc, sem):
    copy = pltpu.make_async_copy(u_ref, state_hbm, sem)
    copy.start()
    samples, nx, ny, nz = u_ref.shape
    ranks = psi_ref.shape[2] // ROWS
    cols = ranks * ROWS
    for x in range(0, nx, 2):
        split_into(snap_ref, x, u_ref[:, x])
        split_into(snap_ref, x + 1, u_ref[:, x + 1])
        left = jnp.concatenate([side_by_side(snap_ref, x), side_by_side(snap_ref, x + 1)], axis=1)
        right = jnp.concatenate([side_by_side(psi_ref, x), side_by_side(psi_ref, x + 1)], axis=1)
        part = lax.dot_general(left, right, (((1,), (1,)), ((), ())), preferred_element_type=F32)
        acc[...] = part if x == 0 else acc[...] + part
    row = lax.broadcasted_iota(jnp.int32, (ROWS, cols), 0)
    col = lax.broadcasted_iota(jnp.int32, (ROWS, cols), 1) % ROWS
    fold = (
        lax.broadcasted_iota(jnp.int32, (cols, ranks), 0) // ROWS
        == lax.broadcasted_iota(jnp.int32, (cols, ranks), 1)
    ).astype(F32)
    picked = jnp.where((row == col)[None], acc[...].reshape(samples, ROWS, cols), 0.0).sum(1)
    out_ref[...] = jnp.dot(picked, fold, precision=lax.Precision.HIGHEST, preferred_element_type=F32)
    copy.wait()


def swap_pairs(count, parity, par):
    partner = {}
    for i in range(parity, count - 1, 2):
        partner[i] = i + 1
        partner[i + 1] = i
    pairs = []
    for i in range(count):
        for p in range(par):
            source = i * par + p
            if i in partner:
                pairs.append((source, partner[i] * par + p))
            else:
                pairs.append((source, i * par + (p + 1) % par))
    return pairs


def exchange(low, high, axis):
    count, par = lax.axis_size(axis), lax.axis_size("par")
    index = lax.axis_index(axis)
    odd = index % 2 == 1
    first = lax.ppermute(jnp.where(odd, low, high), (axis, "par"), swap_pairs(count, 0, par))
    second = lax.ppermute(jnp.where(odd, high, low), (axis, "par"), swap_pairs(count, 1, par))
    zero = jnp.zeros_like(first)
    below = jnp.where(index == 0, zero, jnp.where(odd, first, second))
    above = jnp.where(index == count - 1, zero, jnp.where(odd, second, first))
    return below, above


def total_of(value, axis):
    count = lax.axis_size(axis)
    total = value
    for shift in range(1, count):
        total = total + lax.ppermute(value, axis, [(i, i ^ shift) for i in range(count)])
    return total


def per_device(initial_state, conductivity, omega, psi, range_prev, corange_prev):
    samples, nx, ny, nz = block = initial_state.shape
    ranks = psi.shape[0]
    cells = samples * nx * ny * nz
    x_face, y_face = (samples, ny, nz), (samples, nx, nz)
    par = lax.axis_index("par")
    par_size = lax.axis_size("par")

    sent = vmem_call(
        faces_kernel,
        [((2,) + x_face, BF)] * 2 + [((2,) + y_face, BF)] * 2,
        "faces",
        scratch=[
            pltpu.VMEM((4,) + x_face, F32),
            pltpu.VMEM((4,) + y_face, F32),
            pltpu.SemaphoreType.DMA((8,)),
        ],
        hbm_in=(0, 1),
        flops=cells // 2,
        nbytes=cells,
    )(initial_state, conductivity)
    got_y = exchange(sent[2], sent[3], "sy")
    got = exchange(sent[0], sent[1], "sx") + got_y
    halos = [g[1] for g in got]

    groups = samples // BLOCK
    made = vmem_call(
        coef_kernel,
        [(block, F32)] * 4 + [(x_face, F32)] * 2 + [(y_face, F32)] * 2,
        "coefs",
        limit=6 << 20,
        scratch=[pltpu.VMEM(block, F32), pltpu.SemaphoreType.DMA((groups,))],
        hbm_in=(0,),
        flops=12 * cells,
        nbytes=8 * cells,
    )(conductivity)
    coefs, kfaces = made[:4], made[4:]
    face_coefs = [k + HALF * g[0].astype(F32) for k, g in zip(kfaces, got)]
    own_ranks = range_prev.shape[0]
    own_cols = lax.dynamic_slice_in_dim(omega, par * own_ranks, own_ranks, 1).T
    source = (par + par_size - 1) % par_size
    omega_blocks = jnp.stack(
        [lax.dynamic_slice_in_dim(own_cols, p * samples, samples, 1) for p in (par, source)]
    )
    held_psi, weights = vmem_call(
        psi_kernel,
        [(split_shape(psi.shape), BF), ((2, own_ranks * ROWS, samples * ROWS), BF)],
        "psi",
        limit=6 << 20,
        scratch=[pltpu.VMEM(psi.shape, BF), pltpu.SemaphoreType.DMA((4,))],
        hbm_in=(0,),
        flops=4 * cells,
        nbytes=4 * cells,
    )(psi, omega_blocks)

    cost = dict(flops=24 * cells, nbytes=8 * cells)
    for step in range(STEPS):
        if step == 0:
            state, moved = vmem_call(
                first_step_kernel,
                [(block, F32)] * 2,
                "first_step",
                scratch=[pltpu.SemaphoreType.DMA((groups,))],
                hbm_in=(0,),
                **cost,
            )(initial_state, *coefs)
        else:
            got_y = exchange(edges[2], edges[3], "sy")
            halos = exchange(edges[0], edges[1], "sx") + got_y
            moved = vmem_call(step_kernel, [(block, F32)], "step", **cost)(state, *coefs, held_psi, weights)[0]
        send = step < STEPS - 1
        state, *edges = vmem_call(
            functools.partial(edge_kernel, send),
            [(block, F32)] + [(x_face, BF), (x_face, BF), (y_face, BF), (y_face, BF)] * send,
            "edge",
            aliases={0: 0},
            flops=cells,
            nbytes=cells,
        )(moved, state, *face_coefs, *halos, held_psi, weights)

    snapshot, partial_sum, final_state = vmem_call(
        corange_kernel,
        [(split_shape(block), BF), ((samples, ranks), F32), (block, F32)],
        "corange",
        limit=6 << 20,
        scratch=[pltpu.VMEM((samples * ROWS, ranks * ROWS), F32), pltpu.SemaphoreType.DMA],
        hbm_out=(2,),
        flops=2 * ranks * ROWS * cells,
        nbytes=4 * cells,
    )(held_psi, state)
    other = lax.ppermute(snapshot, "par", [(i, (i + 1) % par_size) for i in range(par_size)])
    range_sketch, done = vmem_call(
        range_kernel,
        [(range_prev.shape, BF), ((samples, ranks), F32)],
        "range",
        limit=8 << 20,
        scratch=[
            pltpu.VMEM(range_prev.shape, BF),
            pltpu.VMEM(range_prev.shape, BF),
            pltpu.SemaphoreType.DMA((2, 4)),
        ],
        hbm_in=(3,),
        hbm_out=(0,),
        flops=2 * ranks * ROWS * cells,
        nbytes=4 * cells,
    )(weights, snapshot, other, range_prev)
    corange = corange_prev.T + total_of(total_of(partial_sum, "sx") + done, "sy")
    return final_state, range_sketch, corange.T


def solution(mesh):
    in_specs = (
        P("par", "sx", "sy", None),
        P("par", "sx", "sy", None),
        P(),
        P(None, "sx", "sy", None),
        P("par", "sx", "sy", None),
        P(None, "par"),
    )
    out_specs = (P("par", "sx", "sy", None), P("par", "sx", "sy", None), P(None, "par"))
    return jax.shard_map(
        per_device, mesh=mesh, in_specs=in_specs, out_specs=out_specs, check_vma=False
    )
```

time: 272 us -> 66.1 us (0.24)
  blocking collectives: 82.9 us -> 0 us
  starting transfers between devices: 62.5 us -> 26.4 us
  other arithmetic: 36.9 us -> 1.23 us
  local copies, waits for them, and re-layouts: 34.4 us -> 0.31 us
  Pallas kernels: 0 us -> 31.1 us
  waiting for transfers between devices: 32.4 us -> 5.89 us
  between operations: 14.4 us -> 1.06 us
  matrix products: 7.86 us -> 0 us
    psum x1 -> x0, blocking collectives: 82.9 us -> none  [per_device(): corange_sketch = corange_prev + lax.psum(partial_value, ('sx', 'sy'))]
    ppermute x20 -> x23, starting transfers between devices: 62.5 us -> 26.4 us  [the longest x8 17.3 us: exchange(): lax.ppermute(jnp.where(odd, low, high), (axis, 'par'), swap_pairs(count,...]
    pallas_call x0 -> x13, Pallas kernels: none -> 31.1 us  [call(): pl.pallas_call(kernel, out_shape=out_shape, in_specs=in_specs, out_specs=...]
    unnamed x22 -> x6, local copies, waits for them, and re-layouts: 30.2 us -> 0.18 us
    add x4 -> x3, other arithmetic: 27.1 us -> 0.14 us  [the longest x2 0.13 us: per_device(): face_coefs = [k + HALF * g[0].astype(F32) for k, g in zip(kfaces, got)]]
    ppermute x20 -> x23, waiting for transfers between devices: 32.4 us -> 5.89 us  [the longest x8 3.3 us: exchange(): lax.ppermute(jnp.where(odd, low, high), (axis, 'par'), swap_pairs(count,...]
    convert_element_type x1 -> x0, other arithmetic: 9.73 us -> none  [per_device(): snapshot = state.astype(jnp.bfloat16)]
    dot_general x2 -> x0, matrix products: 7.86 us -> none  [the longest x1 4.09 us: per_device(): lax.dot_general(own_cols, piece.reshape(rows, -1), (((0,), (0,)), ((), ()...]
  transfers between devices with their start and end apart: 21 -> 23, of which waited for: 12 -> 10; matrix products, arithmetic and copies ran while one was open for 8% -> 1% of each run, Pallas kernels for 0% -> 36%
where the time goes in v2:
time: 66.1 us; the launch traced here: 65.9 us
  Pallas kernels  31.1 us (47%)
  starting transfers between devices  26.4 us (40%)
  waiting for transfers between devices  5.89 us (9%)
  other arithmetic  1.23 us (2%)
  between operations  1.06 us (2%)
    pallas_call x13, Pallas kernels, call(): pl.pallas_call(kernel, out_shape=out_shape, in_specs=in_specs, out_specs=...  31.1 us
    ppermute x8, starting transfers between devices, exchange(): lax.ppermute(jnp.where(odd, low, high), (axis, 'par'), swap_pairs(count,...  17.3 us
    ppermute x6, starting transfers between devices, total_of(): lax.ppermute(value, axis, [(i, i ^ shift) for i in range(count)])  8.01 us
    ppermute x8, waiting for transfers between devices, exchange(): lax.ppermute(jnp.where(odd, low, high), (axis, 'par'), swap_pairs(count,...  3.3 us
    ppermute x6, waiting for transfers between devices, total_of(): lax.ppermute(value, axis, [(i, i ^ shift) for i in range(count)])  1.98 us
  transfers between devices with their start and end apart: 23, of which 10 were waited for; matrix products, arithmetic and copies ran while one was open for 1% of the time, Pallas kernels for 36%

profile of v2, /device:TPU:0, one launch (start us, length us, event | category | flops | bytes accessed | tf_op | source)
XLA Modules:
  0.0 65.9 jit_solution(16121751595669119231)
XLA Ops:
  0.7 1.7 %faces.1 = (bf16[2,32,16,128]{3,2,1,0:T(8,128)(2,1)S(1)}, bf16[2,32,16,128]{3,2,1,0:T(8,128)(2,1)S(1)}, bf16[2,32,16,128]{3,2,1,0:T(8,128)(2,1)S(1)}, bf16[2,32,16,128]{3,2,1,0:T(8,128)(2,1)S(1)}) custom-call(f32[32,16,16,128]{3,2,1,0:T(8,128)} %u_ref.1, f32[32,16,16,128]{3,2,1,0:T(8,128)} %k_ref.1), custom_call_target="tpu_custom_call" | custom-call | flops 524288 | bytes 1048576 | tf_op jit(solution)/shard_map/faces/pallas_call | solution.py:34
  2.4 0.5 collective-permute-start.1
  2.9 4.0 %collective-permute-start = (bf16[2,32,16,128]{3,2,1,0:T(8,128)(2,1)S(1)}, bf16[2,32,16,128]{3,2,1,0:T(8,128)(2,1)S(1)}, u32[]{:S(2)}, u32[]{:S(2)}) collective-permute-start(bf16[2,32,16,128]{3,2,1,0:T(8,128)(2,1)S(1)} %get-tuple-element.82), channel_id=1, source_target_pairs={{0,8},{1,9},{8,0},{9,1},{16,24},{17,25},{24,16},{25,17},{2,10},{3,... | collective-permute-start | bytes 786440 | tf_op jit(solution)/shard_map/ppermute | solution.py:328
  6.9 0.1 collective-permute-start.3
  7.0 3.1 %collective-permute-start.2 = (bf16[2,32,16,128]{3,2,1,0:T(8,128)(2,1)S(1)}, bf16[2,32,16,128]{3,2,1,0:T(8,128)(2,1)S(1)}, u32[]{:S(2)}, u32[]{:S(2)}) collective-permute-start(bf16[2,32,16,128]{3,2,1,0:T(8,128)(2,1)S(1)} %get-tuple-element.78), channel_id=1, source_target_pairs={{0,2},{1,3},{2,0},{3,1},{4,6},{5,7},{6,4},{7,5},{8,10},{9,11},{10,... | collective-permute-start | bytes 786440 | tf_op jit(solution)/shard_map/ppermute | solution.py:328
  10.1 0.1 fusion.1
  10.2 0.1 copy.15
  10.3 0.1 copy.16
  10.4 2.4 %psi.1 = (bf16[16,2,512,128]{3,2,1,0:T(8,128)(2,1)S(1)}, bf16[2,256,256]{2,1,0:T(8,128)(2,1)S(1)}) custom-call(bf16[64,16,16,128]{3,2,1,0:T(8,128)(2,1)} %psi_hbm.1, bf16[2,32,32]{2,1,0:T(8,128)(2,1)S(1)} %pad_maximum_fusion.omega_ref), custom_call_target="tpu_custom_call" | custom-call | flops 4194304 | bytes 4194304 | tf_op jit(solution)/shard_map/psi/pallas_call | solution.py:34
  12.9 4.4 %coefs.1 = (f32[32,16,16,128]{3,2,1,0:T(8,128)S(1)}, f32[32,16,16,128]{3,2,1,0:T(8,128)S(1)}, f32[32,16,16,128]{3,2,1,0:T(8,128)S(1)}, f32[32,16,16,128]{3,2,1,0...) custom-call(f32[32,16,16,128]{3,2,1,0:T(8,128)} %k_ref.1), custom_call_target="tpu_custom_call" | custom-call | flops 12582912 | bytes 8388608 | tf_op jit(solution)/shard_map/coefs/pallas_call | solution.py:34
  17.2 4.3 %first_step.1 = (f32[32,16,16,128]{3,2,1,0:T(8,128)S(1)}, f32[32,16,16,128]{3,2,1,0:T(8,128)S(1)}) custom-call(f32[32,16,16,128]{3,2,1,0:T(8,128)} %u_ref.1, f32[32,16,16,128]{3,2,1,0:T(8,128)S(1)} %get-tuple-element.40.cx_ref, f32[32,16,16,128]{3,2,1,0:T(8,128)S(1)} %get-tuple-element.41.cy_ref, f32[32,16,16,128]{3,2,1,0:T(8,128)S(1)} %get-tuple-element.42.cup_ref, ...), custom_call_target="tpu_custom_call" | custom-call | flops 25165824 | bytes 8388608 | tf_op jit(solution)/shard_map/first_step/pallas_call | solution.py:34
  21.8 1.0 %edge.4 = (f32[32,16,16,128]{3,2,1,0:T(8,128)S(1)}, bf16[32,16,128]{2,1,0:T(8,128)(2,1)S(1)}, bf16[32,16,128]{2,1,0:T(8,128)(2,1)S(1)}, bf16[32,16,128]{2,1,0:T(8,128)(2,1)S(1)}, bf16[32,16,128]{2,1,0:T(8,128)(2,1)S(1)}) custom-call(f32[32,16,16,128]{3,2,1,0:T(8,128)S(1)} %get-tuple-element.44.w_in, ...), custom_call_target="tpu_custom_call", output_to_operand_aliasing={{0}: (0, {})} | custom-call | flops 1048576 | bytes 1048576 | tf_op jit(solution)/shard_map/edge/pallas_call | solution.py:34
  22.9 1.6 %collective-permute-start.4 = (bf16[32,16,128]{2,1,0:T(8,128)(2,1)S(1)}, bf16[32,16,128]{2,1,0:T(8,128)(2,1)S(1)}, u32[]{:S(2)}, u32[]{:S(2)}) collective-permute-start(bf16[32,16,128]{2,1,0:T(8,128)(2,1)S(1)} %get-tuple-element.106), channel_id=1, source_target_pairs={{0,8},{1,9},{8,0},{9,1},{16,24},{17,25},{24,16},{25,17},{2,10},{3,... | collective-permute-start | bytes 393224 | tf_op jit(solution)/shard_map/ppermute | solution.py:328
  24.6 1.7 %collective-permute-start.6 = (bf16[32,16,128]{2,1,0:T(8,128)(2,1)S(1)}, bf16[32,16,128]{2,1,0:T(8,128)(2,1)S(1)}, u32[]{:S(2)}, u32[]{:S(2)}) collective-permute-start(bf16[32,16,128]{2,1,0:T(8,128)(2,1)S(1)} %get-tuple-element.102), channel_id=1, source_target_pairs={{0,2},{1,3},{2,0},{3,1},{4,6},{5,7},{6,4},{7,5},{8,10},{9,11},{10,... | collective-permute-start | bytes 393224 | tf_op jit(solution)/shard_map/ppermute | solution.py:328
  26.3 3.0 %step.3.w_in = f32[32,16,16,128]{3,2,1,0:T(8,128)S(1)} custom-call(f32[32,16,16,128]{3,2,1,0:T(8,128)S(1)} %get-tuple-element.55.u_ref, f32[32,16,16,128]{3,2,1,0:T(8,128)S(1)} %get-tuple-element.40.cx_ref, f32[32,16,16,128]{3,2,1,0:T(8,128)S(1)} %get-tuple-element.41.cy_ref, f32[32,16,16,128]{3,2,1,0:T(8,128)S(1)} %get-tuple-element.42.cup_ref, ...), custom_call_target="tpu_custom_call" | custom-call | flops 25165824 | bytes 8388608 | tf_op jit(solution)/shard_map/step/pallas_call | solution.py:34
  29.3 0.9 %collective-permute-done.4 = bf16[32,16,128]{2,1,0:T(8,128)(2,1)S(1)} collective-permute-done((bf16[32,16,128]{2,1,0:T(8,128)(2,1)S(1)}, bf16[32,16,128]{2,1,0:T(8,128)(2,1)S(1)}, u32[]{:S(2)}, u32[]{:S(2)}) %collective-permute-start.4) | collective-permute-done | bytes 131104 | tf_op jit(solution)/shard_map/ppermute | solution.py:328
  30.3 0.2 collective-permute-done.6
  30.5 1.0 %edge.5 = (f32[32,16,16,128]{3,2,1,0:T(8,128)S(1)}, bf16[32,16,128]{2,1,0:T(8,128)(2,1)S(1)}, bf16[32,16,128]{2,1,0:T(8,128)(2,1)S(1)}, bf16[32,16,128]{2,1,0:T(8,128)(2,1)S(1)}, bf16[32,16,128]{2,1,0:T(8,128)(2,1)S(1)}) custom-call(f32[32,16,16,128]{3,2,1,0:T(8,128)S(1)} %step.3.w_in, ...), custom_call_target="tpu_custom_call", output_to_operand_aliasing={{0}: (0, {})} | custom-call | flops 1048576 | bytes 1048576 | tf_op jit(solution)/shard_map/edge/pallas_call | solution.py:34
  31.5 0.1 collective-permute-start.9
  31.6 1.9 %collective-permute-start.8 = (bf16[32,16,128]{2,1,0:T(8,128)(2,1)S(1)}, bf16[32,16,128]{2,1,0:T(8,128)(2,1)S(1)}, u32[]{:S(2)}, u32[]{:S(2)}) collective-permute-start(bf16[32,16,128]{2,1,0:T(8,128)(2,1)S(1)} %get-tuple-element.98), channel_id=1, source_target_pairs={{0,8},{1,9},{8,0},{9,1},{16,24},{17,25},{24,16},{25,17},{2,10},{3,... | collective-permute-start | bytes 393224 | tf_op jit(solution)/shard_map/ppermute | solution.py:328
  33.5 0.1 collective-permute-start.11
  33.6 1.4 %collective-permute-start.10 = (bf16[32,16,128]{2,1,0:T(8,128)(2,1)S(1)}, bf16[32,16,128]{2,1,0:T(8,128)(2,1)S(1)}, u32[]{:S(2)}, u32[]{:S(2)}) collective-permute-start(bf16[32,16,128]{2,1,0:T(8,128)(2,1)S(1)} %get-tuple-element.94), channel_id=1, source_target_pairs={{0,2},{1,3},{2,0},{3,1},{4,6},{5,7},{6,4},{7,5},{8,10},{9,11},{10,... | collective-permute-start | bytes 393224 | tf_op jit(solution)/shard_map/ppermute | solution.py:328
  35.0 3.0 %step.4.w_in = f32[32,16,16,128]{3,2,1,0:T(8,128)S(1)} custom-call(f32[32,16,16,128]{3,2,1,0:T(8,128)S(1)} %get-tuple-element.60.u_ref, f32[32,16,16,128]{3,2,1,0:T(8,128)S(1)} %get-tuple-element.40.cx_ref, f32[32,16,16,128]{3,2,1,0:T(8,128)S(1)} %get-tuple-element.41.cy_ref, f32[32,16,16,128]{3,2,1,0:T(8,128)S(1)} %get-tuple-element.42.cup_ref, ...), custom_call_target="tpu_custom_call" | custom-call | flops 25165824 | bytes 8388608 | tf_op jit(solution)/shard_map/step/pallas_call | solution.py:34
  38.1 1.2 %collective-permute-done.8 = bf16[32,16,128]{2,1,0:T(8,128)(2,1)S(1)} collective-permute-done((bf16[32,16,128]{2,1,0:T(8,128)(2,1)S(1)}, bf16[32,16,128]{2,1,0:T(8,128)(2,1)S(1)}, u32[]{:S(2)}, u32[]{:S(2)}) %collective-permute-start.8) | collective-permute-done | bytes 131104 | tf_op jit(solution)/shard_map/ppermute | solution.py:328
  39.3 0.3 collective-permute-done.10
  39.6 1.0 %edge.6 = (f32[32,16,16,128]{3,2,1,0:T(8,128)S(1)}, bf16[32,16,128]{2,1,0:T(8,128)(2,1)S(1)}, bf16[32,16,128]{2,1,0:T(8,128)(2,1)S(1)}, bf16[32,16,128]{2,1,0:T(8,128)(2,1)S(1)}, bf16[32,16,128]{2,1,0:T(8,128)(2,1)S(1)}) custom-call(f32[32,16,16,128]{3,2,1,0:T(8,128)S(1)} %step.4.w_in, ...), custom_call_target="tpu_custom_call", output_to_operand_aliasing={{0}: (0, {})} | custom-call | flops 1048576 | bytes 1048576 | tf_op jit(solution)/shard_map/edge/pallas_call | solution.py:34
  40.6 0.1 collective-permute-start.13
  40.6 1.5 %collective-permute-start.12 = (bf16[32,16,128]{2,1,0:T(8,128)(2,1)S(1)}, bf16[32,16,128]{2,1,0:T(8,128)(2,1)S(1)}, u32[]{:S(2)}, u32[]{:S(2)}) collective-permute-start(bf16[32,16,128]{2,1,0:T(8,128)(2,1)S(1)} %get-tuple-element.90), channel_id=1, source_target_pairs={{0,8},{1,9},{8,0},{9,1},{16,24},{17,25},{24,16},{25,17},{2,10},{3,... | collective-permute-start | bytes 393224 | tf_op jit(solution)/shard_map/ppermute | solution.py:328
  42.1 0.1 collective-permute-start.15
  42.2 2.1 %collective-permute-start.14 = (bf16[32,16,128]{2,1,0:T(8,128)(2,1)S(1)}, bf16[32,16,128]{2,1,0:T(8,128)(2,1)S(1)}, u32[]{:S(2)}, u32[]{:S(2)}) collective-permute-start(bf16[32,16,128]{2,1,0:T(8,128)(2,1)S(1)} %get-tuple-element.86), channel_id=1, source_target_pairs={{0,2},{1,3},{2,0},{3,1},{4,6},{5,7},{6,4},{7,5},{8,10},{9,11},{10,... | collective-permute-start | bytes 393224 | tf_op jit(solution)/shard_map/ppermute | solution.py:328
  44.3 3.0 %step.5.w_in = f32[32,16,16,128]{3,2,1,0:T(8,128)S(1)} custom-call(f32[32,16,16,128]{3,2,1,0:T(8,128)S(1)} %get-tuple-element.65.u_ref, f32[32,16,16,128]{3,2,1,0:T(8,128)S(1)} %get-tuple-element.40.cx_ref, f32[32,16,16,128]{3,2,1,0:T(8,128)S(1)} %get-tuple-element.41.cy_ref, f32[32,16,16,128]{3,2,1,0:T(8,128)S(1)} %get-tuple-element.42.cup_ref, ...), custom_call_target="tpu_custom_call" | custom-call | flops 25165824 | bytes 8388608 | tf_op jit(solution)/shard_map/step/pallas_call | solution.py:34
  47.3 0.5 collective-permute-done.12
  47.9 0.2 collective-permute-done.14
  48.1 0.7 %edge.7.u_ref = f32[32,16,16,128]{3,2,1,0:T(8,128)S(1)} custom-call(f32[32,16,16,128]{3,2,1,0:T(8,128)S(1)} %step.5.w_in, f32[32,16,16,128]{3,2,1,0:T(8,128)S(1)} %get-tuple-element.65.u_ref, f32[32,16,128]{2,1,0:T(8,128)S(1)} %get-tuple-element.112.cx0, f32[32,16,128]{2,1,0:T(8,128)S(1)} %get-tuple-element.111.cx1, ...), custom_call_target="tpu_custom_call", output_to_operand_aliasing={{}: (0, {})} | custom-call | flops 1048576 | bytes 1048576 | tf_op jit(solution)/shard_map/edge/pallas_call | solution.py:34
  48.9 2.0 %corange.1 = (bf16[16,2,256,128]{3,2,1,0:T(8,128)(2,1)S(1)}, f32[32,64]{1,0:T(8,128)S(1)}, f32[32,16,16,128]{3,2,1,0:T(8,128)}) custom-call(bf16[16,2,512,128]{3,2,1,0:T(8,128)(2,1)S(1)} %get-tuple-element.39.refs_0_.psi_ref, f32[32,16,16,128]{3,2,1,0:T(8,128)S(1)} %edge.7.u_ref), custom_call_target="tpu_custom_call" | custom-call | flops 1073741824 | bytes 4194304 | tf_op jit(solution)/shard_map/corange/pallas_call | solution.py:34
  50.9 0.1 collective-permute-start.16
  51.0 1.6 %collective-permute-start.19 = (f32[32,64]{1,0:T(8,128)S(1)}, f32[32,64]{1,0:T(8,128)S(1)}, u32[]{:S(2)}, u32[]{:S(2)}) collective-permute-start(f32[32,64]{1,0:T(8,128)S(1)} %get-tuple-element.73), channel_id=1, source_target_pairs={{0,24},{8,16},{16,8},{24,0},{1,25},{9,17},{17,9},{25,1},{2,26},{10... | collective-permute-start | bytes 24584 | tf_op jit(solution)/shard_map/ppermute | solution.py:340
  52.6 0.5 collective-permute-start.18
  53.1 1.4 %collective-permute-start.17 = (f32[32,64]{1,0:T(8,128)S(1)}, f32[32,64]{1,0:T(8,128)S(1)}, u32[]{:S(2)}, u32[]{:S(2)}) collective-permute-start(f32[32,64]{1,0:T(8,128)S(1)} %get-tuple-element.73), channel_id=1, source_target_pairs={{0,8},{8,0},{16,24},{24,16},{1,9},{9,1},{17,25},{25,17},{2,10},{10... | collective-permute-start | bytes 24584 | tf_op jit(solution)/shard_map/ppermute | solution.py:340
  54.6 0.6 collective-permute-done.16.other_ref
  55.1 3.7 %range.1 = (bf16[32,16,16,128]{3,2,1,0:T(8,128)(2,1)}, f32[32,64]{1,0:T(8,128)S(1)}) custom-call(bf16[2,256,256]{2,1,0:T(8,128)(2,1)S(1)} %get-tuple-element.54.refs_1_.weight_ref, bf16[16,2,256,128]{3,2,1,0:T(8,128)(2,1)S(1)} %get-tuple-element.71.own_ref, bf16[16,2,256,128]{3,2,1,0:T(8,128)(2,1)S(1)} %collective-permute-done.16.other_ref, ...), custom_call_target="tpu_custom_call" | custom-call | flops 1073741824 | bytes 4194304 | tf_op jit(solution)/shard_map/range/pallas_call | solution.py:34
  58.9 1.6 %collective-permute-start.22 = (f32[32,64]{1,0:T(8,128)S(1)}, f32[32,64]{1,0:T(8,128)S(1)}, u32[]{:S(2)}, u32[]{:S(2)}) collective-permute-start(f32[32,64]{1,0:T(8,128)S(1)} %add_add_fusion), channel_id=1, source_target_pairs={{0,6},{2,4},{4,2},{6,0},{1,7},{3,5},{5,3},{7,1},{8,14},{10,12},{12... | collective-permute-start | bytes 24584 | tf_op jit(solution)/shard_map/ppermute | solution.py:340
  60.5 1.1 %collective-permute-start.21 = (f32[32,64]{1,0:T(8,128)S(1)}, f32[32,64]{1,0:T(8,128)S(1)}, u32[]{:S(2)}, u32[]{:S(2)}) collective-permute-start(f32[32,64]{1,0:T(8,128)S(1)} %add_add_fusion), channel_id=1, source_target_pairs={{0,4},{2,6},{4,0},{6,2},{1,5},{3,7},{5,1},{7,3},{8,12},{10,14},{12... | collective-permute-start | bytes 24584 | tf_op jit(solution)/shard_map/ppermute | solution.py:340
  61.6 1.8 %collective-permute-start.20 = (f32[32,64]{1,0:T(8,128)S(1)}, f32[32,64]{1,0:T(8,128)S(1)}, u32[]{:S(2)}, u32[]{:S(2)}) collective-permute-start(f32[32,64]{1,0:T(8,128)S(1)} %add_add_fusion), channel_id=1, source_target_pairs={{0,2},{2,0},{4,6},{6,4},{1,3},{3,1},{5,7},{7,5},{8,10},{10,8},{12,... | collective-permute-start | bytes 24584 | tf_op jit(solution)/shard_map/ppermute | solution.py:340
  63.3 1.2 %collective-permute-done.22 = f32[32,64]{1,0:T(8,128)S(1)} collective-permute-done((f32[32,64]{1,0:T(8,128)S(1)}, f32[32,64]{1,0:T(8,128)S(1)}, u32[]{:S(2)}, u32[]{:S(2)}) %collective-permute-start.22) | collective-permute-done | bytes 8224 | tf_op jit(solution)/shard_map/ppermute | solution.py:340
  64.6 0.5 collective-permute-done.21
  65.1 0.2 collective-permute-done.20
  65.3 0.6 fusion
  (41 shorter events, 0.8 us)
Async XLA Ops:
  0.6 9.5 %copy-start = (bf16[64,64]{1,0:T(8,128)(2,1)S(1)}, bf16[64,64]{1,0:T(8,128)(2,1)}, u32[]{:S(2)}) copy-start(bf16[64,64]{1,0:T(8,128)(2,1)} %param.8) | copy-start | bytes 24580
  2.4 19.1 %collective-permute-start.1 = (bf16[2,32,16,128]{3,2,1,0:T(8,128)(2,1)S(1)}, bf16[2,32,16,128]{3,2,1,0:T(8,128)(2,1)S(1)}, u32[]{:S(2)}, u32[]{:S(2)}) collective-permute-start(bf16[2,32,16,128]{3,2,1,0:T(8,128)(2,1)S(1)} %get-tuple-element.81), channel_id=1, source_target_pairs={{0,1},{1,0},{8,16},{9,17},{16,8},{17,9},{24,25},{25,24},{2,3},{3,2... | collective-permute-start | bytes 786440 | tf_op jit(solution)/shard_map/ppermute | solution.py:329
  2.9 18.6 %collective-permute-start = (bf16[2,32,16,128]{3,2,1,0:T(8,128)(2,1)S(1)}, bf16[2,32,16,128]{3,2,1,0:T(8,128)(2,1)S(1)}, u32[]{:S(2)}, u32[]{:S(2)}) collective-permute-start(bf16[2,32,16,128]{3,2,1,0:T(8,128)(2,1)S(1)} %get-tuple-element.82), channel_id=1, source_target_pairs={{0,8},{1,9},{8,0},{9,1},{16,24},{17,25},{24,16},{25,17},{2,10},{3,... | collective-permute-start | bytes 786440 | tf_op jit(solution)/shard_map/ppermute | solution.py:328
  6.9 14.7 %collective-permute-start.3 = (bf16[2,32,16,128]{3,2,1,0:T(8,128)(2,1)S(1)}, bf16[2,32,16,128]{3,2,1,0:T(8,128)(2,1)S(1)}, u32[]{:S(2)}, u32[]{:S(2)}) collective-permute-start(bf16[2,32,16,128]{3,2,1,0:T(8,128)(2,1)S(1)} %get-tuple-element.77), channel_id=1, source_target_pairs={{0,1},{1,0},{2,4},{3,5},{4,2},{5,3},{6,7},{7,6},{8,9},{9,8},{10,12... | collective-permute-start | bytes 786440 | tf_op jit(solution)/shard_map/ppermute | solution.py:329
  7.0 14.6 %collective-permute-start.2 = (bf16[2,32,16,128]{3,2,1,0:T(8,128)(2,1)S(1)}, bf16[2,32,16,128]{3,2,1,0:T(8,128)(2,1)S(1)}, u32[]{:S(2)}, u32[]{:S(2)}) collective-permute-start(bf16[2,32,16,128]{3,2,1,0:T(8,128)(2,1)S(1)} %get-tuple-element.78), channel_id=1, source_target_pairs={{0,2},{1,3},{2,0},{3,1},{4,6},{5,7},{6,4},{7,5},{8,10},{9,11},{10,... | collective-permute-start | bytes 786440 | tf_op jit(solution)/shard_map/ppermute | solution.py:328
  22.8 6.5 %collective-permute-start.5 = (bf16[32,16,128]{2,1,0:T(8,128)(2,1)S(1)}, bf16[32,16,128]{2,1,0:T(8,128)(2,1)S(1)}, u32[]{:S(2)}, u32[]{:S(2)}) collective-permute-start(bf16[32,16,128]{2,1,0:T(8,128)(2,1)S(1)} %get-tuple-element.105), channel_id=1, source_target_pairs={{0,1},{1,0},{8,16},{9,17},{16,8},{17,9},{24,25},{25,24},{2,3},{3,2... | collective-permute-start | bytes 393224 | tf_op jit(solution)/shard_map/ppermute | solution.py:329
  22.9 7.3 %collective-permute-start.4 = (bf16[32,16,128]{2,1,0:T(8,128)(2,1)S(1)}, bf16[32,16,128]{2,1,0:T(8,128)(2,1)S(1)}, u32[]{:S(2)}, u32[]{:S(2)}) collective-permute-start(bf16[32,16,128]{2,1,0:T(8,128)(2,1)S(1)} %get-tuple-element.106), channel_id=1, source_target_pairs={{0,8},{1,9},{8,0},{9,1},{16,24},{17,25},{24,16},{25,17},{2,10},{3,... | collective-permute-start | bytes 393224 | tf_op jit(solution)/shard_map/ppermute | solution.py:328
  24.5 5.8 %collective-permute-start.7 = (bf16[32,16,128]{2,1,0:T(8,128)(2,1)S(1)}, bf16[32,16,128]{2,1,0:T(8,128)(2,1)S(1)}, u32[]{:S(2)}, u32[]{:S(2)}) collective-permute-start(bf16[32,16,128]{2,1,0:T(8,128)(2,1)S(1)} %get-tuple-element.101), channel_id=1, source_target_pairs={{0,1},{1,0},{2,4},{3,5},{4,2},{5,3},{6,7},{7,6},{8,9},{9,8},{10,12... | collective-permute-start | bytes 393224 | tf_op jit(solution)/shard_map/ppermute | solution.py:329
  24.6 5.9 %collective-permute-start.6 = (bf16[32,16,128]{2,1,0:T(8,128)(2,1)S(1)}, bf16[32,16,128]{2,1,0:T(8,128)(2,1)S(1)}, u32[]{:S(2)}, u32[]{:S(2)}) collective-permute-start(bf16[32,16,128]{2,1,0:T(8,128)(2,1)S(1)} %get-tuple-element.102), channel_id=1, source_target_pairs={{0,2},{1,3},{2,0},{3,1},{4,6},{5,7},{6,4},{7,5},{8,10},{9,11},{10,... | collective-permute-start | bytes 393224 | tf_op jit(solution)/shard_map/ppermute | solution.py:328
  31.5 6.6 %collective-permute-start.9 = (bf16[32,16,128]{2,1,0:T(8,128)(2,1)S(1)}, bf16[32,16,128]{2,1,0:T(8,128)(2,1)S(1)}, u32[]{:S(2)}, u32[]{:S(2)}) collective-permute-start(bf16[32,16,128]{2,1,0:T(8,128)(2,1)S(1)} %get-tuple-element.97), channel_id=1, source_target_pairs={{0,1},{1,0},{8,16},{9,17},{16,8},{17,9},{24,25},{25,24},{2,3},{3,2... | collective-permute-start | bytes 393224 | tf_op jit(solution)/shard_map/ppermute | solution.py:329
  31.6 7.7 %collective-permute-start.8 = (bf16[32,16,128]{2,1,0:T(8,128)(2,1)S(1)}, bf16[32,16,128]{2,1,0:T(8,128)(2,1)S(1)}, u32[]{:S(2)}, u32[]{:S(2)}) collective-permute-start(bf16[32,16,128]{2,1,0:T(8,128)(2,1)S(1)} %get-tuple-element.98), channel_id=1, source_target_pairs={{0,8},{1,9},{8,0},{9,1},{16,24},{17,25},{24,16},{25,17},{2,10},{3,... | collective-permute-start | bytes 393224 | tf_op jit(solution)/shard_map/ppermute | solution.py:328
  33.5 5.7 %collective-permute-start.11 = (bf16[32,16,128]{2,1,0:T(8,128)(2,1)S(1)}, bf16[32,16,128]{2,1,0:T(8,128)(2,1)S(1)}, u32[]{:S(2)}, u32[]{:S(2)}) collective-permute-start(bf16[32,16,128]{2,1,0:T(8,128)(2,1)S(1)} %get-tuple-element.93), channel_id=1, source_target_pairs={{0,1},{1,0},{2,4},{3,5},{4,2},{5,3},{6,7},{7,6},{8,9},{9,8},{10,12... | collective-permute-start | bytes 393224 | tf_op jit(solution)/shard_map/ppermute | solution.py:329
  33.6 5.9 %collective-permute-start.10 = (bf16[32,16,128]{2,1,0:T(8,128)(2,1)S(1)}, bf16[32,16,128]{2,1,0:T(8,128)(2,1)S(1)}, u32[]{:S(2)}, u32[]{:S(2)}) collective-permute-start(bf16[32,16,128]{2,1,0:T(8,128)(2,1)S(1)} %get-tuple-element.94), channel_id=1, source_target_pairs={{0,2},{1,3},{2,0},{3,1},{4,6},{5,7},{6,4},{7,5},{8,10},{9,11},{10,... | collective-permute-start | bytes 393224 | tf_op jit(solution)/shard_map/ppermute | solution.py:328
  40.6 6.8 %collective-permute-start.13 = (bf16[32,16,128]{2,1,0:T(8,128)(2,1)S(1)}, bf16[32,16,128]{2,1,0:T(8,128)(2,1)S(1)}, u32[]{:S(2)}, u32[]{:S(2)}) collective-permute-start(bf16[32,16,128]{2,1,0:T(8,128)(2,1)S(1)} %get-tuple-element.89), channel_id=1, source_target_pairs={{0,1},{1,0},{8,16},{9,17},{16,8},{17,9},{24,25},{25,24},{2,3},{3,2... | collective-permute-start | bytes 393224 | tf_op jit(solution)/shard_map/ppermute | solution.py:329
  40.6 7.2 %collective-permute-start.12 = (bf16[32,16,128]{2,1,0:T(8,128)(2,1)S(1)}, bf16[32,16,128]{2,1,0:T(8,128)(2,1)S(1)}, u32[]{:S(2)}, u32[]{:S(2)}) collective-permute-start(bf16[32,16,128]{2,1,0:T(8,128)(2,1)S(1)} %get-tuple-element.90), channel_id=1, source_target_pairs={{0,8},{1,9},{8,0},{9,1},{16,24},{17,25},{24,16},{25,17},{2,10},{3,... | collective-permute-start | bytes 393224 | tf_op jit(solution)/shard_map/ppermute | solution.py:328
  42.1 5.8 %collective-permute-start.15 = (bf16[32,16,128]{2,1,0:T(8,128)(2,1)S(1)}, bf16[32,16,128]{2,1,0:T(8,128)(2,1)S(1)}, u32[]{:S(2)}, u32[]{:S(2)}) collective-permute-start(bf16[32,16,128]{2,1,0:T(8,128)(2,1)S(1)} %get-tuple-element.85), channel_id=1, source_target_pairs={{0,1},{1,0},{2,4},{3,5},{4,2},{5,3},{6,7},{7,6},{8,9},{9,8},{10,12... | collective-permute-start | bytes 393224 | tf_op jit(solution)/shard_map/ppermute | solution.py:329
  42.2 5.9 %collective-permute-start.14 = (bf16[32,16,128]{2,1,0:T(8,128)(2,1)S(1)}, bf16[32,16,128]{2,1,0:T(8,128)(2,1)S(1)}, u32[]{:S(2)}, u32[]{:S(2)}) collective-permute-start(bf16[32,16,128]{2,1,0:T(8,128)(2,1)S(1)} %get-tuple-element.86), channel_id=1, source_target_pairs={{0,2},{1,3},{2,0},{3,1},{4,6},{5,7},{6,4},{7,5},{8,10},{9,11},{10,... | collective-permute-start | bytes 393224 | tf_op jit(solution)/shard_map/ppermute | solution.py:328
  50.9 14.4 %copy-start.1 = (f32[64,32]{0,1:T(8,128)S(1)}, f32[64,32]{0,1:T(8,128)}, u32[]{:S(2)}) copy-start(f32[64,32]{0,1:T(8,128)} %param.11) | copy-start | bytes 24580
  50.9 4.2 %collective-permute-start.16 = (bf16[16,2,256,128]{3,2,1,0:T(8,128)(2,1)S(1)}, bf16[16,2,256,128]{3,2,1,0:T(8,128)(2,1)S(1)}, u32[]{:S(2)}, u32[]{:S(2)}) collective-permute-start(bf16[16,2,256,128]{3,2,1,0:T(8,128)(2,1)S(1)} %get-tuple-element.71.own_ref), channel_id=1, source_target_pairs={{0,1},{1,0},{2,3},{3,2},{4,5},{5,4},{6,7},{7,6},{8,9},{9,8},{10,11... | collective-permute-start | bytes 6291464 | tf_op jit(solution)/shard_map/ppermute | solution.py:434
  51.0 7.8 %collective-permute-start.19 = (f32[32,64]{1,0:T(8,128)S(1)}, f32[32,64]{1,0:T(8,128)S(1)}, u32[]{:S(2)}, u32[]{:S(2)}) collective-permute-start(f32[32,64]{1,0:T(8,128)S(1)} %get-tuple-element.73), channel_id=1, source_target_pairs={{0,24},{8,16},{16,8},{24,0},{1,25},{9,17},{17,9},{25,1},{2,26},{10... | collective-permute-start | bytes 24584 | tf_op jit(solution)/shard_map/ppermute | solution.py:340
  52.6 6.2 %collective-permute-start.18 = (f32[32,64]{1,0:T(8,128)S(1)}, f32[32,64]{1,0:T(8,128)S(1)}, u32[]{:S(2)}, u32[]{:S(2)}) collective-permute-start(f32[32,64]{1,0:T(8,128)S(1)} %get-tuple-element.73), channel_id=1, source_target_pairs={{0,16},{8,24},{16,0},{24,8},{1,17},{9,25},{17,1},{25,9},{2,18},{10... | collective-permute-start | bytes 24584 | tf_op jit(solution)/shard_map/ppermute | solution.py:340
  53.1 5.7 %collective-permute-start.17 = (f32[32,64]{1,0:T(8,128)S(1)}, f32[32,64]{1,0:T(8,128)S(1)}, u32[]{:S(2)}, u32[]{:S(2)}) collective-permute-start(f32[32,64]{1,0:T(8,128)S(1)} %get-tuple-element.73), channel_id=1, source_target_pairs={{0,8},{8,0},{16,24},{24,16},{1,9},{9,1},{17,25},{25,17},{2,10},{10... | collective-permute-start | bytes 24584 | tf_op jit(solution)/shard_map/ppermute | solution.py:340
  58.9 5.7 %collective-permute-start.22 = (f32[32,64]{1,0:T(8,128)S(1)}, f32[32,64]{1,0:T(8,128)S(1)}, u32[]{:S(2)}, u32[]{:S(2)}) collective-permute-start(f32[32,64]{1,0:T(8,128)S(1)} %add_add_fusion), channel_id=1, source_target_pairs={{0,6},{2,4},{4,2},{6,0},{1,7},{3,5},{5,3},{7,1},{8,14},{10,12},{12... | collective-permute-start | bytes 24584 | tf_op jit(solution)/shard_map/ppermute | solution.py:340
  60.5 4.6 %collective-permute-start.21 = (f32[32,64]{1,0:T(8,128)S(1)}, f32[32,64]{1,0:T(8,128)S(1)}, u32[]{:S(2)}, u32[]{:S(2)}) collective-permute-start(f32[32,64]{1,0:T(8,128)S(1)} %add_add_fusion), channel_id=1, source_target_pairs={{0,4},{2,6},{4,0},{6,2},{1,5},{3,7},{5,1},{7,3},{8,12},{10,14},{12... | collective-permute-start | bytes 24584 | tf_op jit(solution)/shard_map/ppermute | solution.py:340
  61.6 3.8 %collective-permute-start.20 = (f32[32,64]{1,0:T(8,128)S(1)}, f32[32,64]{1,0:T(8,128)S(1)}, u32[]{:S(2)}, u32[]{:S(2)}) collective-permute-start(f32[32,64]{1,0:T(8,128)S(1)} %add_add_fusion), channel_id=1, source_target_pairs={{0,2},{2,0},{4,6},{6,4},{1,3},{3,1},{5,7},{7,5},{8,10},{10,8},{12,... | collective-permute-start | bytes 24584 | tf_op jit(solution)/shard_map/ppermute | solution.py:340

commit v3 on v2

--- a/solution.py
+++ b/solution.py
@@ -72,24 +72,33 @@
     return ref.reshape(samples * nx * ny, nz)
 
 
-def coef_kernel(k_hbm, cx_ref, cy_ref, cup_ref, cdown_ref, kx0, kx1, ky0, ky1, buf, sem):
-    samples, nx, ny, nz = k_hbm.shape
+def first_kernel(
+    u_hbm, k_hbm, u_ref, w_ref, cx_ref, cy_ref, cup_ref, cdown_ref, kx0, kx1, ky0, ky1, buf, sem
+):
+    samples, nx, ny, nz = u_ref.shape
     shape = (BLOCK, ny, nz)
     groups = samples // BLOCK
     y_open = lax.broadcasted_iota(jnp.int32, shape, 1) < ny - 1
     lane = lax.broadcasted_iota(jnp.int32, shape, 2)
-
-    def copy_of(g):
+    rows = flat(buf)
+
+    def copies(g):
         part = pl.ds(g * BLOCK, BLOCK)
-        return pltpu.make_async_copy(k_hbm.at[part], buf.at[part], sem.at[g])
+        return (
+            pltpu.make_async_copy(k_hbm.at[part], buf.at[part], sem.at[0, g]),
+            pltpu.make_async_copy(u_hbm.at[part], u_ref.at[part], sem.at[1, g]),
+        )
 
     for g in range(groups):
-        copy_of(g).start()
-    rows = flat(buf)
-    for g in range(groups):
-        copy_of(g).wait()
-        part = slice(g * BLOCK, (g + 1) * BLOCK)
-        for s in range(g * BLOCK, (g + 1) * BLOCK):
+        for copy in copies(g):
+            copy.start()
+
+    def before(g):
+        for copy in copies(g):
+            copy.wait()
+        part = pl.ds(g * BLOCK, BLOCK)
+        for i in range(BLOCK):
+            s = g * BLOCK + i
             ky0[s] = rows[y_line(buf, s, 0), :] * HALF
             ky1[s] = rows[y_line(buf, s, ny - 1), :] * HALF
         k = buf[part, 0] * HALF
@@ -105,6 +114,8 @@
                 k = k_next
         kx1[part] = k
 
+    step_body(u_ref, cx_ref, cy_ref, cup_ref, cdown_ref, w_ref, before)
+
 
 def difference_matrix(nz):
     row = lax.broadcasted_iota(jnp.int32, (nz, nz), 0)
@@ -116,29 +127,36 @@
     return jnp.concatenate([both, both], axis=0)
 
 
-def first_step_kernel(u_hbm, cx_ref, cy_ref, cup_ref, cdown_ref, u_ref, w_ref, sem):
-    groups = u_ref.shape[0] // BLOCK
+def step_kernel(u_ref, cx_ref, cy_ref, cup_ref, cdown_ref, *refs):
+    step_body(u_ref, cx_ref, cy_ref, cup_ref, cdown_ref, refs[-1])
+
+
+def last_step_kernel(u_ref, cx_ref, cy_ref, cup_ref, cdown_ref, *refs):
+    w_ref, state_hbm, sem = refs[-3:]
+    half = u_ref.shape[0] // BLOCK // 2
 
     def copy_of(g):
         part = pl.ds(g * BLOCK, BLOCK)
-        return pltpu.make_async_copy(u_hbm.at[part], u_ref.at[part], sem.at[g])
-
-    for g in range(groups):
-        copy_of(g).start()
-    step_body(u_ref, cx_ref, cy_ref, cup_ref, cdown_ref, w_ref, lambda g: copy_of(g).wait())
-
-
-def step_kernel(u_ref, cx_ref, cy_ref, cup_ref, cdown_ref, *refs):
-    step_body(u_ref, cx_ref, cy_ref, cup_ref, cdown_ref, refs[-1], lambda g: None)
-
-
-def step_body(u_ref, cx_ref, cy_ref, cup_ref, cdown_ref, w_ref, before):
+        return pltpu.make_async_copy(w_ref.at[part], state_hbm.at[part], sem.at[g])
+
+    def after(g):
+        @pl.when(g < half)
+        def _():
+            copy_of(g).start()
+
+    step_body(u_ref, cx_ref, cy_ref, cup_ref, cdown_ref, w_ref, after=after)
+    for g in range(half):
+        copy_of(g).wait()
+
+
+def step_body(u_ref, cx_ref, cy_ref, cup_ref, cdown_ref, w_ref, before=None, after=None):
     samples, nx, ny, nz = u_ref.shape
     shape = (BLOCK, ny, nz)
     matrix = difference_matrix(nz)
 
     def body(g, carry):
-        before(g)
+        if before:
+            before(g)
         part = pl.ds(g * BLOCK, BLOCK)
         u = u_ref[part, 0]
         for x in range(nx):
@@ -160,6 +178,8 @@
             w_ref[part, x] = total
             if x + 1 < nx:
                 u, flux_low = u_next, flux
+        if after:
+            after(g)
         return carry
 
     lax.fori_loop(0, samples // BLOCK, body, 0)
@@ -220,9 +240,13 @@
     return jnp.where(row == col, full, 0.0).astype(BF)
 
 
-def psi_kernel(psi_hbm, omega_ref, out_ref, weight_ref, buf, sem):
+def psi_kernel(psi_hbm, prev_hbm, omega_ref, out_ref, x_ref, y_ref, weight_ref, prev_ref, buf, wide, sem):
     ranks, nx, ny, nz = psi_hbm.shape
     parts = 4
+    rows = wide.reshape(ranks * ny, nz)
+
+    def line(y):
+        return rows[pl.ds(y, ranks, stride=ny), :].astype(BF)
 
     def copy_of(i):
         part = pl.ds(i * (nx // parts), nx // parts)
@@ -230,69 +254,84 @@
 
     for i in range(parts):
         copy_of(i).start()
+    prev_copy = pltpu.make_async_copy(prev_hbm, prev_ref, sem.at[parts])
+    prev_copy.start()
     for i in range(omega_ref.shape[0]):
         weight_ref[i] = spread(omega_ref[i])
 
     def body(x, carry):
-        split_into(out_ref, x, buf[:, x].astype(F32))
+        value = buf[:, x].astype(F32)
+        split_into(out_ref, x, value)
+        wide[...] = value
+        y_ref[0, x] = line(0)
+        y_ref[1, x] = line(ny - 1)
         return carry
 
     for i in range(parts):
         copy_of(i).wait()
         lax.fori_loop(i * (nx // parts), (i + 1) * (nx // parts), body, 0)
+    for end in range(2):
+        wide[...] = buf[:, end * (nx - 1)].astype(F32)
+        for y in range(ny):
+            x_ref[end, y] = line(y)
+    prev_copy.wait()
 
 
 def side_by_side(ref, x):
     return jnp.concatenate([ref[x, h] for h in range(ref.shape[1])], axis=1)
 
 
-def range_kernel(weight_ref, own_ref, other_ref, prev_hbm, out_ref, done_ref, prev, buf, sem):
-    ranks, nx, ny, nz = prev_hbm.shape
+def range_kernel(
+    weight_ref, own_ref, other_ref, prev_ref, u_ref, state_in, out_ref, state_hbm, done_ref, buf, sem
+):
+    del state_in
+    ranks, nx, ny, nz = prev_ref.shape
     parts = 4
-
-    def prev_copy(i):
-        part = pl.ds(i * (nx // parts), nx // parts)
-        return pltpu.make_async_copy(prev_hbm.at[:, part], prev.at[:, part], sem.at[1, i])
-
-    for i in range(parts):
-        prev_copy(i).start()
+    inner = pl.ds(1, nx - 2)
+    copies = []
+    for i, (x, y) in enumerate(((0, 0), (nx - 1, ny - 1))):
+        copies.append(pltpu.make_async_copy(u_ref.at[:, x], state_hbm.at[:, x], sem.at[1, i]))
+        copies.append(
+            pltpu.make_async_copy(u_ref.at[:, inner, y], state_hbm.at[:, inner, y], sem.at[1, 2 + i])
+        )
+    for copy in copies:
+        copy.start()
+    done_ref[...] = jnp.zeros_like(done_ref)
 
     def copy_of(i):
         part = pl.ds(i * (nx // parts), nx // parts)
         return pltpu.make_async_copy(buf.at[:, part], out_ref.at[:, part], sem.at[0, i])
 
-    done_ref[...] = jnp.zeros_like(done_ref)
-
-    def body(x):
-        value = jnp.dot(weight_ref[0], side_by_side(own_ref, x), preferred_element_type=F32)
-        value += jnp.dot(weight_ref[1], side_by_side(other_ref, x), preferred_element_type=F32)
-        halves = [
-            value[:, h * nz : (h + 1) * nz].reshape(ranks, ROWS, nz) for h in range(ny // ROWS)
-        ]
-        total = jnp.concatenate(halves, axis=1) + prev[:, x].astype(F32)
-        buf[:, x] = total.astype(BF)
-
     for i in range(parts):
-        prev_copy(i).wait()
         for x in range(i * (nx // parts), (i + 1) * (nx // parts)):
-            body(x)
+            value = jnp.dot(weight_ref[0], side_by_side(own_ref, x), preferred_element_type=F32)
+            value += jnp.dot(weight_ref[1], side_by_side(other_ref, x), preferred_element_type=F32)
+            halves = [
+                value[:, h * nz : (h + 1) * nz].reshape(ranks, ROWS, nz) for h in range(ny // ROWS)
+            ]
+            total = jnp.concatenate(halves, axis=1) + prev_ref[:, x].astype(F32)
+            buf[:, x] = total.astype(BF)
         copy_of(i).start()
     for i in range(parts):
         copy_of(i).wait()
-
-
-def corange_kernel(psi_ref, u_ref, snap_ref, out_ref, state_hbm, acc, sem):
-    copy = pltpu.make_async_copy(u_ref, state_hbm, sem)
+    for copy in copies:
+        copy.wait()
+
+
+def corange_kernel(psi_ref, u_ref, state_in, out_ref, state_hbm, snap, acc, sem):
+    del state_in
+    samples, nx, ny, nz = u_ref.shape
+    part = pl.ds(samples // 2, samples // 2)
+    copy = pltpu.make_async_copy(u_ref.at[part], state_hbm.at[part], sem)
     copy.start()
-    samples, nx, ny, nz = u_ref.shape
     ranks = psi_ref.shape[2] // ROWS
     cols = ranks * ROWS
     for x in range(0, nx, 2):
-        split_into(snap_ref, x, u_ref[:, x])
-        split_into(snap_ref, x + 1, u_ref[:, x + 1])
-        left = jnp.concatenate([side_by_side(snap_ref, x), side_by_side(snap_ref, x + 1)], axis=1)
+        split_into(snap, x, u_ref[:, x])
+        split_into(snap, x + 1, u_ref[:, x + 1])
+        left = jnp.concatenate([side_by_side(snap, x), side_by_side(snap, x + 1)], axis=1)
         right = jnp.concatenate([side_by_side(psi_ref, x), side_by_side(psi_ref, x + 1)], axis=1)
-        part = lax.dot_general(left, right, (((1,), (1,)), ((), ())), preferred_element_type=F32)
+        part = contract(left, right)
         acc[...] = part if x == 0 else acc[...] + part
     row = lax.broadcasted_iota(jnp.int32, (ROWS, cols), 0)
     col = lax.broadcasted_iota(jnp.int32, (ROWS, cols), 1) % ROWS
@@ -303,6 +342,46 @@
     picked = jnp.where((row == col)[None], acc[...].reshape(samples, ROWS, cols), 0.0).sum(1)
     out_ref[...] = jnp.dot(picked, fold, precision=lax.Precision.HIGHEST, preferred_element_type=F32)
     copy.wait()
+
+
+def contract(left, right):
+    return lax.dot_general(left, right, (((1,), (1,)), ((), ())), preferred_element_type=F32)
+
+
+def corange_faces_kernel(
+    main_ref, px, py, u_ref, cx0, cx1, cy0, cy1, hx0, hx1, hy0, hy1, out_ref, xbuf, ybuf
+):
+    samples, nx, ny, nz = u_ref.shape
+    rows = flat(u_ref)
+    for end, x, coef, halo in ((0, 0, cx0, hx0), (1, nx - 1, cx1, hx1)):
+        xbuf[end] = coef[...] * (halo[...].astype(F32) - u_ref[:, x])
+    for end, y, coef, halo in ((0, 0, cy0, hy0), (1, ny - 1, cy1, hy1)):
+        for s in range(samples):
+            ybuf[end, s] = coef[s] * (halo[s].astype(F32) - rows[y_line(u_ref, s, y), :])
+    total = main_ref[...]
+    for buf, psi in ((xbuf, px), (ybuf, py)):
+        count = buf.shape[2]
+        lines = buf.reshape(2 * samples * count, nz)
+        for i in range(count):
+            left = [
+                lines[pl.ds(end * samples * count + i, samples, stride=count), :].astype(BF)
+                for end in range(2)
+            ]
+            right = [psi[end, i] for end in range(2)]
+            total = total + contract(jnp.concatenate(left, axis=1), jnp.concatenate(right, axis=1))
+    out_ref[...] = total
+
+
+def finish_kernel(*refs):
+    w_ref, snap_ref = refs[-2:]
+    edge_kernel(False, *refs[:-1])
+    nx = w_ref.shape[1]
+
+    def body(x, carry):
+        split_into(snap_ref, x, w_ref[:, x])
+        return carry
+
+    lax.fori_loop(0, nx, body, 0)
 
 
 def swap_pairs(count, parity, par):
@@ -321,24 +400,33 @@
     return pairs
 
 
-def exchange(low, high, axis):
-    count, par = lax.axis_size(axis), lax.axis_size("par")
-    index = lax.axis_index(axis)
-    odd = index % 2 == 1
-    first = lax.ppermute(jnp.where(odd, low, high), (axis, "par"), swap_pairs(count, 0, par))
-    second = lax.ppermute(jnp.where(odd, high, low), (axis, "par"), swap_pairs(count, 1, par))
-    zero = jnp.zeros_like(first)
-    below = jnp.where(index == 0, zero, jnp.where(odd, first, second))
-    above = jnp.where(index == count - 1, zero, jnp.where(odd, second, first))
-    return below, above
-
-
-def total_of(value, axis):
+ORDER = (("sy", 0), ("sy", 1), ("sx", 0), ("sx", 1))
+
+
+def exchange(faces):
+    ends = {"sx": faces[:2], "sy": faces[2:]}
+    par = lax.axis_size("par")
+    got = {}
+    for axis, parity in ORDER:
+        low, high = ends[axis]
+        odd = lax.axis_index(axis) % 2 == 1
+        mine = jnp.where(odd, high, low) if parity else jnp.where(odd, low, high)
+        pairs = swap_pairs(lax.axis_size(axis), parity, par)
+        got[axis, parity] = lax.ppermute(mine, (axis, "par"), pairs)
+    halos = []
+    for axis in ("sx", "sy"):
+        index, count = lax.axis_index(axis), lax.axis_size(axis)
+        odd = index % 2 == 1
+        first, second = got[axis, 0], got[axis, 1]
+        zero = jnp.zeros_like(first)
+        halos.append(jnp.where(index == 0, zero, jnp.where(odd, first, second)))
+        halos.append(jnp.where(index == count - 1, zero, jnp.where(odd, second, first)))
+    return halos
+
+
+def received(value, axis):
     count = lax.axis_size(axis)
-    total = value
-    for shift in range(1, count):
-        total = total + lax.ppermute(value, axis, [(i, i ^ shift) for i in range(count)])
-    return total
+    return [lax.ppermute(value, axis, [(i, i ^ shift) for i in range(count)]) for shift in range(1, count)]
 
 
 def per_device(initial_state, conductivity, omega, psi, range_prev, corange_prev):
@@ -362,92 +450,122 @@
         flops=cells // 2,
         nbytes=cells,
     )(initial_state, conductivity)
-    got_y = exchange(sent[2], sent[3], "sy")
-    got = exchange(sent[0], sent[1], "sx") + got_y
+    got = exchange(sent)
     halos = [g[1] for g in got]
 
     groups = samples // BLOCK
-    made = vmem_call(
-        coef_kernel,
-        [(block, F32)] * 4 + [(x_face, F32)] * 2 + [(y_face, F32)] * 2,
-        "coefs",
-        limit=6 << 20,
-        scratch=[pltpu.VMEM(block, F32), pltpu.SemaphoreType.DMA((groups,))],
-        hbm_in=(0,),
-        flops=12 * cells,
-        nbytes=8 * cells,
-    )(conductivity)
+    state, moved, *made = vmem_call(
+        first_kernel,
+        [(block, F32)] * 6 + [(x_face, F32)] * 2 + [(y_face, F32)] * 2,
+        "first",
+        limit=7 << 20,
+        scratch=[pltpu.VMEM(block, F32), pltpu.SemaphoreType.DMA((2, groups))],
+        hbm_in=(0, 1),
+        flops=36 * cells,
+        nbytes=16 * cells,
+    )(initial_state, conductivity)
     coefs, kfaces = made[:4], made[4:]
     face_coefs = [k + HALF * g[0].astype(F32) for k, g in zip(kfaces, got)]
+
     own_ranks = range_prev.shape[0]
     own_cols = lax.dynamic_slice_in_dim(omega, par * own_ranks, own_ranks, 1).T
     source = (par + par_size - 1) % par_size
     omega_blocks = jnp.stack(
         [lax.dynamic_slice_in_dim(own_cols, p * samples, samples, 1) for p in (par, source)]
     )
-    held_psi, weights = vmem_call(
+    held_psi, psi_x, psi_y, weights, prev = vmem_call(
         psi_kernel,
-        [(split_shape(psi.shape), BF), ((2, own_ranks * ROWS, samples * ROWS), BF)],
+        [
+            (split_shape(psi.shape), BF),
+            ((2, ny, ranks, nz), BF),
+            ((2, nx, ranks, nz), BF),
+            ((2, own_ranks * ROWS, samples * ROWS), BF),
+            (range_prev.shape, BF),
+        ],
         "psi",
-        limit=6 << 20,
-        scratch=[pltpu.VMEM(psi.shape, BF), pltpu.SemaphoreType.DMA((4,))],
-        hbm_in=(0,),
+        limit=7 << 20,
+        scratch=[
+            pltpu.VMEM(psi.shape, BF),
+            pltpu.VMEM((ranks, ny, nz), F32),
+            pltpu.SemaphoreType.DMA((5,)),
+        ],
+        hbm_in=(0, 1),
         flops=4 * cells,
         nbytes=4 * cells,
-    )(psi, omega_blocks)
-
-    cost = dict(flops=24 * cells, nbytes=8 * cells)
+    )(psi, range_prev, omega_blocks)
+    kept = (held_psi, psi_x, psi_y, weights, prev)
+
     for step in range(STEPS):
-        if step == 0:
-            state, moved = vmem_call(
-                first_step_kernel,
-                [(block, F32)] * 2,
-                "first_step",
-                scratch=[pltpu.SemaphoreType.DMA((groups,))],
-                hbm_in=(0,),
-                **cost,
-            )(initial_state, *coefs)
-        else:
-            got_y = exchange(edges[2], edges[3], "sy")
-            halos = exchange(edges[0], edges[1], "sx") + got_y
-            moved = vmem_call(step_kernel, [(block, F32)], "step", **cost)(state, *coefs, held_psi, weights)[0]
-        send = step < STEPS - 1
-        state, *edges = vmem_call(
-            functools.partial(edge_kernel, send),
-            [(block, F32)] + [(x_face, BF), (x_face, BF), (y_face, BF), (y_face, BF)] * send,
-            "edge",
-            aliases={0: 0},
-            flops=cells,
-            nbytes=cells,
-        )(moved, state, *face_coefs, *halos, held_psi, weights)
-
-    snapshot, partial_sum, final_state = vmem_call(
+        if step > 0:
+            halos = exchange(edges)
+            last = step == STEPS - 1
+            moved, *written = vmem_call(
+                last_step_kernel if last else step_kernel,
+                [(block, F32)] * (2 if last else 1),
+                "step",
+                scratch=[pltpu.SemaphoreType.DMA((groups,))] if last else [],
+                hbm_out=(1,),
+                flops=24 * cells,
+                nbytes=8 * cells,
+            )(state, *coefs, *kept)
+        if step < STEPS - 1:
+            state, *edges = vmem_call(
+                functools.partial(edge_kernel, True),
+                [(block, F32), (x_face, BF), (x_face, BF), (y_face, BF), (y_face, BF)],
+                "edge",
+                aliases={0: 0},
+                flops=cells,
+                nbytes=cells,
+            )(moved, state, *face_coefs, *halos, *kept)
+
+    main, written = vmem_call(
         corange_kernel,
-        [(split_shape(block), BF), ((samples, ranks), F32), (block, F32)],
+        [((samples, ranks), F32), (block, F32)],
         "corange",
         limit=6 << 20,
-        scratch=[pltpu.VMEM((samples * ROWS, ranks * ROWS), F32), pltpu.SemaphoreType.DMA],
-        hbm_out=(2,),
+        scratch=[
+            pltpu.VMEM(split_shape(block), BF),
+            pltpu.VMEM((samples * ROWS, ranks * ROWS), F32),
+            pltpu.SemaphoreType.DMA,
+        ],
+        hbm_in=(2,),
+        hbm_out=(1,),
+        aliases={2: 1},
         flops=2 * ranks * ROWS * cells,
         nbytes=4 * cells,
-    )(held_psi, state)
+    )(held_psi, moved, *written)
+    partial_sum = vmem_call(
+        corange_faces_kernel,
+        [((samples, ranks), F32)],
+        "corange_faces",
+        scratch=[pltpu.VMEM((2,) + x_face, F32), pltpu.VMEM((2,) + y_face, F32)],
+        flops=cells,
+        nbytes=cells,
+    )(main, psi_x, psi_y, state, *face_coefs, *halos)[0]
+    first_sums = received(partial_sum, "sx")
+    final, snapshot = vmem_call(
+        finish_kernel,
+        [(block, F32), (split_shape(block), BF)],
+        "finish",
+        aliases={0: 0},
+        flops=cells,
+        nbytes=2 * cells,
+    )(moved, state, *face_coefs, *halos, prev, weights, partial_sum)
     other = lax.ppermute(snapshot, "par", [(i, (i + 1) % par_size) for i in range(par_size)])
-    range_sketch, done = vmem_call(
+    range_sketch, final_state, done = vmem_call(
         range_kernel,
-        [(range_prev.shape, BF), ((samples, ranks), F32)],
+        [(range_prev.shape, BF), (block, F32), ((samples, ranks), F32)],
         "range",
-        limit=8 << 20,
-        scratch=[
-            pltpu.VMEM(range_prev.shape, BF),
-            pltpu.VMEM(range_prev.shape, BF),
-            pltpu.SemaphoreType.DMA((2, 4)),
-        ],
-        hbm_in=(3,),
-        hbm_out=(0,),
+        limit=6 << 20,
+        scratch=[pltpu.VMEM(range_prev.shape, BF), pltpu.SemaphoreType.DMA((2, 4))],
+        hbm_in=(5,),
+        hbm_out=(0, 1),
+        aliases={5: 1},
         flops=2 * ranks * ROWS * cells,
         nbytes=4 * cells,
-    )(weights, snapshot, other, range_prev)
-    corange = corange_prev.T + total_of(total_of(partial_sum, "sx") + done, "sy")
+    )(weights, snapshot, other, prev, final, written)
+    line_sum = sum(first_sums, partial_sum) + done
+    corange = sum(received(line_sum, "sy"), corange_prev.T + line_sum)
     return final_state, range_sketch, corange.T
 
 

time: 66.1 us -> 64.1 us (0.970)
  Pallas kernels: 31.1 us -> 29.3 us
    pallas_call x13, Pallas kernels: 31.1 us -> 29.3 us  [call(): pl.pallas_call(kernel, out_shape=out_shape, in_specs=in_specs, out_specs=...]
  transfers between devices with their start and end apart: 23 -> 23, of which waited for: 10 -> 7; matrix products, arithmetic and copies ran while one was open for 1% -> 1% of each run, Pallas kernels for 36% -> 36%
where the time goes in v3:
time: 64.1 us; the launch traced here: 64 us
  Pallas kernels  29.3 us (46%)
  starting transfers between devices  26.4 us (41%)
  waiting for transfers between devices  5.68 us (9%)
  other arithmetic  1.21 us (2%)
  between operations  1.08 us (2%)
    pallas_call x13, Pallas kernels, call(): pl.pallas_call(kernel, out_shape=out_shape, in_specs=in_specs, out_specs=...  29.3 us
    ppermute x16, starting transfers between devices, exchange(): got[axis, parity] = lax.ppermute(mine, (axis, 'par'), pairs)  18.3 us
    ppermute x6, starting transfers between devices, received(): lax.ppermute(value, axis, [(i, i ^ shift) for i in range(count)])  8.01 us
    ppermute x16, waiting for transfers between devices, exchange(): got[axis, parity] = lax.ppermute(mine, (axis, 'par'), pairs)  2.58 us
    ppermute x6, waiting for transfers between devices, received(): lax.ppermute(value, axis, [(i, i ^ shift) for i in range(count)])  2.51 us
  transfers between devices with their start and end apart: 23, of which 7 were waited for; matrix products, arithmetic and copies ran while one was open for 1% of the time, Pallas kernels for 36%

profile of v3, /device:TPU:0, one launch (start us, length us, event | category | flops | bytes accessed | tf_op | source)
XLA Modules:
  0.0 64.0 jit_solution(12946482414176610196)
XLA Ops:
  0.7 1.7 %faces.1 = (bf16[2,32,16,128]{3,2,1,0:T(8,128)(2,1)S(1)}, bf16[2,32,16,128]{3,2,1,0:T(8,128)(2,1)S(1)}, bf16[2,32,16,128]{3,2,1,0:T(8,128)(2,1)S(1)}, bf16[2,32,16,128]{3,2,1,0:T(8,128)(2,1)S(1)}) custom-call(f32[32,16,16,128]{3,2,1,0:T(8,128)} %u_ref.1, f32[32,16,16,128]{3,2,1,0:T(8,128)} %k_ref.1), custom_call_target="tpu_custom_call" | custom-call | flops 524288 | bytes 1048576 | tf_op jit(solution)/shard_map/faces/pallas_call | solution.py:34
  2.4 0.5 collective-permute-start.1
  2.9 4.0 %collective-permute-start = (bf16[2,32,16,128]{3,2,1,0:T(8,128)(2,1)S(1)}, bf16[2,32,16,128]{3,2,1,0:T(8,128)(2,1)S(1)}, u32[]{:S(2)}, u32[]{:S(2)}) collective-permute-start(bf16[2,32,16,128]{3,2,1,0:T(8,128)(2,1)S(1)} %get-tuple-element.96), channel_id=1, source_target_pairs={{0,8},{1,9},{8,0},{9,1},{16,24},{17,25},{24,16},{25,17},{2,10},{3,... | collective-permute-start | bytes 786440 | tf_op jit(solution)/shard_map/ppermute | solution.py:415
  6.9 0.1 collective-permute-start.3
  7.0 3.1 %collective-permute-start.2 = (bf16[2,32,16,128]{3,2,1,0:T(8,128)(2,1)S(1)}, bf16[2,32,16,128]{3,2,1,0:T(8,128)(2,1)S(1)}, u32[]{:S(2)}, u32[]{:S(2)}) collective-permute-start(bf16[2,32,16,128]{3,2,1,0:T(8,128)(2,1)S(1)} %get-tuple-element.92), channel_id=1, source_target_pairs={{0,2},{1,3},{2,0},{3,1},{4,6},{5,7},{6,4},{7,5},{8,10},{9,11},{10,... | collective-permute-start | bytes 786440 | tf_op jit(solution)/shard_map/ppermute | solution.py:415
  10.1 0.1 fusion.4
  10.2 0.1 copy.17
  10.3 0.1 copy.18
  10.4 3.4 %psi.1 = (bf16[16,2,512,128]{3,2,1,0:T(8,128)(2,1)S(1)}, bf16[2,16,64,128]{3,2,1,0:T(8,128)(2,1)S(1)}, bf16[2,16,64,128]{3,2,1,0:T(8,128)(2,1)S(1)}, bf16[2,256,...) custom-call(bf16[64,16,16,128]{3,2,1,0:T(8,128)(2,1)} %psi_hbm.1, bf16[32,16,16,128]{3,2,1,0:T(8,128)(2,1)} %prev_hbm.1, ...), custom_call_target="tpu_custom_call" | custom-call | flops 4194304 | bytes 4194304 | tf_op jit(solution)/shard_map/psi/pallas_call | solution.py:34
  13.8 6.7 %first.1 = (f32[32,16,16,128]{3,2,1,0:T(8,128)S(1)}, f32[32,16,16,128]{3,2,1,0:T(8,128)S(1)}, f32[32,16,16,128]{3,2,1,0:T(8,128)S(1)}, f32[32,16,16,128]{3,2,1,0...) custom-call(f32[32,16,16,128]{3,2,1,0:T(8,128)} %u_ref.1, ...), custom_call_target="tpu_custom_call" | custom-call | flops 37748736 | bytes 16777216 | tf_op jit(solution)/shard_map/first/pallas_call | solution.py:34
  20.6 0.1 bitcast_add_fusion.2
  20.7 0.1 bitcast_add_fusion
  20.8 1.0 %edge.3 = (f32[32,16,16,128]{3,2,1,0:T(8,128)S(1)}, bf16[32,16,128]{2,1,0:T(8,128)(2,1)S(1)}, bf16[32,16,128]{2,1,0:T(8,128)(2,1)S(1)}, bf16[32,16,128]{2,1,0:T(8,128)(2,1)S(1)}, bf16[32,16,128]{2,1,0:T(8,128)(2,1)S(1)}) custom-call(f32[32,16,16,128]{3,2,1,0:T(8,128)S(1)} %get-tuple-element.47.w_in, ...), custom_call_target="tpu_custom_call", output_to_operand_aliasing={{0}: (0, {})} | custom-call | flops 1048576 | bytes 1048576 | tf_op jit(solution)/shard_map/edge/pallas_call | solution.py:34
  21.8 0.1 collective-permute-start.5
  21.9 1.5 %collective-permute-start.4 = (bf16[32,16,128]{2,1,0:T(8,128)(2,1)S(1)}, bf16[32,16,128]{2,1,0:T(8,128)(2,1)S(1)}, u32[]{:S(2)}, u32[]{:S(2)}) collective-permute-start(bf16[32,16,128]{2,1,0:T(8,128)(2,1)S(1)} %get-tuple-element.120), channel_id=1, source_target_pairs={{0,8},{1,9},{8,0},{9,1},{16,24},{17,25},{24,16},{25,17},{2,10},{3,... | collective-permute-start | bytes 393224 | tf_op jit(solution)/shard_map/ppermute | solution.py:415
  23.4 0.1 collective-permute-start.7
  23.5 1.7 %collective-permute-start.6 = (bf16[32,16,128]{2,1,0:T(8,128)(2,1)S(1)}, bf16[32,16,128]{2,1,0:T(8,128)(2,1)S(1)}, u32[]{:S(2)}, u32[]{:S(2)}) collective-permute-start(bf16[32,16,128]{2,1,0:T(8,128)(2,1)S(1)} %get-tuple-element.116), channel_id=1, source_target_pairs={{0,2},{1,3},{2,0},{3,1},{4,6},{5,7},{6,4},{7,5},{8,10},{9,11},{10,... | collective-permute-start | bytes 393224 | tf_op jit(solution)/shard_map/ppermute | solution.py:415
  25.3 3.0 %step.3.w_in = f32[32,16,16,128]{3,2,1,0:T(8,128)S(1)} custom-call(f32[32,16,16,128]{3,2,1,0:T(8,128)S(1)} %get-tuple-element.61.u_ref, f32[32,16,16,128]{3,2,1,0:T(8,128)S(1)} %get-tuple-element.62.cx_ref, f32[32,16,16,128]{3,2,1,0:T(8,128)S(1)} %get-tuple-element.63.cy_ref, f32[32,16,16,128]{3,2,1,0:T(8,128)S(1)} %get-tuple-element.64.cup_ref, ...), custom_call_target="tpu_custom_call" | custom-call | flops 25165824 | bytes 8388608 | tf_op jit(solution)/shard_map/step/pallas_call | solution.py:34
  28.3 0.9 %collective-permute-done.4 = bf16[32,16,128]{2,1,0:T(8,128)(2,1)S(1)} collective-permute-done((bf16[32,16,128]{2,1,0:T(8,128)(2,1)S(1)}, bf16[32,16,128]{2,1,0:T(8,128)(2,1)S(1)}, u32[]{:S(2)}, u32[]{:S(2)}) %collective-permute-start.4) | collective-permute-done | bytes 131104 | tf_op jit(solution)/shard_map/ppermute | solution.py:415
  29.2 0.2 collective-permute-done.6
  29.5 1.0 %edge.4 = (f32[32,16,16,128]{3,2,1,0:T(8,128)S(1)}, bf16[32,16,128]{2,1,0:T(8,128)(2,1)S(1)}, bf16[32,16,128]{2,1,0:T(8,128)(2,1)S(1)}, bf16[32,16,128]{2,1,0:T(8,128)(2,1)S(1)}, bf16[32,16,128]{2,1,0:T(8,128)(2,1)S(1)}) custom-call(f32[32,16,16,128]{3,2,1,0:T(8,128)S(1)} %step.3.w_in, ...), custom_call_target="tpu_custom_call", output_to_operand_aliasing={{0}: (0, {})} | custom-call | flops 1048576 | bytes 1048576 | tf_op jit(solution)/shard_map/edge/pallas_call | solution.py:34
  30.4 0.1 collective-permute-start.9
  30.5 2.0 %collective-permute-start.8 = (bf16[32,16,128]{2,1,0:T(8,128)(2,1)S(1)}, bf16[32,16,128]{2,1,0:T(8,128)(2,1)S(1)}, u32[]{:S(2)}, u32[]{:S(2)}) collective-permute-start(bf16[32,16,128]{2,1,0:T(8,128)(2,1)S(1)} %get-tuple-element.112), channel_id=1, source_target_pairs={{0,8},{1,9},{8,0},{9,1},{16,24},{17,25},{24,16},{25,17},{2,10},{3,... | collective-permute-start | bytes 393224 | tf_op jit(solution)/shard_map/ppermute | solution.py:415
  32.5 0.1 collective-permute-start.11
  32.6 1.4 %collective-permute-start.10 = (bf16[32,16,128]{2,1,0:T(8,128)(2,1)S(1)}, bf16[32,16,128]{2,1,0:T(8,128)(2,1)S(1)}, u32[]{:S(2)}, u32[]{:S(2)}) collective-permute-start(bf16[32,16,128]{2,1,0:T(8,128)(2,1)S(1)} %get-tuple-element.108), channel_id=1, source_target_pairs={{0,2},{1,3},{2,0},{3,1},{4,6},{5,7},{6,4},{7,5},{8,10},{9,11},{10,... | collective-permute-start | bytes 393224 | tf_op jit(solution)/shard_map/ppermute | solution.py:415
  34.0 3.0 %step.4.w_in = f32[32,16,16,128]{3,2,1,0:T(8,128)S(1)} custom-call(f32[32,16,16,128]{3,2,1,0:T(8,128)S(1)} %get-tuple-element.70.u_ref, f32[32,16,16,128]{3,2,1,0:T(8,128)S(1)} %get-tuple-element.62.cx_ref, f32[32,16,16,128]{3,2,1,0:T(8,128)S(1)} %get-tuple-element.63.cy_ref, f32[32,16,16,128]{3,2,1,0:T(8,128)S(1)} %get-tuple-element.64.cup_ref, ...), custom_call_target="tpu_custom_call" | custom-call | flops 25165824 | bytes 8388608 | tf_op jit(solution)/shard_map/step/pallas_call | solution.py:34
  37.0 1.2 %collective-permute-done.8 = bf16[32,16,128]{2,1,0:T(8,128)(2,1)S(1)} collective-permute-done((bf16[32,16,128]{2,1,0:T(8,128)(2,1)S(1)}, bf16[32,16,128]{2,1,0:T(8,128)(2,1)S(1)}, u32[]{:S(2)}, u32[]{:S(2)}) %collective-permute-start.8) | collective-permute-done | bytes 131104 | tf_op jit(solution)/shard_map/ppermute | solution.py:415
  38.2 0.3 collective-permute-done.10
  38.5 1.0 %edge.5 = (f32[32,16,16,128]{3,2,1,0:T(8,128)S(1)}, bf16[32,16,128]{2,1,0:T(8,128)(2,1)S(1)}, bf16[32,16,128]{2,1,0:T(8,128)(2,1)S(1)}, bf16[32,16,128]{2,1,0:T(8,128)(2,1)S(1)}, bf16[32,16,128]{2,1,0:T(8,128)(2,1)S(1)}) custom-call(f32[32,16,16,128]{3,2,1,0:T(8,128)S(1)} %step.4.w_in, ...), custom_call_target="tpu_custom_call", output_to_operand_aliasing={{0}: (0, {})} | custom-call | flops 1048576 | bytes 1048576 | tf_op jit(solution)/shard_map/edge/pallas_call | solution.py:34
  39.5 0.1 collective-permute-start.13
  39.6 1.5 %collective-permute-start.12 = (bf16[32,16,128]{2,1,0:T(8,128)(2,1)S(1)}, bf16[32,16,128]{2,1,0:T(8,128)(2,1)S(1)}, u32[]{:S(2)}, u32[]{:S(2)}) collective-permute-start(bf16[32,16,128]{2,1,0:T(8,128)(2,1)S(1)} %get-tuple-element.104), channel_id=1, source_target_pairs={{0,8},{1,9},{8,0},{9,1},{16,24},{17,25},{24,16},{25,17},{2,10},{3,... | collective-permute-start | bytes 393224 | tf_op jit(solution)/shard_map/ppermute | solution.py:415
  41.1 0.1 collective-permute-start.15
  41.2 2.1 %collective-permute-start.14 = (bf16[32,16,128]{2,1,0:T(8,128)(2,1)S(1)}, bf16[32,16,128]{2,1,0:T(8,128)(2,1)S(1)}, u32[]{:S(2)}, u32[]{:S(2)}) collective-permute-start(bf16[32,16,128]{2,1,0:T(8,128)(2,1)S(1)} %get-tuple-element.100), channel_id=1, source_target_pairs={{0,2},{1,3},{2,0},{3,1},{4,6},{5,7},{6,4},{7,5},{8,10},{9,11},{10,... | collective-permute-start | bytes 393224 | tf_op jit(solution)/shard_map/ppermute | solution.py:415
  43.3 3.1 %step.5 = (f32[32,16,16,128]{3,2,1,0:T(8,128)S(1)}, f32[32,16,16,128]{3,2,1,0:T(8,128)}) custom-call(f32[32,16,16,128]{3,2,1,0:T(8,128)S(1)} %get-tuple-element.75.u_ref.refs_1_, f32[32,16,16,128]{3,2,1,0:T(8,128)S(1)} %get-tuple-element.62.cx_ref, f32[32,16,16,128]{3,2,1,0:T(8,128)S(1)} %get-tuple-element.63.cy_ref, ...), custom_call_target="tpu_custom_call" | custom-call | flops 25165824 | bytes 8388608 | tf_op jit(solution)/shard_map/step/pallas_call | solution.py:34
  46.3 1.6 %corange.1 = (f32[32,64]{1,0:T(8,128)S(1)}, f32[32,16,16,128]{3,2,1,0:T(8,128)}) custom-call(bf16[16,2,512,128]{3,2,1,0:T(8,128)(2,1)S(1)} %get-tuple-element.57.refs_0_.psi_ref, f32[32,16,16,128]{3,2,1,0:T(8,128)S(1)} %get-tuple-element.76.u_ref.refs_0_, f32[32,16,16,128]{3,2,1,0:T(8,128)} %get-tuple-element.81.state_in), custom_call_target="tpu_custom_call", output_to_operand_aliasing={{1}: (2, {})} | custom-call | flops 1073741824 | bytes 4194304 | tf_op jit(solution)/shard_map/corange/pallas_call | solution.py:34
  48.0 0.9 %corange_faces.1.refs_12_ = f32[32,64]{1,0:T(8,128)S(1)} custom-call(f32[32,64]{1,0:T(8,128)S(1)} %get-tuple-element.82.main_ref, bf16[2,16,64,128]{3,2,1,0:T(8,128)(2,1)S(1)} %get-tuple-element.58.refs_1_.px, bf16[2,16,64,128]{3,2,1,0:T(8,128)(2,1)S(1)} %get-tuple-element.59.refs_2_.py, f32[32,16,16,128]{3,2,1,0:T(8,128)S(1)} %get-tuple-element.75.u_ref.refs_1_, ...), custom_call_target="tpu_custom_call" | custom-call | flops 1048576 | bytes 1048576 | tf_op jit(solution)/shard_map/corange_faces/pallas_call | solution.py:34
  48.9 1.1 %finish.1 = (f32[32,16,16,128]{3,2,1,0:T(8,128)S(1)}, bf16[16,2,256,128]{3,2,1,0:T(8,128)(2,1)S(1)}) custom-call(f32[32,16,16,128]{3,2,1,0:T(8,128)S(1)} %get-tuple-element.76.u_ref.refs_0_, f32[32,16,16,128]{3,2,1,0:T(8,128)S(1)} %get-tuple-element.75.u_ref.refs_1_, ...), custom_call_target="tpu_custom_call", output_to_operand_aliasing={{0}: (0, {})} | custom-call | flops 1048576 | bytes 2097152 | tf_op jit(solution)/shard_map/finish/pallas_call | solution.py:34
  50.0 0.1 collective-permute-start.16
  50.0 1.7 %collective-permute-start.19 = (f32[32,64]{1,0:T(8,128)S(1)}, f32[32,64]{1,0:T(8,128)S(1)}, u32[]{:S(2)}, u32[]{:S(2)}) collective-permute-start(f32[32,64]{1,0:T(8,128)S(1)} %corange_faces.1.refs_12_), channel_id=1, source_target_pairs={{0,24},{8,16},{16,8},{24,0},{1,25},{9,17},{17,9},{25,1},{2,26},{10... | collective-permute-start | bytes 24584 | tf_op jit(solution)/shard_map/ppermute | solution.py:429
  51.8 0.4 collective-permute-start.18
  52.2 1.4 %collective-permute-start.17 = (f32[32,64]{1,0:T(8,128)S(1)}, f32[32,64]{1,0:T(8,128)S(1)}, u32[]{:S(2)}, u32[]{:S(2)}) collective-permute-start(f32[32,64]{1,0:T(8,128)S(1)} %corange_faces.1.refs_12_), channel_id=1, source_target_pairs={{0,8},{8,0},{16,24},{24,16},{1,9},{9,1},{17,25},{25,17},{2,10},{10... | collective-permute-start | bytes 24584 | tf_op jit(solution)/shard_map/ppermute | solution.py:429
  53.6 0.6 collective-permute-done.16.other_ref
  54.2 2.1 %range.1 = (bf16[32,16,16,128]{3,2,1,0:T(8,128)(2,1)}, f32[32,16,16,128]{3,2,1,0:T(8,128)}, f32[32,64]{1,0:T(8,128)S(1)}) custom-call(bf16[2,256,256]{2,1,0:T(8,128)(2,1)S(1)} %get-tuple-element.46.refs_3_.refs_11_.weight_ref, bf16[16,2,256,128]{3,2,1,0:T(8,128)(2,1)S(1)} %get-tuple-element.83.own_ref, ...), custom_call_target="tpu_custom_call", output_to_operand_aliasing={{1}: (5, {})} | custom-call | flops 1073741824 | bytes 4194304 | tf_op jit(solution)/shard_map/range/pallas_call | solution.py:34
  56.4 2.3 %collective-permute-start.22 = (f32[32,64]{1,0:T(8,128)S(1)}, f32[32,64]{1,0:T(8,128)S(1)}, u32[]{:S(2)}, u32[]{:S(2)}) collective-permute-start(f32[32,64]{1,0:T(8,128)S(1)} %add_add_fusion), channel_id=1, source_target_pairs={{0,6},{2,4},{4,2},{6,0},{1,7},{3,5},{5,3},{7,1},{8,14},{10,12},{12... | collective-permute-start | bytes 24584 | tf_op jit(solution)/shard_map/ppermute | solution.py:429
  58.7 2.1 %collective-permute-start.20 = (f32[32,64]{1,0:T(8,128)S(1)}, f32[32,64]{1,0:T(8,128)S(1)}, u32[]{:S(2)}, u32[]{:S(2)}) collective-permute-start(f32[32,64]{1,0:T(8,128)S(1)} %add_add_fusion), channel_id=1, source_target_pairs={{0,2},{2,0},{4,6},{6,4},{1,3},{3,1},{5,7},{7,5},{8,10},{10,8},{12,... | collective-permute-start | bytes 24584 | tf_op jit(solution)/shard_map/ppermute | solution.py:429
  60.8 1.1 %collective-permute-done.22 = f32[32,64]{1,0:T(8,128)S(1)} collective-permute-done((f32[32,64]{1,0:T(8,128)S(1)}, f32[32,64]{1,0:T(8,128)S(1)}, u32[]{:S(2)}, u32[]{:S(2)}) %collective-permute-start.22) | collective-permute-done | bytes 8224 | tf_op jit(solution)/shard_map/ppermute | solution.py:429
  62.0 1.4 %collective-permute-done.21 = f32[32,64]{1,0:T(8,128)S(1)} collective-permute-done((f32[32,64]{1,0:T(8,128)S(1)}, f32[32,64]{1,0:T(8,128)S(1)}, u32[]{:S(2)}, u32[]{:S(2)}) %collective-permute-start.21) | collective-permute-done | bytes 8224 | tf_op jit(solution)/shard_map/ppermute | solution.py:429
  63.3 0.6 fusion.3
  (41 shorter events, 0.6 us)
Async XLA Ops:
  0.6 9.5 %copy-start = (bf16[64,64]{1,0:T(8,128)(2,1)S(1)}, bf16[64,64]{1,0:T(8,128)(2,1)}, u32[]{:S(2)}) copy-start(bf16[64,64]{1,0:T(8,128)(2,1)} %param.8) | copy-start | bytes 24580
  2.4 18.1 %collective-permute-start.1 = (bf16[2,32,16,128]{3,2,1,0:T(8,128)(2,1)S(1)}, bf16[2,32,16,128]{3,2,1,0:T(8,128)(2,1)S(1)}, u32[]{:S(2)}, u32[]{:S(2)}) collective-permute-start(bf16[2,32,16,128]{3,2,1,0:T(8,128)(2,1)S(1)} %get-tuple-element.95), channel_id=1, source_target_pairs={{0,1},{1,0},{8,16},{9,17},{16,8},{17,9},{24,25},{25,24},{2,3},{3,2... | collective-permute-start | bytes 786440 | tf_op jit(solution)/shard_map/ppermute | solution.py:415
  2.9 17.6 %collective-permute-start = (bf16[2,32,16,128]{3,2,1,0:T(8,128)(2,1)S(1)}, bf16[2,32,16,128]{3,2,1,0:T(8,128)(2,1)S(1)}, u32[]{:S(2)}, u32[]{:S(2)}) collective-permute-start(bf16[2,32,16,128]{3,2,1,0:T(8,128)(2,1)S(1)} %get-tuple-element.96), channel_id=1, source_target_pairs={{0,8},{1,9},{8,0},{9,1},{16,24},{17,25},{24,16},{25,17},{2,10},{3,... | collective-permute-start | bytes 786440 | tf_op jit(solution)/shard_map/ppermute | solution.py:415
  6.9 13.6 %collective-permute-start.3 = (bf16[2,32,16,128]{3,2,1,0:T(8,128)(2,1)S(1)}, bf16[2,32,16,128]{3,2,1,0:T(8,128)(2,1)S(1)}, u32[]{:S(2)}, u32[]{:S(2)}) collective-permute-start(bf16[2,32,16,128]{3,2,1,0:T(8,128)(2,1)S(1)} %get-tuple-element.91), channel_id=1, source_target_pairs={{0,1},{1,0},{2,4},{3,5},{4,2},{5,3},{6,7},{7,6},{8,9},{9,8},{10,12... | collective-permute-start | bytes 786440 | tf_op jit(solution)/shard_map/ppermute | solution.py:415
  7.0 13.6 %collective-permute-start.2 = (bf16[2,32,16,128]{3,2,1,0:T(8,128)(2,1)S(1)}, bf16[2,32,16,128]{3,2,1,0:T(8,128)(2,1)S(1)}, u32[]{:S(2)}, u32[]{:S(2)}) collective-permute-start(bf16[2,32,16,128]{3,2,1,0:T(8,128)(2,1)S(1)} %get-tuple-element.92), channel_id=1, source_target_pairs={{0,2},{1,3},{2,0},{3,1},{4,6},{5,7},{6,4},{7,5},{8,10},{9,11},{10,... | collective-permute-start | bytes 786440 | tf_op jit(solution)/shard_map/ppermute | solution.py:415
  21.8 6.5 %collective-permute-start.5 = (bf16[32,16,128]{2,1,0:T(8,128)(2,1)S(1)}, bf16[32,16,128]{2,1,0:T(8,128)(2,1)S(1)}, u32[]{:S(2)}, u32[]{:S(2)}) collective-permute-start(bf16[32,16,128]{2,1,0:T(8,128)(2,1)S(1)} %get-tuple-element.119), channel_id=1, source_target_pairs={{0,1},{1,0},{8,16},{9,17},{16,8},{17,9},{24,25},{25,24},{2,3},{3,2... | collective-permute-start | bytes 393224 | tf_op jit(solution)/shard_map/ppermute | solution.py:415
  21.9 7.3 %collective-permute-start.4 = (bf16[32,16,128]{2,1,0:T(8,128)(2,1)S(1)}, bf16[32,16,128]{2,1,0:T(8,128)(2,1)S(1)}, u32[]{:S(2)}, u32[]{:S(2)}) collective-permute-start(bf16[32,16,128]{2,1,0:T(8,128)(2,1)S(1)} %get-tuple-element.120), channel_id=1, source_target_pairs={{0,8},{1,9},{8,0},{9,1},{16,24},{17,25},{24,16},{25,17},{2,10},{3,... | collective-permute-start | bytes 393224 | tf_op jit(solution)/shard_map/ppermute | solution.py:415
  23.4 5.8 %collective-permute-start.7 = (bf16[32,16,128]{2,1,0:T(8,128)(2,1)S(1)}, bf16[32,16,128]{2,1,0:T(8,128)(2,1)S(1)}, u32[]{:S(2)}, u32[]{:S(2)}) collective-permute-start(bf16[32,16,128]{2,1,0:T(8,128)(2,1)S(1)} %get-tuple-element.115), channel_id=1, source_target_pairs={{0,1},{1,0},{2,4},{3,5},{4,2},{5,3},{6,7},{7,6},{8,9},{9,8},{10,12... | collective-permute-start | bytes 393224 | tf_op jit(solution)/shard_map/ppermute | solution.py:415
  23.5 5.9 %collective-permute-start.6 = (bf16[32,16,128]{2,1,0:T(8,128)(2,1)S(1)}, bf16[32,16,128]{2,1,0:T(8,128)(2,1)S(1)}, u32[]{:S(2)}, u32[]{:S(2)}) collective-permute-start(bf16[32,16,128]{2,1,0:T(8,128)(2,1)S(1)} %get-tuple-element.116), channel_id=1, source_target_pairs={{0,2},{1,3},{2,0},{3,1},{4,6},{5,7},{6,4},{7,5},{8,10},{9,11},{10,... | collective-permute-start | bytes 393224 | tf_op jit(solution)/shard_map/ppermute | solution.py:415
  30.4 6.6 %collective-permute-start.9 = (bf16[32,16,128]{2,1,0:T(8,128)(2,1)S(1)}, bf16[32,16,128]{2,1,0:T(8,128)(2,1)S(1)}, u32[]{:S(2)}, u32[]{:S(2)}) collective-permute-start(bf16[32,16,128]{2,1,0:T(8,128)(2,1)S(1)} %get-tuple-element.111), channel_id=1, source_target_pairs={{0,1},{1,0},{8,16},{9,17},{16,8},{17,9},{24,25},{25,24},{2,3},{3,2... | collective-permute-start | bytes 393224 | tf_op jit(solution)/shard_map/ppermute | solution.py:415
  30.5 7.7 %collective-permute-start.8 = (bf16[32,16,128]{2,1,0:T(8,128)(2,1)S(1)}, bf16[32,16,128]{2,1,0:T(8,128)(2,1)S(1)}, u32[]{:S(2)}, u32[]{:S(2)}) collective-permute-start(bf16[32,16,128]{2,1,0:T(8,128)(2,1)S(1)} %get-tuple-element.112), channel_id=1, source_target_pairs={{0,8},{1,9},{8,0},{9,1},{16,24},{17,25},{24,16},{25,17},{2,10},{3,... | collective-permute-start | bytes 393224 | tf_op jit(solution)/shard_map/ppermute | solution.py:415
  32.5 5.7 %collective-permute-start.11 = (bf16[32,16,128]{2,1,0:T(8,128)(2,1)S(1)}, bf16[32,16,128]{2,1,0:T(8,128)(2,1)S(1)}, u32[]{:S(2)}, u32[]{:S(2)}) collective-permute-start(bf16[32,16,128]{2,1,0:T(8,128)(2,1)S(1)} %get-tuple-element.107), channel_id=1, source_target_pairs={{0,1},{1,0},{2,4},{3,5},{4,2},{5,3},{6,7},{7,6},{8,9},{9,8},{10,12... | collective-permute-start | bytes 393224 | tf_op jit(solution)/shard_map/ppermute | solution.py:415
  32.6 5.9 %collective-permute-start.10 = (bf16[32,16,128]{2,1,0:T(8,128)(2,1)S(1)}, bf16[32,16,128]{2,1,0:T(8,128)(2,1)S(1)}, u32[]{:S(2)}, u32[]{:S(2)}) collective-permute-start(bf16[32,16,128]{2,1,0:T(8,128)(2,1)S(1)} %get-tuple-element.108), channel_id=1, source_target_pairs={{0,2},{1,3},{2,0},{3,1},{4,6},{5,7},{6,4},{7,5},{8,10},{9,11},{10,... | collective-permute-start | bytes 393224 | tf_op jit(solution)/shard_map/ppermute | solution.py:415
  39.5 8.4 %collective-permute-start.13 = (bf16[32,16,128]{2,1,0:T(8,128)(2,1)S(1)}, bf16[32,16,128]{2,1,0:T(8,128)(2,1)S(1)}, u32[]{:S(2)}, u32[]{:S(2)}) collective-permute-start(bf16[32,16,128]{2,1,0:T(8,128)(2,1)S(1)} %get-tuple-element.103), channel_id=1, source_target_pairs={{0,1},{1,0},{8,16},{9,17},{16,8},{17,9},{24,25},{25,24},{2,3},{3,2... | collective-permute-start | bytes 393224 | tf_op jit(solution)/shard_map/ppermute | solution.py:415
  39.6 8.3 %collective-permute-start.12 = (bf16[32,16,128]{2,1,0:T(8,128)(2,1)S(1)}, bf16[32,16,128]{2,1,0:T(8,128)(2,1)S(1)}, u32[]{:S(2)}, u32[]{:S(2)}) collective-permute-start(bf16[32,16,128]{2,1,0:T(8,128)(2,1)S(1)} %get-tuple-element.104), channel_id=1, source_target_pairs={{0,8},{1,9},{8,0},{9,1},{16,24},{17,25},{24,16},{25,17},{2,10},{3,... | collective-permute-start | bytes 393224 | tf_op jit(solution)/shard_map/ppermute | solution.py:415
  41.1 6.9 %collective-permute-start.15 = (bf16[32,16,128]{2,1,0:T(8,128)(2,1)S(1)}, bf16[32,16,128]{2,1,0:T(8,128)(2,1)S(1)}, u32[]{:S(2)}, u32[]{:S(2)}) collective-permute-start(bf16[32,16,128]{2,1,0:T(8,128)(2,1)S(1)} %get-tuple-element.99), channel_id=1, source_target_pairs={{0,1},{1,0},{2,4},{3,5},{4,2},{5,3},{6,7},{7,6},{8,9},{9,8},{10,12... | collective-permute-start | bytes 393224 | tf_op jit(solution)/shard_map/ppermute | solution.py:415
  41.2 6.8 %collective-permute-start.14 = (bf16[32,16,128]{2,1,0:T(8,128)(2,1)S(1)}, bf16[32,16,128]{2,1,0:T(8,128)(2,1)S(1)}, u32[]{:S(2)}, u32[]{:S(2)}) collective-permute-start(bf16[32,16,128]{2,1,0:T(8,128)(2,1)S(1)} %get-tuple-element.100), channel_id=1, source_target_pairs={{0,2},{1,3},{2,0},{3,1},{4,6},{5,7},{6,4},{7,5},{8,10},{9,11},{10,... | collective-permute-start | bytes 393224 | tf_op jit(solution)/shard_map/ppermute | solution.py:415
  50.0 4.2 %collective-permute-start.16 = (bf16[16,2,256,128]{3,2,1,0:T(8,128)(2,1)S(1)}, bf16[16,2,256,128]{3,2,1,0:T(8,128)(2,1)S(1)}, u32[]{:S(2)}, u32[]{:S(2)}) collective-permute-start(bf16[16,2,256,128]{3,2,1,0:T(8,128)(2,1)S(1)} %get-tuple-element.83.own_ref), channel_id=1, source_target_pairs={{0,1},{1,0},{2,3},{3,2},{4,5},{5,4},{6,7},{7,6},{8,9},{9,8},{10,11... | collective-permute-start | bytes 6291464 | tf_op jit(solution)/shard_map/ppermute | solution.py:554
  50.0 6.3 %collective-permute-start.19 = (f32[32,64]{1,0:T(8,128)S(1)}, f32[32,64]{1,0:T(8,128)S(1)}, u32[]{:S(2)}, u32[]{:S(2)}) collective-permute-start(f32[32,64]{1,0:T(8,128)S(1)} %corange_faces.1.refs_12_), channel_id=1, source_target_pairs={{0,24},{8,16},{16,8},{24,0},{1,25},{9,17},{17,9},{25,1},{2,26},{10... | collective-permute-start | bytes 24584 | tf_op jit(solution)/shard_map/ppermute | solution.py:429
  51.8 4.6 %collective-permute-start.18 = (f32[32,64]{1,0:T(8,128)S(1)}, f32[32,64]{1,0:T(8,128)S(1)}, u32[]{:S(2)}, u32[]{:S(2)}) collective-permute-start(f32[32,64]{1,0:T(8,128)S(1)} %corange_faces.1.refs_12_), channel_id=1, source_target_pairs={{0,16},{8,24},{16,0},{24,8},{1,17},{9,25},{17,1},{25,9},{2,18},{10... | collective-permute-start | bytes 24584 | tf_op jit(solution)/shard_map/ppermute | solution.py:429
  52.2 4.2 %collective-permute-start.17 = (f32[32,64]{1,0:T(8,128)S(1)}, f32[32,64]{1,0:T(8,128)S(1)}, u32[]{:S(2)}, u32[]{:S(2)}) collective-permute-start(f32[32,64]{1,0:T(8,128)S(1)} %corange_faces.1.refs_12_), channel_id=1, source_target_pairs={{0,8},{8,0},{16,24},{24,16},{1,9},{9,1},{17,25},{25,17},{2,10},{10... | collective-permute-start | bytes 24584 | tf_op jit(solution)/shard_map/ppermute | solution.py:429
  54.2 9.2 %copy-start.1 = (f32[64,32]{0,1:T(8,128)S(1)}, f32[64,32]{0,1:T(8,128)}, u32[]{:S(2)}) copy-start(f32[64,32]{0,1:T(8,128)} %param.11) | copy-start | bytes 24580
  56.4 5.6 %collective-permute-start.22 = (f32[32,64]{1,0:T(8,128)S(1)}, f32[32,64]{1,0:T(8,128)S(1)}, u32[]{:S(2)}, u32[]{:S(2)}) collective-permute-start(f32[32,64]{1,0:T(8,128)S(1)} %add_add_fusion), channel_id=1, source_target_pairs={{0,6},{2,4},{4,2},{6,0},{1,7},{3,5},{5,3},{7,1},{8,14},{10,12},{12... | collective-permute-start | bytes 24584 | tf_op jit(solution)/shard_map/ppermute | solution.py:429
  58.7 4.6 %collective-permute-start.21 = (f32[32,64]{1,0:T(8,128)S(1)}, f32[32,64]{1,0:T(8,128)S(1)}, u32[]{:S(2)}, u32[]{:S(2)}) collective-permute-start(f32[32,64]{1,0:T(8,128)S(1)} %add_add_fusion), channel_id=1, source_target_pairs={{0,4},{2,6},{4,0},{6,2},{1,5},{3,7},{5,1},{7,3},{8,12},{10,14},{12... | collective-permute-start | bytes 24584 | tf_op jit(solution)/shard_map/ppermute | solution.py:429
  58.7 4.6 %collective-permute-start.20 = (f32[32,64]{1,0:T(8,128)S(1)}, f32[32,64]{1,0:T(8,128)S(1)}, u32[]{:S(2)}, u32[]{:S(2)}) collective-permute-start(f32[32,64]{1,0:T(8,128)S(1)} %add_add_fusion), channel_id=1, source_target_pairs={{0,2},{2,0},{4,6},{6,4},{1,3},{3,1},{5,7},{7,5},{8,10},{10,8},{12,... | collective-permute-start | bytes 24584 | tf_op jit(solution)/shard_map/ppermute | solution.py:429

commit v4 on v3

--- a/solution.py
+++ b/solution.py
@@ -13,6 +13,7 @@
 HALF = 0.16 * 0.5
 BLOCK = 8
 ROWS = 8
+SUM_COST = 20 << 20
 
 
 def vmem_call(
@@ -240,41 +241,51 @@
     return jnp.where(row == col, full, 0.0).astype(BF)
 
 
-def psi_kernel(psi_hbm, prev_hbm, omega_ref, out_ref, x_ref, y_ref, weight_ref, prev_ref, buf, wide, sem):
+def lines_kernel(psi_hbm, prev_hbm, omega_ref, after, x_ref, weight_ref, prev_ref, xbuf, wide, sem):
+    del after
+    ranks, nx, ny, nz = psi_hbm.shape
+    rows = wide.reshape(ranks * ny, nz)
+    copies = []
+    for end in range(2):
+        copies.append(
+            pltpu.make_async_copy(psi_hbm.at[:, end * (nx - 1)], xbuf.at[end], sem.at[end])
+        )
+    copies.append(pltpu.make_async_copy(prev_hbm, prev_ref, sem.at[2]))
+    for copy in copies:
+        copy.start()
+    for i in range(omega_ref.shape[0]):
+        weight_ref[i] = spread(omega_ref[i])
+    for end in range(2):
+        copies[end].wait()
+        wide[...] = xbuf[end].astype(F32)
+        for y in range(ny):
+            x_ref[end, y] = rows[pl.ds(y, ranks, stride=ny), :].astype(BF)
+    copies[2].wait()
+
+
+def psi_kernel(psi_hbm, out_ref, y_ref, buf, wide, sem):
     ranks, nx, ny, nz = psi_hbm.shape
     parts = 4
     rows = wide.reshape(ranks * ny, nz)
 
-    def line(y):
-        return rows[pl.ds(y, ranks, stride=ny), :].astype(BF)
-
     def copy_of(i):
         part = pl.ds(i * (nx // parts), nx // parts)
         return pltpu.make_async_copy(psi_hbm.at[:, part], buf.at[:, part], sem.at[i])
 
     for i in range(parts):
         copy_of(i).start()
-    prev_copy = pltpu.make_async_copy(prev_hbm, prev_ref, sem.at[parts])
-    prev_copy.start()
-    for i in range(omega_ref.shape[0]):
-        weight_ref[i] = spread(omega_ref[i])
 
     def body(x, carry):
         value = buf[:, x].astype(F32)
         split_into(out_ref, x, value)
         wide[...] = value
-        y_ref[0, x] = line(0)
-        y_ref[1, x] = line(ny - 1)
+        for end in range(2):
+            y_ref[end, x] = rows[pl.ds(end * (ny - 1), ranks, stride=ny), :].astype(BF)
         return carry
 
     for i in range(parts):
         copy_of(i).wait()
         lax.fori_loop(i * (nx // parts), (i + 1) * (nx // parts), body, 0)
-    for end in range(2):
-        wide[...] = buf[:, end * (nx - 1)].astype(F32)
-        for y in range(ny):
-            x_ref[end, y] = line(y)
-    prev_copy.wait()
 
 
 def side_by_side(ref, x):
@@ -384,6 +395,13 @@
     lax.fori_loop(0, nx, body, 0)
 
 
+def sum_kernel(*refs):
+    total = refs[0][...]
+    for ref in refs[1:-1]:
+        total = total + ref[...]
+    refs[-1][...] = total
+
+
 def swap_pairs(count, parity, par):
     partner = {}
     for i in range(parity, count - 1, 2):
@@ -473,28 +491,21 @@
     omega_blocks = jnp.stack(
         [lax.dynamic_slice_in_dim(own_cols, p * samples, samples, 1) for p in (par, source)]
     )
-    held_psi, psi_x, psi_y, weights, prev = vmem_call(
+    held_psi, psi_y = vmem_call(
         psi_kernel,
-        [
-            (split_shape(psi.shape), BF),
-            ((2, ny, ranks, nz), BF),
-            ((2, nx, ranks, nz), BF),
-            ((2, own_ranks * ROWS, samples * ROWS), BF),
-            (range_prev.shape, BF),
-        ],
+        [(split_shape(psi.shape), BF), ((2, nx, ranks, nz), BF)],
         "psi",
-        limit=7 << 20,
+        limit=6 << 20,
         scratch=[
             pltpu.VMEM(psi.shape, BF),
             pltpu.VMEM((ranks, ny, nz), F32),
-            pltpu.SemaphoreType.DMA((5,)),
+            pltpu.SemaphoreType.DMA((4,)),
         ],
-        hbm_in=(0, 1),
+        hbm_in=(0,),
         flops=4 * cells,
         nbytes=4 * cells,
-    )(psi, range_prev, omega_blocks)
-    kept = (held_psi, psi_x, psi_y, weights, prev)
-
+    )(psi)
+    kept = (held_psi, psi_y)
     for step in range(STEPS):
         if step > 0:
             halos = exchange(edges)
@@ -508,6 +519,26 @@
                 flops=24 * cells,
                 nbytes=8 * cells,
             )(state, *coefs, *kept)
+        if step == 2:
+            psi_x, weights, prev = vmem_call(
+                lines_kernel,
+                [
+                    ((2, ny, ranks, nz), BF),
+                    ((2, own_ranks * ROWS, samples * ROWS), BF),
+                    (range_prev.shape, BF),
+                ],
+                "lines",
+                limit=4 << 20,
+                scratch=[
+                    pltpu.VMEM((2, ranks, ny, nz), BF),
+                    pltpu.VMEM((ranks, ny, nz), F32),
+                    pltpu.SemaphoreType.DMA((3,)),
+                ],
+                hbm_in=(0, 1),
+                flops=cells,
+                nbytes=cells,
+            )(psi, range_prev, omega_blocks, moved)
+            kept += (psi_x, weights, prev)
         if step < STEPS - 1:
             state, *edges = vmem_call(
                 functools.partial(edge_kernel, True),
@@ -564,8 +595,10 @@
         flops=2 * ranks * ROWS * cells,
         nbytes=4 * cells,
     )(weights, snapshot, other, prev, final, written)
-    line_sum = sum(first_sums, partial_sum) + done
-    corange = sum(received(line_sum, "sy"), corange_prev.T + line_sum)
+    line_sum = vmem_call(
+        sum_kernel, [((samples, ranks), F32)], "line_sum", flops=SUM_COST, nbytes=SUM_COST
+    )(partial_sum, *first_sums)[0]
+    corange = sum(received(line_sum, "sy"), corange_prev.T + line_sum) + done
     return final_state, range_sketch, corange.T
 
 

time: 64.1 us -> 63.2 us (0.986)
  waiting for transfers between devices: 5.68 us -> 3.56 us
  Pallas kernels: 29.3 us -> 30.8 us
    pallas_call x13 -> x15, Pallas kernels: 29.3 us -> 30.8 us  [call(): pl.pallas_call(kernel, out_shape=out_shape, in_specs=in_specs, out_specs=...]
    ppermute x16, waiting for transfers between devices: 2.58 us -> 1.2 us  [exchange(): got[axis, parity] = lax.ppermute(mine, (axis, 'par'), pairs)]
  transfers between devices with their start and end apart: 23 -> 23, of which waited for: 7 -> 6; matrix products, arithmetic and copies ran while one was open for 1% -> 1% of each run, Pallas kernels for 36% -> 39%
where the time goes in v4:
time: 63.2 us; the launch traced here: 63 us
  Pallas kernels  30.8 us (49%)
  starting transfers between devices  26.1 us (41%)
  waiting for transfers between devices  3.56 us (6%)
  other arithmetic  1.23 us (2%)
  between operations  1.08 us (2%)
    pallas_call x15, Pallas kernels, call(): pl.pallas_call(kernel, out_shape=out_shape, in_specs=in_specs, out_specs=...  30.8 us
    ppermute x16, starting transfers between devices, exchange(): got[axis, parity] = lax.ppermute(mine, (axis, 'par'), pairs)  18 us
    ppermute x6, starting transfers between devices, received(): lax.ppermute(value, axis, [(i, i ^ shift) for i in range(count)])  8 us
    ppermute x6, waiting for transfers between devices, received(): lax.ppermute(value, axis, [(i, i ^ shift) for i in range(count)])  2.37 us
  transfers between devices with their start and end apart: 23, of which 6 were waited for; matrix products, arithmetic and copies ran while one was open for 1% of the time, Pallas kernels for 39%

profile of v4, /device:TPU:0, one launch (start us, length us, event | category | flops | bytes accessed | tf_op | source)
XLA Modules:
  0.0 63.0 jit_solution(3089377182406860082)
XLA Ops:
  0.7 1.7 %faces.1 = (bf16[2,32,16,128]{3,2,1,0:T(8,128)(2,1)S(1)}, bf16[2,32,16,128]{3,2,1,0:T(8,128)(2,1)S(1)}, bf16[2,32,16,128]{3,2,1,0:T(8,128)(2,1)S(1)}, bf16[2,32,16,128]{3,2,1,0:T(8,128)(2,1)S(1)}) custom-call(f32[32,16,16,128]{3,2,1,0:T(8,128)} %u_ref.1, f32[32,16,16,128]{3,2,1,0:T(8,128)} %k_ref.1), custom_call_target="tpu_custom_call" | custom-call | flops 524288 | bytes 1048576 | tf_op jit(solution)/shard_map/faces/pallas_call | solution.py:35
  2.4 0.5 collective-permute-start.1
  2.9 4.0 %collective-permute-start = (bf16[2,32,16,128]{3,2,1,0:T(8,128)(2,1)S(1)}, bf16[2,32,16,128]{3,2,1,0:T(8,128)(2,1)S(1)}, u32[]{:S(2)}, u32[]{:S(2)}) collective-permute-start(bf16[2,32,16,128]{3,2,1,0:T(8,128)(2,1)S(1)} %get-tuple-element.96), channel_id=1, source_target_pairs={{0,8},{1,9},{8,0},{9,1},{16,24},{17,25},{24,16},{25,17},{2,10},{3,... | collective-permute-start | bytes 786440 | tf_op jit(solution)/shard_map/ppermute | solution.py:433
  6.9 0.1 collective-permute-start.3
  7.0 3.1 %collective-permute-start.2 = (bf16[2,32,16,128]{3,2,1,0:T(8,128)(2,1)S(1)}, bf16[2,32,16,128]{3,2,1,0:T(8,128)(2,1)S(1)}, u32[]{:S(2)}, u32[]{:S(2)}) collective-permute-start(bf16[2,32,16,128]{3,2,1,0:T(8,128)(2,1)S(1)} %get-tuple-element.92), channel_id=1, source_target_pairs={{0,2},{1,3},{2,0},{3,1},{4,6},{5,7},{6,4},{7,5},{8,10},{9,11},{10,... | collective-permute-start | bytes 786440 | tf_op jit(solution)/shard_map/ppermute | solution.py:433
  10.1 0.1 fusion.5
  10.2 0.1 copy.17
  10.3 0.1 copy.18
  10.4 3.0 %psi.1 = (bf16[16,2,512,128]{3,2,1,0:T(8,128)(2,1)S(1)}, bf16[2,16,64,128]{3,2,1,0:T(8,128)(2,1)S(1)}) custom-call(bf16[64,16,16,128]{3,2,1,0:T(8,128)(2,1)} %psi_hbm.3), custom_call_target="tpu_custom_call" | custom-call | flops 4194304 | bytes 4194304 | tf_op jit(solution)/shard_map/psi/pallas_call | solution.py:35
  13.4 6.7 %first.1 = (f32[32,16,16,128]{3,2,1,0:T(8,128)S(1)}, f32[32,16,16,128]{3,2,1,0:T(8,128)S(1)}, f32[32,16,16,128]{3,2,1,0:T(8,128)S(1)}, f32[32,16,16,128]{3,2,1,0...) custom-call(f32[32,16,16,128]{3,2,1,0:T(8,128)} %u_ref.1, ...), custom_call_target="tpu_custom_call" | custom-call | flops 37748736 | bytes 16777216 | tf_op jit(solution)/shard_map/first/pallas_call | solution.py:35
  20.3 0.1 bitcast_add_fusion.2
  20.4 1.0 %edge.3 = (f32[32,16,16,128]{3,2,1,0:T(8,128)S(1)}, bf16[32,16,128]{2,1,0:T(8,128)(2,1)S(1)}, bf16[32,16,128]{2,1,0:T(8,128)(2,1)S(1)}, bf16[32,16,128]{2,1,0:T(8,128)(2,1)S(1)}, bf16[32,16,128]{2,1,0:T(8,128)(2,1)S(1)}) custom-call(f32[32,16,16,128]{3,2,1,0:T(8,128)S(1)} %get-tuple-element.46.w_in, ...), custom_call_target="tpu_custom_call", output_to_operand_aliasing={{0}: (0, {})} | custom-call | flops 1048576 | bytes 1048576 | tf_op jit(solution)/shard_map/edge/pallas_call | solution.py:35
  21.4 0.1 collective-permute-start.5
  21.5 1.6 %collective-permute-start.4 = (bf16[32,16,128]{2,1,0:T(8,128)(2,1)S(1)}, bf16[32,16,128]{2,1,0:T(8,128)(2,1)S(1)}, u32[]{:S(2)}, u32[]{:S(2)}) collective-permute-start(bf16[32,16,128]{2,1,0:T(8,128)(2,1)S(1)} %get-tuple-element.120), channel_id=1, source_target_pairs={{0,8},{1,9},{8,0},{9,1},{16,24},{17,25},{24,16},{25,17},{2,10},{3,... | collective-permute-start | bytes 393224 | tf_op jit(solution)/shard_map/ppermute | solution.py:433
  23.1 0.1 collective-permute-start.7
  23.2 1.7 %collective-permute-start.6 = (bf16[32,16,128]{2,1,0:T(8,128)(2,1)S(1)}, bf16[32,16,128]{2,1,0:T(8,128)(2,1)S(1)}, u32[]{:S(2)}, u32[]{:S(2)}) collective-permute-start(bf16[32,16,128]{2,1,0:T(8,128)(2,1)S(1)} %get-tuple-element.116), channel_id=1, source_target_pairs={{0,2},{1,3},{2,0},{3,1},{4,6},{5,7},{6,4},{7,5},{8,10},{9,11},{10,... | collective-permute-start | bytes 393224 | tf_op jit(solution)/shard_map/ppermute | solution.py:433
  24.9 3.0 %step.3.w_in = f32[32,16,16,128]{3,2,1,0:T(8,128)S(1)} custom-call(f32[32,16,16,128]{3,2,1,0:T(8,128)S(1)} %get-tuple-element.58.u_ref, f32[32,16,16,128]{3,2,1,0:T(8,128)S(1)} %get-tuple-element.59.cx_ref, f32[32,16,16,128]{3,2,1,0:T(8,128)S(1)} %get-tuple-element.60.cy_ref, f32[32,16,16,128]{3,2,1,0:T(8,128)S(1)} %get-tuple-element.61.cup_ref, ...), custom_call_target="tpu_custom_call" | custom-call | flops 25165824 | bytes 8388608 | tf_op jit(solution)/shard_map/step/pallas_call | solution.py:35
  28.0 0.9 %collective-permute-done.4 = bf16[32,16,128]{2,1,0:T(8,128)(2,1)S(1)} collective-permute-done((bf16[32,16,128]{2,1,0:T(8,128)(2,1)S(1)}, bf16[32,16,128]{2,1,0:T(8,128)(2,1)S(1)}, u32[]{:S(2)}, u32[]{:S(2)}) %collective-permute-start.4) | collective-permute-done | bytes 131104 | tf_op jit(solution)/shard_map/ppermute | solution.py:433
  28.9 0.2 collective-permute-done.6
  29.1 1.0 %edge.4 = (f32[32,16,16,128]{3,2,1,0:T(8,128)S(1)}, bf16[32,16,128]{2,1,0:T(8,128)(2,1)S(1)}, bf16[32,16,128]{2,1,0:T(8,128)(2,1)S(1)}, bf16[32,16,128]{2,1,0:T(8,128)(2,1)S(1)}, bf16[32,16,128]{2,1,0:T(8,128)(2,1)S(1)}) custom-call(f32[32,16,16,128]{3,2,1,0:T(8,128)S(1)} %step.3.w_in, ...), custom_call_target="tpu_custom_call", output_to_operand_aliasing={{0}: (0, {})} | custom-call | flops 1048576 | bytes 1048576 | tf_op jit(solution)/shard_map/edge/pallas_call | solution.py:35
  30.1 0.1 collective-permute-start.9
  30.2 1.9 %collective-permute-start.8 = (bf16[32,16,128]{2,1,0:T(8,128)(2,1)S(1)}, bf16[32,16,128]{2,1,0:T(8,128)(2,1)S(1)}, u32[]{:S(2)}, u32[]{:S(2)}) collective-permute-start(bf16[32,16,128]{2,1,0:T(8,128)(2,1)S(1)} %get-tuple-element.112), channel_id=1, source_target_pairs={{0,8},{1,9},{8,0},{9,1},{16,24},{17,25},{24,16},{25,17},{2,10},{3,... | collective-permute-start | bytes 393224 | tf_op jit(solution)/shard_map/ppermute | solution.py:433
  32.2 0.1 collective-permute-start.11
  32.2 1.4 %collective-permute-start.10 = (bf16[32,16,128]{2,1,0:T(8,128)(2,1)S(1)}, bf16[32,16,128]{2,1,0:T(8,128)(2,1)S(1)}, u32[]{:S(2)}, u32[]{:S(2)}) collective-permute-start(bf16[32,16,128]{2,1,0:T(8,128)(2,1)S(1)} %get-tuple-element.108), channel_id=1, source_target_pairs={{0,2},{1,3},{2,0},{3,1},{4,6},{5,7},{6,4},{7,5},{8,10},{9,11},{10,... | collective-permute-start | bytes 393224 | tf_op jit(solution)/shard_map/ppermute | solution.py:433
  33.6 3.0 %step.4.after.w_in = f32[32,16,16,128]{3,2,1,0:T(8,128)S(1)} custom-call(f32[32,16,16,128]{3,2,1,0:T(8,128)S(1)} %get-tuple-element.67.u_ref, f32[32,16,16,128]{3,2,1,0:T(8,128)S(1)} %get-tuple-element.59.cx_ref, f32[32,16,16,128]{3,2,1,0:T(8,128)S(1)} %get-tuple-element.60.cy_ref, f32[32,16,16,128]{3,2,1,0:T(8,128)S(1)} %get-tuple-element.61.cup_ref, ...), custom_call_target="tpu_custom_call" | custom-call | flops 25165824 | bytes 8388608 | tf_op jit(solution)/shard_map/step/pallas_call | solution.py:35
  36.7 1.8 %lines.1 = (bf16[2,16,64,128]{3,2,1,0:T(8,128)(2,1)S(1)}, bf16[2,256,256]{2,1,0:T(8,128)(2,1)S(1)}, bf16[32,16,16,128]{3,2,1,0:T(8,128)(2,1)S(1)}) custom-call(bf16[64,16,16,128]{3,2,1,0:T(8,128)(2,1)} %psi_hbm.3, bf16[32,16,16,128]{3,2,1,0:T(8,128)(2,1)} %prev_hbm.1, bf16[2,32,32]{2,1,0:T(8,128)(2,1)S(1)} %pad_maximum_fusion.omega_ref, ...), custom_call_target="tpu_custom_call" | custom-call | flops 1048576 | bytes 1048576 | tf_op jit(solution)/shard_map/lines/pallas_call | solution.py:35
  38.6 1.0 %edge.5 = (f32[32,16,16,128]{3,2,1,0:T(8,128)S(1)}, bf16[32,16,128]{2,1,0:T(8,128)(2,1)S(1)}, bf16[32,16,128]{2,1,0:T(8,128)(2,1)S(1)}, bf16[32,16,128]{2,1,0:T(8,128)(2,1)S(1)}, bf16[32,16,128]{2,1,0:T(8,128)(2,1)S(1)}) custom-call(f32[32,16,16,128]{3,2,1,0:T(8,128)S(1)} %step.4.after.w_in, ...), custom_call_target="tpu_custom_call", output_to_operand_aliasing={{0}: (0, {})} | custom-call | flops 1048576 | bytes 1048576 | tf_op jit(solution)/shard_map/edge/pallas_call | solution.py:35
  39.6 0.1 collective-permute-start.13
  39.7 2.2 %collective-permute-start.12 = (bf16[32,16,128]{2,1,0:T(8,128)(2,1)S(1)}, bf16[32,16,128]{2,1,0:T(8,128)(2,1)S(1)}, u32[]{:S(2)}, u32[]{:S(2)}) collective-permute-start(bf16[32,16,128]{2,1,0:T(8,128)(2,1)S(1)} %get-tuple-element.104), channel_id=1, source_target_pairs={{0,8},{1,9},{8,0},{9,1},{16,24},{17,25},{24,16},{25,17},{2,10},{3,... | collective-permute-start | bytes 393224 | tf_op jit(solution)/shard_map/ppermute | solution.py:433
  41.8 0.1 collective-permute-start.15
  41.9 1.1 %collective-permute-start.14 = (bf16[32,16,128]{2,1,0:T(8,128)(2,1)S(1)}, bf16[32,16,128]{2,1,0:T(8,128)(2,1)S(1)}, u32[]{:S(2)}, u32[]{:S(2)}) collective-permute-start(bf16[32,16,128]{2,1,0:T(8,128)(2,1)S(1)} %get-tuple-element.100), channel_id=1, source_target_pairs={{0,2},{1,3},{2,0},{3,1},{4,6},{5,7},{6,4},{7,5},{8,10},{9,11},{10,... | collective-permute-start | bytes 393224 | tf_op jit(solution)/shard_map/ppermute | solution.py:433
  43.0 3.1 %step.5 = (f32[32,16,16,128]{3,2,1,0:T(8,128)S(1)}, f32[32,16,16,128]{3,2,1,0:T(8,128)}) custom-call(f32[32,16,16,128]{3,2,1,0:T(8,128)S(1)} %get-tuple-element.75.u_ref.refs_1_, f32[32,16,16,128]{3,2,1,0:T(8,128)S(1)} %get-tuple-element.59.cx_ref, f32[32,16,16,128]{3,2,1,0:T(8,128)S(1)} %get-tuple-element.60.cy_ref, ...), custom_call_target="tpu_custom_call" | custom-call | flops 25165824 | bytes 8388608 | tf_op jit(solution)/shard_map/step/pallas_call | solution.py:35
  46.1 1.6 %corange.1 = (f32[32,64]{1,0:T(8,128)S(1)}, f32[32,16,16,128]{3,2,1,0:T(8,128)}) custom-call(bf16[16,2,512,128]{3,2,1,0:T(8,128)(2,1)S(1)} %get-tuple-element.56.refs_0_.psi_ref, f32[32,16,16,128]{3,2,1,0:T(8,128)S(1)} %get-tuple-element.76.u_ref.refs_0_, f32[32,16,16,128]{3,2,1,0:T(8,128)} %get-tuple-element.81.state_in), custom_call_target="tpu_custom_call", output_to_operand_aliasing={{1}: (2, {})} | custom-call | flops 1073741824 | bytes 4194304 | tf_op jit(solution)/shard_map/corange/pallas_call | solution.py:35
  47.8 0.1 collective-permute-done.14
  47.9 0.9 %corange_faces.1.refs_12_.refs_0_ = f32[32,64]{1,0:T(8,128)S(1)} custom-call(f32[32,64]{1,0:T(8,128)S(1)} %get-tuple-element.82.main_ref, bf16[2,16,64,128]{3,2,1,0:T(8,128)(2,1)S(1)} %get-tuple-element.73.refs_2_.px, bf16[2,16,64,128]{3,2,1,0:T(8,128)(2,1)S(1)} %get-tuple-element.57.refs_1_.py, f32[32,16,16,128]{3,2,1,0:T(8,128)S(1)} %get-tuple-element.75.u_ref.refs_1_, ...), custom_call_target="tpu_custom_call" | custom-call | flops 1048576 | bytes 1048576 | tf_op jit(solution)/shard_map/corange_faces/pallas_call | solution.py:35
  48.7 1.1 %finish.1 = (f32[32,16,16,128]{3,2,1,0:T(8,128)S(1)}, bf16[16,2,256,128]{3,2,1,0:T(8,128)(2,1)S(1)}) custom-call(f32[32,16,16,128]{3,2,1,0:T(8,128)S(1)} %get-tuple-element.76.u_ref.refs_0_, f32[32,16,16,128]{3,2,1,0:T(8,128)S(1)} %get-tuple-element.75.u_ref.refs_1_, ...), custom_call_target="tpu_custom_call", output_to_operand_aliasing={{0}: (0, {})} | custom-call | flops 1048576 | bytes 2097152 | tf_op jit(solution)/shard_map/finish/pallas_call | solution.py:35
  49.8 0.1 collective-permute-start.16
  49.9 1.6 %collective-permute-start.19 = (f32[32,64]{1,0:T(8,128)S(1)}, f32[32,64]{1,0:T(8,128)S(1)}, u32[]{:S(2)}, u32[]{:S(2)}) collective-permute-start(f32[32,64]{1,0:T(8,128)S(1)} %corange_faces.1.refs_12_.refs_0_), channel_id=1, source_target_pairs={{0,24},{8,16},{16,8},{24,0},{1,25},{9,17},{17,9},{25,1},{2,26},{10... | collective-permute-start | bytes 24584 | tf_op jit(solution)/shard_map/ppermute | solution.py:447
  51.5 0.6 collective-permute-start.18
  52.0 1.4 %collective-permute-start.17 = (f32[32,64]{1,0:T(8,128)S(1)}, f32[32,64]{1,0:T(8,128)S(1)}, u32[]{:S(2)}, u32[]{:S(2)}) collective-permute-start(f32[32,64]{1,0:T(8,128)S(1)} %corange_faces.1.refs_12_.refs_0_), channel_id=1, source_target_pairs={{0,8},{8,0},{16,24},{24,16},{1,9},{9,1},{17,25},{25,17},{2,10},{10... | collective-permute-start | bytes 24584 | tf_op jit(solution)/shard_map/ppermute | solution.py:447
  53.4 1.2 %collective-permute-done.19.refs_3_ = f32[32,64]{1,0:T(8,128)S(1)} collective-permute-done((f32[32,64]{1,0:T(8,128)S(1)}, f32[32,64]{1,0:T(8,128)S(1)}, u32[]{:S(2)}, u32[]{:S(2)}) %collective-permute-start.19) | collective-permute-done | bytes 8224 | tf_op jit(solution)/shard_map/ppermute | solution.py:447
  54.6 0.6 collective-permute-done.18.refs_2_
  55.2 0.6 collective-permute-done.17.refs_1_
  55.8 1.9 %collective-permute-start.22 = (f32[32,64]{1,0:T(8,128)S(1)}, f32[32,64]{1,0:T(8,128)S(1)}, u32[]{:S(2)}, u32[]{:S(2)}) collective-permute-start(f32[32,64]{1,0:T(8,128)S(1)} %line_sum.1), channel_id=1, source_target_pairs={{0,6},{2,4},{4,2},{6,0},{1,7},{3,5},{5,3},{7,1},{8,14},{10,12},{12... | collective-permute-start | bytes 24584 | tf_op jit(solution)/shard_map/ppermute | solution.py:447
  57.7 0.1 collective-permute-start.21
  57.8 2.5 %collective-permute-start.20 = (f32[32,64]{1,0:T(8,128)S(1)}, f32[32,64]{1,0:T(8,128)S(1)}, u32[]{:S(2)}, u32[]{:S(2)}) collective-permute-start(f32[32,64]{1,0:T(8,128)S(1)} %line_sum.1), channel_id=1, source_target_pairs={{0,2},{2,0},{4,6},{6,4},{1,3},{3,1},{5,7},{7,5},{8,10},{10,8},{12,... | collective-permute-start | bytes 24584 | tf_op jit(solution)/shard_map/ppermute | solution.py:447
  60.2 2.1 %range.1 = (bf16[32,16,16,128]{3,2,1,0:T(8,128)(2,1)}, f32[32,16,16,128]{3,2,1,0:T(8,128)}, f32[32,64]{1,0:T(8,128)S(1)}) custom-call(bf16[2,256,256]{2,1,0:T(8,128)(2,1)S(1)} %get-tuple-element.68.refs_3_.refs_11_.weight_ref, bf16[16,2,256,128]{3,2,1,0:T(8,128)(2,1)S(1)} %get-tuple-element.83.own_ref, ...), custom_call_target="tpu_custom_call", output_to_operand_aliasing={{1}: (5, {})} | custom-call | flops 1073741824 | bytes 4194304 | tf_op jit(solution)/shard_map/range/pallas_call | solution.py:35
  62.4 0.6 fusion.4
  (42 shorter events, 0.6 us)
Async XLA Ops:
  0.6 9.5 %copy-start.1 = (bf16[64,64]{1,0:T(8,128)(2,1)S(1)}, bf16[64,64]{1,0:T(8,128)(2,1)}, u32[]{:S(2)}) copy-start(bf16[64,64]{1,0:T(8,128)(2,1)} %param.8) | copy-start | bytes 24580
  2.4 17.7 %collective-permute-start.1 = (bf16[2,32,16,128]{3,2,1,0:T(8,128)(2,1)S(1)}, bf16[2,32,16,128]{3,2,1,0:T(8,128)(2,1)S(1)}, u32[]{:S(2)}, u32[]{:S(2)}) collective-permute-start(bf16[2,32,16,128]{3,2,1,0:T(8,128)(2,1)S(1)} %get-tuple-element.95), channel_id=1, source_target_pairs={{0,1},{1,0},{8,16},{9,17},{16,8},{17,9},{24,25},{25,24},{2,3},{3,2... | collective-permute-start | bytes 786440 | tf_op jit(solution)/shard_map/ppermute | solution.py:433
  2.9 17.2 %collective-permute-start = (bf16[2,32,16,128]{3,2,1,0:T(8,128)(2,1)S(1)}, bf16[2,32,16,128]{3,2,1,0:T(8,128)(2,1)S(1)}, u32[]{:S(2)}, u32[]{:S(2)}) collective-permute-start(bf16[2,32,16,128]{3,2,1,0:T(8,128)(2,1)S(1)} %get-tuple-element.96), channel_id=1, source_target_pairs={{0,8},{1,9},{8,0},{9,1},{16,24},{17,25},{24,16},{25,17},{2,10},{3,... | collective-permute-start | bytes 786440 | tf_op jit(solution)/shard_map/ppermute | solution.py:433
  6.9 13.3 %collective-permute-start.3 = (bf16[2,32,16,128]{3,2,1,0:T(8,128)(2,1)S(1)}, bf16[2,32,16,128]{3,2,1,0:T(8,128)(2,1)S(1)}, u32[]{:S(2)}, u32[]{:S(2)}) collective-permute-start(bf16[2,32,16,128]{3,2,1,0:T(8,128)(2,1)S(1)} %get-tuple-element.91), channel_id=1, source_target_pairs={{0,1},{1,0},{2,4},{3,5},{4,2},{5,3},{6,7},{7,6},{8,9},{9,8},{10,12... | collective-permute-start | bytes 786440 | tf_op jit(solution)/shard_map/ppermute | solution.py:433
  7.0 13.2 %collective-permute-start.2 = (bf16[2,32,16,128]{3,2,1,0:T(8,128)(2,1)S(1)}, bf16[2,32,16,128]{3,2,1,0:T(8,128)(2,1)S(1)}, u32[]{:S(2)}, u32[]{:S(2)}) collective-permute-start(bf16[2,32,16,128]{3,2,1,0:T(8,128)(2,1)S(1)} %get-tuple-element.92), channel_id=1, source_target_pairs={{0,2},{1,3},{2,0},{3,1},{4,6},{5,7},{6,4},{7,5},{8,10},{9,11},{10,... | collective-permute-start | bytes 786440 | tf_op jit(solution)/shard_map/ppermute | solution.py:433
  21.4 6.5 %collective-permute-start.5 = (bf16[32,16,128]{2,1,0:T(8,128)(2,1)S(1)}, bf16[32,16,128]{2,1,0:T(8,128)(2,1)S(1)}, u32[]{:S(2)}, u32[]{:S(2)}) collective-permute-start(bf16[32,16,128]{2,1,0:T(8,128)(2,1)S(1)} %get-tuple-element.119), channel_id=1, source_target_pairs={{0,1},{1,0},{8,16},{9,17},{16,8},{17,9},{24,25},{25,24},{2,3},{3,2... | collective-permute-start | bytes 393224 | tf_op jit(solution)/shard_map/ppermute | solution.py:433
  21.5 7.3 %collective-permute-start.4 = (bf16[32,16,128]{2,1,0:T(8,128)(2,1)S(1)}, bf16[32,16,128]{2,1,0:T(8,128)(2,1)S(1)}, u32[]{:S(2)}, u32[]{:S(2)}) collective-permute-start(bf16[32,16,128]{2,1,0:T(8,128)(2,1)S(1)} %get-tuple-element.120), channel_id=1, source_target_pairs={{0,8},{1,9},{8,0},{9,1},{16,24},{17,25},{24,16},{25,17},{2,10},{3,... | collective-permute-start | bytes 393224 | tf_op jit(solution)/shard_map/ppermute | solution.py:433
  23.1 5.8 %collective-permute-start.7 = (bf16[32,16,128]{2,1,0:T(8,128)(2,1)S(1)}, bf16[32,16,128]{2,1,0:T(8,128)(2,1)S(1)}, u32[]{:S(2)}, u32[]{:S(2)}) collective-permute-start(bf16[32,16,128]{2,1,0:T(8,128)(2,1)S(1)} %get-tuple-element.115), channel_id=1, source_target_pairs={{0,1},{1,0},{2,4},{3,5},{4,2},{5,3},{6,7},{7,6},{8,9},{9,8},{10,12... | collective-permute-start | bytes 393224 | tf_op jit(solution)/shard_map/ppermute | solution.py:433
  23.2 5.9 %collective-permute-start.6 = (bf16[32,16,128]{2,1,0:T(8,128)(2,1)S(1)}, bf16[32,16,128]{2,1,0:T(8,128)(2,1)S(1)}, u32[]{:S(2)}, u32[]{:S(2)}) collective-permute-start(bf16[32,16,128]{2,1,0:T(8,128)(2,1)S(1)} %get-tuple-element.116), channel_id=1, source_target_pairs={{0,2},{1,3},{2,0},{3,1},{4,6},{5,7},{6,4},{7,5},{8,10},{9,11},{10,... | collective-permute-start | bytes 393224 | tf_op jit(solution)/shard_map/ppermute | solution.py:433
  30.1 8.4 %collective-permute-start.9 = (bf16[32,16,128]{2,1,0:T(8,128)(2,1)S(1)}, bf16[32,16,128]{2,1,0:T(8,128)(2,1)S(1)}, u32[]{:S(2)}, u32[]{:S(2)}) collective-permute-start(bf16[32,16,128]{2,1,0:T(8,128)(2,1)S(1)} %get-tuple-element.111), channel_id=1, source_target_pairs={{0,1},{1,0},{8,16},{9,17},{16,8},{17,9},{24,25},{25,24},{2,3},{3,2... | collective-permute-start | bytes 393224 | tf_op jit(solution)/shard_map/ppermute | solution.py:433
  30.2 8.3 %collective-permute-start.8 = (bf16[32,16,128]{2,1,0:T(8,128)(2,1)S(1)}, bf16[32,16,128]{2,1,0:T(8,128)(2,1)S(1)}, u32[]{:S(2)}, u32[]{:S(2)}) collective-permute-start(bf16[32,16,128]{2,1,0:T(8,128)(2,1)S(1)} %get-tuple-element.112), channel_id=1, source_target_pairs={{0,8},{1,9},{8,0},{9,1},{16,24},{17,25},{24,16},{25,17},{2,10},{3,... | collective-permute-start | bytes 393224 | tf_op jit(solution)/shard_map/ppermute | solution.py:433
  32.2 6.4 %collective-permute-start.11 = (bf16[32,16,128]{2,1,0:T(8,128)(2,1)S(1)}, bf16[32,16,128]{2,1,0:T(8,128)(2,1)S(1)}, u32[]{:S(2)}, u32[]{:S(2)}) collective-permute-start(bf16[32,16,128]{2,1,0:T(8,128)(2,1)S(1)} %get-tuple-element.107), channel_id=1, source_target_pairs={{0,1},{1,0},{2,4},{3,5},{4,2},{5,3},{6,7},{7,6},{8,9},{9,8},{10,12... | collective-permute-start | bytes 393224 | tf_op jit(solution)/shard_map/ppermute | solution.py:433
  32.2 6.3 %collective-permute-start.10 = (bf16[32,16,128]{2,1,0:T(8,128)(2,1)S(1)}, bf16[32,16,128]{2,1,0:T(8,128)(2,1)S(1)}, u32[]{:S(2)}, u32[]{:S(2)}) collective-permute-start(bf16[32,16,128]{2,1,0:T(8,128)(2,1)S(1)} %get-tuple-element.108), channel_id=1, source_target_pairs={{0,2},{1,3},{2,0},{3,1},{4,6},{5,7},{6,4},{7,5},{8,10},{9,11},{10,... | collective-permute-start | bytes 393224 | tf_op jit(solution)/shard_map/ppermute | solution.py:433
  39.6 8.1 %collective-permute-start.13 = (bf16[32,16,128]{2,1,0:T(8,128)(2,1)S(1)}, bf16[32,16,128]{2,1,0:T(8,128)(2,1)S(1)}, u32[]{:S(2)}, u32[]{:S(2)}) collective-permute-start(bf16[32,16,128]{2,1,0:T(8,128)(2,1)S(1)} %get-tuple-element.103), channel_id=1, source_target_pairs={{0,1},{1,0},{8,16},{9,17},{16,8},{17,9},{24,25},{25,24},{2,3},{3,2... | collective-permute-start | bytes 393224 | tf_op jit(solution)/shard_map/ppermute | solution.py:433
  39.7 8.1 %collective-permute-start.12 = (bf16[32,16,128]{2,1,0:T(8,128)(2,1)S(1)}, bf16[32,16,128]{2,1,0:T(8,128)(2,1)S(1)}, u32[]{:S(2)}, u32[]{:S(2)}) collective-permute-start(bf16[32,16,128]{2,1,0:T(8,128)(2,1)S(1)} %get-tuple-element.104), channel_id=1, source_target_pairs={{0,8},{1,9},{8,0},{9,1},{16,24},{17,25},{24,16},{25,17},{2,10},{3,... | collective-permute-start | bytes 393224 | tf_op jit(solution)/shard_map/ppermute | solution.py:433
  41.8 5.9 %collective-permute-start.15 = (bf16[32,16,128]{2,1,0:T(8,128)(2,1)S(1)}, bf16[32,16,128]{2,1,0:T(8,128)(2,1)S(1)}, u32[]{:S(2)}, u32[]{:S(2)}) collective-permute-start(bf16[32,16,128]{2,1,0:T(8,128)(2,1)S(1)} %get-tuple-element.99), channel_id=1, source_target_pairs={{0,1},{1,0},{2,4},{3,5},{4,2},{5,3},{6,7},{7,6},{8,9},{9,8},{10,12... | collective-permute-start | bytes 393224 | tf_op jit(solution)/shard_map/ppermute | solution.py:433
  41.9 5.9 %collective-permute-start.14 = (bf16[32,16,128]{2,1,0:T(8,128)(2,1)S(1)}, bf16[32,16,128]{2,1,0:T(8,128)(2,1)S(1)}, u32[]{:S(2)}, u32[]{:S(2)}) collective-permute-start(bf16[32,16,128]{2,1,0:T(8,128)(2,1)S(1)} %get-tuple-element.100), channel_id=1, source_target_pairs={{0,2},{1,3},{2,0},{3,1},{4,6},{5,7},{6,4},{7,5},{8,10},{9,11},{10,... | collective-permute-start | bytes 393224 | tf_op jit(solution)/shard_map/ppermute | solution.py:433
  49.8 10.5 %collective-permute-start.16 = (bf16[16,2,256,128]{3,2,1,0:T(8,128)(2,1)S(1)}, bf16[16,2,256,128]{3,2,1,0:T(8,128)(2,1)S(1)}, u32[]{:S(2)}, u32[]{:S(2)}) collective-permute-start(bf16[16,2,256,128]{3,2,1,0:T(8,128)(2,1)S(1)} %get-tuple-element.83.own_ref), channel_id=1, source_target_pairs={{0,1},{1,0},{2,3},{3,2},{4,5},{5,4},{6,7},{7,6},{8,9},{9,8},{10,11... | collective-permute-start | bytes 6291464 | tf_op jit(solution)/shard_map/ppermute | solution.py:585
  49.9 4.7 %collective-permute-start.19 = (f32[32,64]{1,0:T(8,128)S(1)}, f32[32,64]{1,0:T(8,128)S(1)}, u32[]{:S(2)}, u32[]{:S(2)}) collective-permute-start(f32[32,64]{1,0:T(8,128)S(1)} %corange_faces.1.refs_12_.refs_0_), channel_id=1, source_target_pairs={{0,24},{8,16},{16,8},{24,0},{1,25},{9,17},{17,9},{25,1},{2,26},{10... | collective-permute-start | bytes 24584 | tf_op jit(solution)/shard_map/ppermute | solution.py:447
  51.5 3.7 %collective-permute-start.18 = (f32[32,64]{1,0:T(8,128)S(1)}, f32[32,64]{1,0:T(8,128)S(1)}, u32[]{:S(2)}, u32[]{:S(2)}) collective-permute-start(f32[32,64]{1,0:T(8,128)S(1)} %corange_faces.1.refs_12_.refs_0_), channel_id=1, source_target_pairs={{0,16},{8,24},{16,0},{24,8},{1,17},{9,25},{17,1},{25,9},{2,18},{10... | collective-permute-start | bytes 24584 | tf_op jit(solution)/shard_map/ppermute | solution.py:447
  52.0 3.7 %collective-permute-start.17 = (f32[32,64]{1,0:T(8,128)S(1)}, f32[32,64]{1,0:T(8,128)S(1)}, u32[]{:S(2)}, u32[]{:S(2)}) collective-permute-start(f32[32,64]{1,0:T(8,128)S(1)} %corange_faces.1.refs_12_.refs_0_), channel_id=1, source_target_pairs={{0,8},{8,0},{16,24},{24,16},{1,9},{9,1},{17,25},{25,17},{2,10},{10... | collective-permute-start | bytes 24584 | tf_op jit(solution)/shard_map/ppermute | solution.py:447
  55.8 6.6 %collective-permute-start.22 = (f32[32,64]{1,0:T(8,128)S(1)}, f32[32,64]{1,0:T(8,128)S(1)}, u32[]{:S(2)}, u32[]{:S(2)}) collective-permute-start(f32[32,64]{1,0:T(8,128)S(1)} %line_sum.1), channel_id=1, source_target_pairs={{0,6},{2,4},{4,2},{6,0},{1,7},{3,5},{5,3},{7,1},{8,14},{10,12},{12... | collective-permute-start | bytes 24584 | tf_op jit(solution)/shard_map/ppermute | solution.py:447
  57.7 4.7 %collective-permute-start.21 = (f32[32,64]{1,0:T(8,128)S(1)}, f32[32,64]{1,0:T(8,128)S(1)}, u32[]{:S(2)}, u32[]{:S(2)}) collective-permute-start(f32[32,64]{1,0:T(8,128)S(1)} %line_sum.1), channel_id=1, source_target_pairs={{0,4},{2,6},{4,0},{6,2},{1,5},{3,7},{5,1},{7,3},{8,12},{10,14},{12... | collective-permute-start | bytes 24584 | tf_op jit(solution)/shard_map/ppermute | solution.py:447
  57.8 4.6 %collective-permute-start.20 = (f32[32,64]{1,0:T(8,128)S(1)}, f32[32,64]{1,0:T(8,128)S(1)}, u32[]{:S(2)}, u32[]{:S(2)}) collective-permute-start(f32[32,64]{1,0:T(8,128)S(1)} %line_sum.1), channel_id=1, source_target_pairs={{0,2},{2,0},{4,6},{6,4},{1,3},{3,1},{5,7},{7,5},{8,10},{10,8},{12,... | collective-permute-start | bytes 24584 | tf_op jit(solution)/shard_map/ppermute | solution.py:447
  60.2 2.2 %copy-start = (f32[64,32]{0,1:T(8,128)S(1)}, f32[64,32]{0,1:T(8,128)}, u32[]{:S(2)}) copy-start(f32[64,32]{0,1:T(8,128)} %param.11) | copy-start | bytes 24580

commit v5 on v4

--- a/solution.py
+++ b/solution.py
@@ -186,25 +186,25 @@
     lax.fori_loop(0, samples // BLOCK, body, 0)
 
 
-def edge_kernel(send, w_in, u_ref, cx0, cx1, cy0, cy1, hx0, hx1, hy0, hy1, *refs):
+def edge_kernel(lined, w_in, u_ref, *refs):
     del w_in
-    w_ref, lx, ux, ly, uy = refs[-5:] if send else (refs[-1],) + (None,) * 4
+    cx0, cx1, cy0, cy1, hx0, hx1, hy0, hy1 = refs[:8]
+    w_ref, lx, ux, ly, uy, *lines = refs[-7:]
     samples, nx, ny, nz = u_ref.shape
     w_rows, u_rows = flat(w_ref), flat(u_ref)
 
     def one(s):
-        for y, coef, halo in ((0, cy0, hy0), (ny - 1, cy1, hy1)):
-            line = y_line(u_ref, s, y)
-            flux = coef[s] * (halo[s].astype(F32) - u_rows[line, :])
-            w_rows[line, :] = w_rows[line, :] + flux
-        for x, coef, halo, out in ((0, cx0, hx0, lx), (nx - 1, cx1, hx1, ux)):
-            value = w_ref[s, x] + coef[s] * (halo[s].astype(F32) - u_ref[s, x])
-            w_ref[s, x] = value
-            if send:
-                out[s] = value.astype(BF)
-        if send:
-            for y, out in ((0, ly), (ny - 1, uy)):
-                out[s] = w_rows[y_line(u_ref, s, y), :].astype(BF)
+        for x, coef, halo in ((0, cx0, hx0), (nx - 1, cx1, hx1)):
+            w_ref[s, x] = w_ref[s, x] + coef[s] * (halo[s].astype(F32) - u_ref[s, x])
+        for end, (coef, halo, out) in enumerate(((cy0, hy0, ly), (cy1, hy1, uy))):
+            line = y_line(u_ref, s, end * (ny - 1))
+            state = refs[8 + end][s] if lined else u_rows[line, :]
+            value = w_rows[line, :] + coef[s] * (halo[s].astype(F32) - state)
+            w_rows[line, :] = value
+            out[s] = value.astype(BF)
+            lines[end][s] = value
+        lx[s] = w_ref[s, 0].astype(BF)
+        ux[s] = w_ref[s, nx - 1].astype(BF)
 
     def body(i, carry):
         for j in range(4):
@@ -359,16 +359,31 @@
     return lax.dot_general(left, right, (((1,), (1,)), ((), ())), preferred_element_type=F32)
 
 
-def corange_faces_kernel(
-    main_ref, px, py, u_ref, cx0, cx1, cy0, cy1, hx0, hx1, hy0, hy1, out_ref, xbuf, ybuf
-):
+def finish_kernel(w_in, u_ref, cx0, cx1, cy0, cy1, hx0, hx1, hy0, hy1, *refs):
+    del w_in
+    ends, (main_ref, px, py) = refs[:2], refs[2:5]
+    w_ref, out_ref, snap_ref, xbuf, ybuf = refs[-5:]
     samples, nx, ny, nz = u_ref.shape
-    rows = flat(u_ref)
-    for end, x, coef, halo in ((0, 0, cx0, hx0), (1, nx - 1, cx1, hx1)):
-        xbuf[end] = coef[...] * (halo[...].astype(F32) - u_ref[:, x])
-    for end, y, coef, halo in ((0, 0, cy0, hy0), (1, ny - 1, cy1, hy1)):
-        for s in range(samples):
-            ybuf[end, s] = coef[s] * (halo[s].astype(F32) - rows[y_line(u_ref, s, y), :])
+    w_rows = flat(w_ref)
+
+    def one(s):
+        for end, (coef, halo) in enumerate(((cx0, hx0), (cx1, hx1))):
+            x = end * (nx - 1)
+            flux = coef[s] * (halo[s].astype(F32) - u_ref[s, x])
+            xbuf[end, s] = flux
+            w_ref[s, x] = w_ref[s, x] + flux
+        for end, (coef, halo) in enumerate(((cy0, hy0), (cy1, hy1))):
+            line = y_line(u_ref, s, end * (ny - 1))
+            flux = coef[s] * (halo[s].astype(F32) - ends[end][s])
+            ybuf[end, s] = flux
+            w_rows[line, :] = w_rows[line, :] + flux
+
+    def patch(i, carry):
+        for j in range(4):
+            one(i * 4 + j)
+        return carry
+
+    lax.fori_loop(0, samples // 4, patch, 0)
     total = main_ref[...]
     for buf, psi in ((xbuf, px), (ybuf, py)):
         count = buf.shape[2]
@@ -381,12 +396,6 @@
             right = [psi[end, i] for end in range(2)]
             total = total + contract(jnp.concatenate(left, axis=1), jnp.concatenate(right, axis=1))
     out_ref[...] = total
-
-
-def finish_kernel(*refs):
-    w_ref, snap_ref = refs[-2:]
-    edge_kernel(False, *refs[:-1])
-    nx = w_ref.shape[1]
 
     def body(x, carry):
         split_into(snap_ref, x, w_ref[:, x])
@@ -506,6 +515,7 @@
         nbytes=4 * cells,
     )(psi)
     kept = (held_psi, psi_y)
+    lines = []
     for step in range(STEPS):
         if step > 0:
             halos = exchange(edges)
@@ -540,14 +550,16 @@
             )(psi, range_prev, omega_blocks, moved)
             kept += (psi_x, weights, prev)
         if step < STEPS - 1:
+            outs = [(block, F32)] + [(x_face, BF)] * 2 + [(y_face, BF)] * 2 + [(y_face, F32)] * 2
             state, *edges = vmem_call(
-                functools.partial(edge_kernel, True),
-                [(block, F32), (x_face, BF), (x_face, BF), (y_face, BF), (y_face, BF)],
+                functools.partial(edge_kernel, step > 0),
+                outs,
                 "edge",
                 aliases={0: 0},
                 flops=cells,
                 nbytes=cells,
-            )(moved, state, *face_coefs, *halos, *kept)
+            )(moved, state, *face_coefs, *halos, *lines, *kept)
+            edges, lines = edges[:4], edges[4:]
 
     main, written = vmem_call(
         corange_kernel,
@@ -565,23 +577,16 @@
         flops=2 * ranks * ROWS * cells,
         nbytes=4 * cells,
     )(held_psi, moved, *written)
-    partial_sum = vmem_call(
-        corange_faces_kernel,
-        [((samples, ranks), F32)],
-        "corange_faces",
+    final, partial_sum, snapshot = vmem_call(
+        finish_kernel,
+        [(block, F32), ((samples, ranks), F32), (split_shape(block), BF)],
+        "finish",
         scratch=[pltpu.VMEM((2,) + x_face, F32), pltpu.VMEM((2,) + y_face, F32)],
-        flops=cells,
-        nbytes=cells,
-    )(main, psi_x, psi_y, state, *face_coefs, *halos)[0]
-    first_sums = received(partial_sum, "sx")
-    final, snapshot = vmem_call(
-        finish_kernel,
-        [(block, F32), (split_shape(block), BF)],
-        "finish",
         aliases={0: 0},
         flops=cells,
         nbytes=2 * cells,
-    )(moved, state, *face_coefs, *halos, prev, weights, partial_sum)
+    )(moved, state, *face_coefs, *halos, *lines, main, psi_x, psi_y, prev, weights)
+    first_sums = received(partial_sum, "sx")
     other = lax.ppermute(snapshot, "par", [(i, (i + 1) % par_size) for i in range(par_size)])
     range_sketch, final_state, done = vmem_call(
         range_kernel,

time: 63.2 us -> 61.9 us (0.979)
  Pallas kernels: 30.8 us -> 29.5 us
    pallas_call x15 -> x14, Pallas kernels: 30.8 us -> 29.5 us  [call(): pl.pallas_call(kernel, out_shape=out_shape, in_specs=in_specs, out_specs=...]
  transfers between devices with their start and end apart: 23 -> 23, of which waited for: 6 -> 6; matrix products, arithmetic and copies ran while one was open for 1% -> 1% of each run, Pallas kernels for 39% -> 40%
where the time goes in v5:
time: 61.9 us; the launch traced here: 61.7 us
  Pallas kernels  29.5 us (48%)
  starting transfers between devices  26.1 us (42%)
  waiting for transfers between devices  3.56 us (6%)
  other arithmetic  1.25 us (2%)
  between operations  1.07 us (2%)
    pallas_call x14, Pallas kernels, call(): pl.pallas_call(kernel, out_shape=out_shape, in_specs=in_specs, out_specs=...  29.5 us
    ppermute x16, starting transfers between devices, exchange(): got[axis, parity] = lax.ppermute(mine, (axis, 'par'), pairs)  18 us
    ppermute x6, starting transfers between devices, received(): lax.ppermute(value, axis, [(i, i ^ shift) for i in range(count)])  8 us
    ppermute x6, waiting for transfers between devices, received(): lax.ppermute(value, axis, [(i, i ^ shift) for i in range(count)])  2.36 us
  transfers between devices with their start and end apart: 23, of which 6 were waited for; matrix products, arithmetic and copies ran while one was open for 1% of the time, Pallas kernels for 40%

profile of v5, /device:TPU:0, one launch (start us, length us, event | category | flops | bytes accessed | tf_op | source)
XLA Modules:
  0.0 61.7 jit_solution(11199789640561110298)
XLA Ops:
  0.7 1.7 %faces.1 = (bf16[2,32,16,128]{3,2,1,0:T(8,128)(2,1)S(1)}, bf16[2,32,16,128]{3,2,1,0:T(8,128)(2,1)S(1)}, bf16[2,32,16,128]{3,2,1,0:T(8,128)(2,1)S(1)}, bf16[2,32,16,128]{3,2,1,0:T(8,128)(2,1)S(1)}) custom-call(f32[32,16,16,128]{3,2,1,0:T(8,128)} %u_ref.1, f32[32,16,16,128]{3,2,1,0:T(8,128)} %k_ref.1), custom_call_target="tpu_custom_call" | custom-call | flops 524288 | bytes 1048576 | tf_op jit(solution)/shard_map/faces/pallas_call | solution.py:35
  2.4 0.5 collective-permute-start.1
  2.9 4.0 %collective-permute-start = (bf16[2,32,16,128]{3,2,1,0:T(8,128)(2,1)S(1)}, bf16[2,32,16,128]{3,2,1,0:T(8,128)(2,1)S(1)}, u32[]{:S(2)}, u32[]{:S(2)}) collective-permute-start(bf16[2,32,16,128]{3,2,1,0:T(8,128)(2,1)S(1)} %get-tuple-element.110), channel_id=1, source_target_pairs={{0,8},{1,9},{8,0},{9,1},{16,24},{17,25},{24,16},{25,17},{2,10},{3,... | collective-permute-start | bytes 786440 | tf_op jit(solution)/shard_map/ppermute | solution.py:442
  6.9 0.1 collective-permute-start.3
  7.0 3.1 %collective-permute-start.2 = (bf16[2,32,16,128]{3,2,1,0:T(8,128)(2,1)S(1)}, bf16[2,32,16,128]{3,2,1,0:T(8,128)(2,1)S(1)}, u32[]{:S(2)}, u32[]{:S(2)}) collective-permute-start(bf16[2,32,16,128]{3,2,1,0:T(8,128)(2,1)S(1)} %get-tuple-element.106), channel_id=1, source_target_pairs={{0,2},{1,3},{2,0},{3,1},{4,6},{5,7},{6,4},{7,5},{8,10},{9,11},{10,... | collective-permute-start | bytes 786440 | tf_op jit(solution)/shard_map/ppermute | solution.py:442
  10.1 0.1 fusion.5
  10.2 0.1 copy.17
  10.3 0.1 copy.18
  10.4 3.0 %psi.1 = (bf16[16,2,512,128]{3,2,1,0:T(8,128)(2,1)S(1)}, bf16[2,16,64,128]{3,2,1,0:T(8,128)(2,1)S(1)}) custom-call(bf16[64,16,16,128]{3,2,1,0:T(8,128)(2,1)} %psi_hbm.3), custom_call_target="tpu_custom_call" | custom-call | flops 4194304 | bytes 4194304 | tf_op jit(solution)/shard_map/psi/pallas_call | solution.py:35
  13.4 6.7 %first.1 = (f32[32,16,16,128]{3,2,1,0:T(8,128)S(1)}, f32[32,16,16,128]{3,2,1,0:T(8,128)S(1)}, f32[32,16,16,128]{3,2,1,0:T(8,128)S(1)}, f32[32,16,16,128]{3,2,1,0...) custom-call(f32[32,16,16,128]{3,2,1,0:T(8,128)} %u_ref.1, ...), custom_call_target="tpu_custom_call" | custom-call | flops 37748736 | bytes 16777216 | tf_op jit(solution)/shard_map/first/pallas_call | solution.py:35
  20.3 0.1 bitcast_add_fusion.2
  20.4 0.1 bitcast_add_fusion
  20.4 0.8 %edge.3 = (f32[32,16,16,128]{3,2,1,0:T(8,128)S(1)}, bf16[32,16,128]{2,1,0:T(8,128)(2,1)S(1)}, bf16[32,16,128]{2,1,0:T(8,128)(2,1)S(1)}, bf16[32,16,128]{2,1,0:T(...) custom-call(f32[32,16,16,128]{3,2,1,0:T(8,128)S(1)} %get-tuple-eleme, ...), custom_call_target="tpu_custom_call", output_to_operand_aliasing={{0}: (0, {})} | custom-call | flops 1048576 | bytes 1048576 | tf_op jit(solution)/shard_map/edge/pallas_call | solution.py:35
  21.3 0.1 collective-permute-start.5
  21.3 1.6 %collective-permute-start.4 = (bf16[32,16,128]{2,1,0:T(8,128)(2,1)S(1)}, bf16[32,16,128]{2,1,0:T(8,128)(2,1)S(1)}, u32[]{:S(2)}, u32[]{:S(2)}) collective-permute-start(bf16[32,16,128]{2,1,0:T(8,128)(2,1)S(1)} %get-tuple-element.134), channel_id=1, source_target_pairs={{0,8},{1,9},{8,0},{9,1},{16,24},{17,25},{24,16},{25,17},{2,10},{3,... | collective-permute-start | bytes 393224 | tf_op jit(solution)/shard_map/ppermute | solution.py:442
  22.9 0.1 collective-permute-start.7
  23.0 1.7 %collective-permute-start.6 = (bf16[32,16,128]{2,1,0:T(8,128)(2,1)S(1)}, bf16[32,16,128]{2,1,0:T(8,128)(2,1)S(1)}, u32[]{:S(2)}, u32[]{:S(2)}) collective-permute-start(bf16[32,16,128]{2,1,0:T(8,128)(2,1)S(1)} %get-tuple-element.130), channel_id=1, source_target_pairs={{0,2},{1,3},{2,0},{3,1},{4,6},{5,7},{6,4},{7,5},{8,10},{9,11},{10,... | collective-permute-start | bytes 393224 | tf_op jit(solution)/shard_map/ppermute | solution.py:442
  24.7 3.0 %step.3.w_in = f32[32,16,16,128]{3,2,1,0:T(8,128)S(1)} custom-call(f32[32,16,16,128]{3,2,1,0:T(8,128)S(1)} %get-tuple-element.65.u_ref, f32[32,16,16,128]{3,2,1,0:T(8,128)S(1)} %get-tuple-element.66.cx_ref, f32[32,16,16,128]{3,2,1,0:T(8,128)S(1)} %get-tuple-element.67.cy_ref, f32[32,16,16,128]{3,2,1,0:T(8,128)S(1)} %get-tuple-element.68.cup_ref, ...), custom_call_target="tpu_custom_call" | custom-call | flops 25165824 | bytes 8388608 | tf_op jit(solution)/shard_map/step/pallas_call | solution.py:35
  27.8 0.9 %collective-permute-done.4 = bf16[32,16,128]{2,1,0:T(8,128)(2,1)S(1)} collective-permute-done((bf16[32,16,128]{2,1,0:T(8,128)(2,1)S(1)}, bf16[32,16,128]{2,1,0:T(8,128)(2,1)S(1)}, u32[]{:S(2)}, u32[]{:S(2)}) %collective-permute-start.4) | collective-permute-done | bytes 131104 | tf_op jit(solution)/shard_map/ppermute | solution.py:442
  28.7 0.2 collective-permute-done.6
  29.0 0.6 %edge.4 = (f32[32,16,16,128]{3,2,1,0:T(8,128)S(1)}, bf16[32,16,128]{2,1,0:T(8,128)(2,1)S(1)}, bf16[32,16,128]{2,1,0:T(8,128)(2,1)S(1)}, bf16[32,16,128]{2,1,0:T(...) custom-call(f32[32,16,16,128]{3,2,1,0:T(8,128)S(1)} %step.3.w_in, ...), custom_call_target="tpu_custom_call", output_to_operand_aliasing={{0}: (0, {})} | custom-call | flops 1048576 | bytes 1048576 | tf_op jit(solution)/shard_map/edge/pallas_call | solution.py:35
  29.6 0.1 collective-permute-start.9
  29.7 1.9 %collective-permute-start.8 = (bf16[32,16,128]{2,1,0:T(8,128)(2,1)S(1)}, bf16[32,16,128]{2,1,0:T(8,128)(2,1)S(1)}, u32[]{:S(2)}, u32[]{:S(2)}) collective-permute-start(bf16[32,16,128]{2,1,0:T(8,128)(2,1)S(1)} %get-tuple-element.126), channel_id=1, source_target_pairs={{0,8},{1,9},{8,0},{9,1},{16,24},{17,25},{24,16},{25,17},{2,10},{3,... | collective-permute-start | bytes 393224 | tf_op jit(solution)/shard_map/ppermute | solution.py:442
  31.7 0.1 collective-permute-start.11
  31.8 1.4 %collective-permute-start.10 = (bf16[32,16,128]{2,1,0:T(8,128)(2,1)S(1)}, bf16[32,16,128]{2,1,0:T(8,128)(2,1)S(1)}, u32[]{:S(2)}, u32[]{:S(2)}) collective-permute-start(bf16[32,16,128]{2,1,0:T(8,128)(2,1)S(1)} %get-tuple-element.122), channel_id=1, source_target_pairs={{0,2},{1,3},{2,0},{3,1},{4,6},{5,7},{6,4},{7,5},{8,10},{9,11},{10,... | collective-permute-start | bytes 393224 | tf_op jit(solution)/shard_map/ppermute | solution.py:442
  33.1 3.0 %step.4.after.w_in = f32[32,16,16,128]{3,2,1,0:T(8,128)S(1)} custom-call(f32[32,16,16,128]{3,2,1,0:T(8,128)S(1)} %get-tuple-element.76.u_ref, f32[32,16,16,128]{3,2,1,0:T(8,128)S(1)} %get-tuple-element.66.cx_ref, f32[32,16,16,128]{3,2,1,0:T(8,128)S(1)} %get-tuple-element.67.cy_ref, f32[32,16,16,128]{3,2,1,0:T(8,128)S(1)} %get-tuple-element.68.cup_ref, ...), custom_call_target="tpu_custom_call" | custom-call | flops 25165824 | bytes 8388608 | tf_op jit(solution)/shard_map/step/pallas_call | solution.py:35
  36.2 1.8 %lines.1 = (bf16[2,16,64,128]{3,2,1,0:T(8,128)(2,1)S(1)}, bf16[2,256,256]{2,1,0:T(8,128)(2,1)S(1)}, bf16[32,16,16,128]{3,2,1,0:T(8,128)(2,1)S(1)}) custom-call(bf16[64,16,16,128]{3,2,1,0:T(8,128)(2,1)} %psi_hbm.3, bf16[32,16,16,128]{3,2,1,0:T(8,128)(2,1)} %prev_hbm.1, bf16[2,32,32]{2,1,0:T(8,128)(2,1)S(1)} %pad_maximum_fusion.omega_ref, ...), custom_call_target="tpu_custom_call" | custom-call | flops 1048576 | bytes 1048576 | tf_op jit(solution)/shard_map/lines/pallas_call | solution.py:35
  38.1 0.6 %edge.5 = (f32[32,16,16,128]{3,2,1,0:T(8,128)S(1)}, bf16[32,16,128]{2,1,0:T(8,128)(2,1)S(1)}, bf16[32,16,128]{2,1,0:T(8,128)(2,1)S(1)}, bf16[32,16,128]{2,1,0:T(...) custom-call(f32[32,16,16,128]{3,2,1,0:T(8,128)S(1)} %step.4.after.w_, ...), custom_call_target="tpu_custom_call", output_to_operand_aliasing={{0}: (0, {})} | custom-call | flops 1048576 | bytes 1048576 | tf_op jit(solution)/shard_map/edge/pallas_call | solution.py:35
  38.8 0.1 collective-permute-start.13
  38.9 2.1 %collective-permute-start.12 = (bf16[32,16,128]{2,1,0:T(8,128)(2,1)S(1)}, bf16[32,16,128]{2,1,0:T(8,128)(2,1)S(1)}, u32[]{:S(2)}, u32[]{:S(2)}) collective-permute-start(bf16[32,16,128]{2,1,0:T(8,128)(2,1)S(1)} %get-tuple-element.118), channel_id=1, source_target_pairs={{0,8},{1,9},{8,0},{9,1},{16,24},{17,25},{24,16},{25,17},{2,10},{3,... | collective-permute-start | bytes 393224 | tf_op jit(solution)/shard_map/ppermute | solution.py:442
  41.0 0.1 collective-permute-start.15
  41.1 1.1 %collective-permute-start.14 = (bf16[32,16,128]{2,1,0:T(8,128)(2,1)S(1)}, bf16[32,16,128]{2,1,0:T(8,128)(2,1)S(1)}, u32[]{:S(2)}, u32[]{:S(2)}) collective-permute-start(bf16[32,16,128]{2,1,0:T(8,128)(2,1)S(1)} %get-tuple-element.114), channel_id=1, source_target_pairs={{0,2},{1,3},{2,0},{3,1},{4,6},{5,7},{6,4},{7,5},{8,10},{9,11},{10,... | collective-permute-start | bytes 393224 | tf_op jit(solution)/shard_map/ppermute | solution.py:442
  42.2 3.1 %step.5 = (f32[32,16,16,128]{3,2,1,0:T(8,128)S(1)}, f32[32,16,16,128]{3,2,1,0:T(8,128)}) custom-call(f32[32,16,16,128]{3,2,1,0:T(8,128)S(1)} %get-tuple-element.86.u_ref, f32[32,16,16,128]{3,2,1,0:T(8,128)S(1)} %get-tuple-element.66.cx_ref, f32[32,16,16,128]{3,2,1,0:T(8,128)S(1)} %get-tuple-element.67.cy_ref, ...), custom_call_target="tpu_custom_call" | custom-call | flops 25165824 | bytes 8388608 | tf_op jit(solution)/shard_map/step/pallas_call | solution.py:35
  45.3 1.6 %corange.1 = (f32[32,64]{1,0:T(8,128)S(1)}, f32[32,16,16,128]{3,2,1,0:T(8,128)}) custom-call(bf16[16,2,512,128]{3,2,1,0:T(8,128)(2,1)S(1)} %get-tuple-element.63.refs_8_.refs_0_.refs_10_.psi_ref, f32[32,16,16,128]{3,2,1,0:T(8,128)S(1)} %get-tuple-element.87.u_ref.w_in, f32[32,16,16,128]{3,2,1,0:T(8,128)} %get-tuple-element.94.state_in), custom_call_target="tpu_custom_call", output_to_operand_aliasing={{1}: (2, {})} | custom-call | flops 1073741824 | bytes 4194304 | tf_op jit(solution)/shard_map/corange/pallas_call | solution.py:35
  47.0 0.1 collective-permute-done.14
  47.1 1.4 %finish.1 = (f32[32,16,16,128]{3,2,1,0:T(8,128)S(1)}, f32[32,64]{1,0:T(8,128)S(1)}, bf16[16,2,256,128]{3,2,1,0:T(8,128)(2,1)S(1)}) custom-call(f32[32,16,16,128]{3,2,1,0:T(8,128)S(1)} %get-tuple-element.87.u_ref.w_in, f32[32,16,16,128]{3,2,1,0:T(8,128)S(1)} %get-tuple-element.86.u_ref, ...), custom_call_target="tpu_custom_call", output_to_operand_aliasing={{0}: (0, {})} | custom-call | flops 1048576 | bytes 2097152 | tf_op jit(solution)/shard_map/finish/pallas_call | solution.py:35
  48.4 0.1 collective-permute-start.16
  48.5 1.6 %collective-permute-start.19 = (f32[32,64]{1,0:T(8,128)S(1)}, f32[32,64]{1,0:T(8,128)S(1)}, u32[]{:S(2)}, u32[]{:S(2)}) collective-permute-start(f32[32,64]{1,0:T(8,128)S(1)} %get-tuple-element.101.refs_0_), channel_id=1, source_target_pairs={{0,24},{8,16},{16,8},{24,0},{1,25},{9,17},{17,9},{25,1},{2,26},{10... | collective-permute-start | bytes 24584 | tf_op jit(solution)/shard_map/ppermute | solution.py:456
  50.1 0.6 collective-permute-start.18
  50.7 1.4 %collective-permute-start.17 = (f32[32,64]{1,0:T(8,128)S(1)}, f32[32,64]{1,0:T(8,128)S(1)}, u32[]{:S(2)}, u32[]{:S(2)}) collective-permute-start(f32[32,64]{1,0:T(8,128)S(1)} %get-tuple-element.101.refs_0_), channel_id=1, source_target_pairs={{0,8},{8,0},{16,24},{24,16},{1,9},{9,1},{17,25},{25,17},{2,10},{10... | collective-permute-start | bytes 24584 | tf_op jit(solution)/shard_map/ppermute | solution.py:456
  52.1 1.2 %collective-permute-done.19.refs_3_ = f32[32,64]{1,0:T(8,128)S(1)} collective-permute-done((f32[32,64]{1,0:T(8,128)S(1)}, f32[32,64]{1,0:T(8,128)S(1)}, u32[]{:S(2)}, u32[]{:S(2)}) %collective-permute-start.19) | collective-permute-done | bytes 8224 | tf_op jit(solution)/shard_map/ppermute | solution.py:456
  53.2 0.6 %collective-permute-done.18.refs_2_ = f32[32,64]{1,0:T(8,128)S(1)} collective-permute-done((f32[32,64]{1,0:T(8,128)S(1)}, f32[32,64]{1,0:T(8,128)S(1)}, u32[]{:S(2)}, u32[]{:S(2)}) %collective-permute-start.18) | collective-permute-done | bytes 8224 | tf_op jit(solution)/shard_map/ppermute | solution.py:456
  53.9 0.6 collective-permute-done.17.refs_1_
  54.4 1.9 %collective-permute-start.22 = (f32[32,64]{1,0:T(8,128)S(1)}, f32[32,64]{1,0:T(8,128)S(1)}, u32[]{:S(2)}, u32[]{:S(2)}) collective-permute-start(f32[32,64]{1,0:T(8,128)S(1)} %line_sum.1), channel_id=1, source_target_pairs={{0,6},{2,4},{4,2},{6,0},{1,7},{3,5},{5,3},{7,1},{8,14},{10,12},{12... | collective-permute-start | bytes 24584 | tf_op jit(solution)/shard_map/ppermute | solution.py:456
  56.3 0.1 collective-permute-start.21
  56.4 2.5 %collective-permute-start.20 = (f32[32,64]{1,0:T(8,128)S(1)}, f32[32,64]{1,0:T(8,128)S(1)}, u32[]{:S(2)}, u32[]{:S(2)}) collective-permute-start(f32[32,64]{1,0:T(8,128)S(1)} %line_sum.1), channel_id=1, source_target_pairs={{0,2},{2,0},{4,6},{6,4},{1,3},{3,1},{5,7},{7,5},{8,10},{10,8},{12,... | collective-permute-start | bytes 24584 | tf_op jit(solution)/shard_map/ppermute | solution.py:456
  58.9 2.2 %range.1 = (bf16[32,16,16,128]{3,2,1,0:T(8,128)(2,1)}, f32[32,16,16,128]{3,2,1,0:T(8,128)}, f32[32,64]{1,0:T(8,128)S(1)}) custom-call(bf16[2,256,256]{2,1,0:T(8,128)(2,1)S(1)} %get-tuple-element.77.refs_13_.refs_3_.refs_6_.weight_ref, bf16[16,2,256,128]{3,2,1,0:T(8,128)(2,1)S(1)} %get-tuple-element.96.own_ref, ...), custom_call_target="tpu_custom_call", output_to_operand_aliasing={{1}: (5, {})} | custom-call | flops 1073741824 | bytes 4194304 | tf_op jit(solution)/shard_map/range/pallas_call | solution.py:35
  61.1 0.6 fusion.4
  (41 shorter events, 0.6 us)
Async XLA Ops:
  0.6 9.5 %copy-start.1 = (bf16[64,64]{1,0:T(8,128)(2,1)S(1)}, bf16[64,64]{1,0:T(8,128)(2,1)}, u32[]{:S(2)}) copy-start(bf16[64,64]{1,0:T(8,128)(2,1)} %param.8) | copy-start | bytes 24580
  2.4 17.7 %collective-permute-start.1 = (bf16[2,32,16,128]{3,2,1,0:T(8,128)(2,1)S(1)}, bf16[2,32,16,128]{3,2,1,0:T(8,128)(2,1)S(1)}, u32[]{:S(2)}, u32[]{:S(2)}) collective-permute-start(bf16[2,32,16,128]{3,2,1,0:T(8,128)(2,1)S(1)} %get-tuple-element.109), channel_id=1, source_target_pairs={{0,1},{1,0},{8,16},{9,17},{16,8},{17,9},{24,25},{25,24},{2,3},{3,2... | collective-permute-start | bytes 786440 | tf_op jit(solution)/shard_map/ppermute | solution.py:442
  2.9 17.2 %collective-permute-start = (bf16[2,32,16,128]{3,2,1,0:T(8,128)(2,1)S(1)}, bf16[2,32,16,128]{3,2,1,0:T(8,128)(2,1)S(1)}, u32[]{:S(2)}, u32[]{:S(2)}) collective-permute-start(bf16[2,32,16,128]{3,2,1,0:T(8,128)(2,1)S(1)} %get-tuple-element.110), channel_id=1, source_target_pairs={{0,8},{1,9},{8,0},{9,1},{16,24},{17,25},{24,16},{25,17},{2,10},{3,... | collective-permute-start | bytes 786440 | tf_op jit(solution)/shard_map/ppermute | solution.py:442
  6.9 13.3 %collective-permute-start.3 = (bf16[2,32,16,128]{3,2,1,0:T(8,128)(2,1)S(1)}, bf16[2,32,16,128]{3,2,1,0:T(8,128)(2,1)S(1)}, u32[]{:S(2)}, u32[]{:S(2)}) collective-permute-start(bf16[2,32,16,128]{3,2,1,0:T(8,128)(2,1)S(1)} %get-tuple-element.105), channel_id=1, source_target_pairs={{0,1},{1,0},{2,4},{3,5},{4,2},{5,3},{6,7},{7,6},{8,9},{9,8},{10,12... | collective-permute-start | bytes 786440 | tf_op jit(solution)/shard_map/ppermute | solution.py:442
  7.0 13.2 %collective-permute-start.2 = (bf16[2,32,16,128]{3,2,1,0:T(8,128)(2,1)S(1)}, bf16[2,32,16,128]{3,2,1,0:T(8,128)(2,1)S(1)}, u32[]{:S(2)}, u32[]{:S(2)}) collective-permute-start(bf16[2,32,16,128]{3,2,1,0:T(8,128)(2,1)S(1)} %get-tuple-element.106), channel_id=1, source_target_pairs={{0,2},{1,3},{2,0},{3,1},{4,6},{5,7},{6,4},{7,5},{8,10},{9,11},{10,... | collective-permute-start | bytes 786440 | tf_op jit(solution)/shard_map/ppermute | solution.py:442
  21.3 6.5 %collective-permute-start.5 = (bf16[32,16,128]{2,1,0:T(8,128)(2,1)S(1)}, bf16[32,16,128]{2,1,0:T(8,128)(2,1)S(1)}, u32[]{:S(2)}, u32[]{:S(2)}) collective-permute-start(bf16[32,16,128]{2,1,0:T(8,128)(2,1)S(1)} %get-tuple-element.133), channel_id=1, source_target_pairs={{0,1},{1,0},{8,16},{9,17},{16,8},{17,9},{24,25},{25,24},{2,3},{3,2... | collective-permute-start | bytes 393224 | tf_op jit(solution)/shard_map/ppermute | solution.py:442
  21.3 7.3 %collective-permute-start.4 = (bf16[32,16,128]{2,1,0:T(8,128)(2,1)S(1)}, bf16[32,16,128]{2,1,0:T(8,128)(2,1)S(1)}, u32[]{:S(2)}, u32[]{:S(2)}) collective-permute-start(bf16[32,16,128]{2,1,0:T(8,128)(2,1)S(1)} %get-tuple-element.134), channel_id=1, source_target_pairs={{0,8},{1,9},{8,0},{9,1},{16,24},{17,25},{24,16},{25,17},{2,10},{3,... | collective-permute-start | bytes 393224 | tf_op jit(solution)/shard_map/ppermute | solution.py:442
  22.9 5.8 %collective-permute-start.7 = (bf16[32,16,128]{2,1,0:T(8,128)(2,1)S(1)}, bf16[32,16,128]{2,1,0:T(8,128)(2,1)S(1)}, u32[]{:S(2)}, u32[]{:S(2)}) collective-permute-start(bf16[32,16,128]{2,1,0:T(8,128)(2,1)S(1)} %get-tuple-element.129), channel_id=1, source_target_pairs={{0,1},{1,0},{2,4},{3,5},{4,2},{5,3},{6,7},{7,6},{8,9},{9,8},{10,12... | collective-permute-start | bytes 393224 | tf_op jit(solution)/shard_map/ppermute | solution.py:442
  23.0 5.9 %collective-permute-start.6 = (bf16[32,16,128]{2,1,0:T(8,128)(2,1)S(1)}, bf16[32,16,128]{2,1,0:T(8,128)(2,1)S(1)}, u32[]{:S(2)}, u32[]{:S(2)}) collective-permute-start(bf16[32,16,128]{2,1,0:T(8,128)(2,1)S(1)} %get-tuple-element.130), channel_id=1, source_target_pairs={{0,2},{1,3},{2,0},{3,1},{4,6},{5,7},{6,4},{7,5},{8,10},{9,11},{10,... | collective-permute-start | bytes 393224 | tf_op jit(solution)/shard_map/ppermute | solution.py:442
  29.6 8.4 %collective-permute-start.9 = (bf16[32,16,128]{2,1,0:T(8,128)(2,1)S(1)}, bf16[32,16,128]{2,1,0:T(8,128)(2,1)S(1)}, u32[]{:S(2)}, u32[]{:S(2)}) collective-permute-start(bf16[32,16,128]{2,1,0:T(8,128)(2,1)S(1)} %get-tuple-element.125), channel_id=1, source_target_pairs={{0,1},{1,0},{8,16},{9,17},{16,8},{17,9},{24,25},{25,24},{2,3},{3,2... | collective-permute-start | bytes 393224 | tf_op jit(solution)/shard_map/ppermute | solution.py:442
  29.7 8.3 %collective-permute-start.8 = (bf16[32,16,128]{2,1,0:T(8,128)(2,1)S(1)}, bf16[32,16,128]{2,1,0:T(8,128)(2,1)S(1)}, u32[]{:S(2)}, u32[]{:S(2)}) collective-permute-start(bf16[32,16,128]{2,1,0:T(8,128)(2,1)S(1)} %get-tuple-element.126), channel_id=1, source_target_pairs={{0,8},{1,9},{8,0},{9,1},{16,24},{17,25},{24,16},{25,17},{2,10},{3,... | collective-permute-start | bytes 393224 | tf_op jit(solution)/shard_map/ppermute | solution.py:442
  31.7 6.4 %collective-permute-start.11 = (bf16[32,16,128]{2,1,0:T(8,128)(2,1)S(1)}, bf16[32,16,128]{2,1,0:T(8,128)(2,1)S(1)}, u32[]{:S(2)}, u32[]{:S(2)}) collective-permute-start(bf16[32,16,128]{2,1,0:T(8,128)(2,1)S(1)} %get-tuple-element.121), channel_id=1, source_target_pairs={{0,1},{1,0},{2,4},{3,5},{4,2},{5,3},{6,7},{7,6},{8,9},{9,8},{10,12... | collective-permute-start | bytes 393224 | tf_op jit(solution)/shard_map/ppermute | solution.py:442
  31.8 6.3 %collective-permute-start.10 = (bf16[32,16,128]{2,1,0:T(8,128)(2,1)S(1)}, bf16[32,16,128]{2,1,0:T(8,128)(2,1)S(1)}, u32[]{:S(2)}, u32[]{:S(2)}) collective-permute-start(bf16[32,16,128]{2,1,0:T(8,128)(2,1)S(1)} %get-tuple-element.122), channel_id=1, source_target_pairs={{0,2},{1,3},{2,0},{3,1},{4,6},{5,7},{6,4},{7,5},{8,10},{9,11},{10,... | collective-permute-start | bytes 393224 | tf_op jit(solution)/shard_map/ppermute | solution.py:442
  38.8 8.1 %collective-permute-start.13 = (bf16[32,16,128]{2,1,0:T(8,128)(2,1)S(1)}, bf16[32,16,128]{2,1,0:T(8,128)(2,1)S(1)}, u32[]{:S(2)}, u32[]{:S(2)}) collective-permute-start(bf16[32,16,128]{2,1,0:T(8,128)(2,1)S(1)} %get-tuple-element.117), channel_id=1, source_target_pairs={{0,1},{1,0},{8,16},{9,17},{16,8},{17,9},{24,25},{25,24},{2,3},{3,2... | collective-permute-start | bytes 393224 | tf_op jit(solution)/shard_map/ppermute | solution.py:442
  38.9 8.0 %collective-permute-start.12 = (bf16[32,16,128]{2,1,0:T(8,128)(2,1)S(1)}, bf16[32,16,128]{2,1,0:T(8,128)(2,1)S(1)}, u32[]{:S(2)}, u32[]{:S(2)}) collective-permute-start(bf16[32,16,128]{2,1,0:T(8,128)(2,1)S(1)} %get-tuple-element.118), channel_id=1, source_target_pairs={{0,8},{1,9},{8,0},{9,1},{16,24},{17,25},{24,16},{25,17},{2,10},{3,... | collective-permute-start | bytes 393224 | tf_op jit(solution)/shard_map/ppermute | solution.py:442
  41.0 5.9 %collective-permute-start.15 = (bf16[32,16,128]{2,1,0:T(8,128)(2,1)S(1)}, bf16[32,16,128]{2,1,0:T(8,128)(2,1)S(1)}, u32[]{:S(2)}, u32[]{:S(2)}) collective-permute-start(bf16[32,16,128]{2,1,0:T(8,128)(2,1)S(1)} %get-tuple-element.113), channel_id=1, source_target_pairs={{0,1},{1,0},{2,4},{3,5},{4,2},{5,3},{6,7},{7,6},{8,9},{9,8},{10,12... | collective-permute-start | bytes 393224 | tf_op jit(solution)/shard_map/ppermute | solution.py:442
  41.1 5.9 %collective-permute-start.14 = (bf16[32,16,128]{2,1,0:T(8,128)(2,1)S(1)}, bf16[32,16,128]{2,1,0:T(8,128)(2,1)S(1)}, u32[]{:S(2)}, u32[]{:S(2)}) collective-permute-start(bf16[32,16,128]{2,1,0:T(8,128)(2,1)S(1)} %get-tuple-element.114), channel_id=1, source_target_pairs={{0,2},{1,3},{2,0},{3,1},{4,6},{5,7},{6,4},{7,5},{8,10},{9,11},{10,... | collective-permute-start | bytes 393224 | tf_op jit(solution)/shard_map/ppermute | solution.py:442
  48.4 10.4 %collective-permute-start.16 = (bf16[16,2,256,128]{3,2,1,0:T(8,128)(2,1)S(1)}, bf16[16,2,256,128]{3,2,1,0:T(8,128)(2,1)S(1)}, u32[]{:S(2)}, u32[]{:S(2)}) collective-permute-start(bf16[16,2,256,128]{3,2,1,0:T(8,128)(2,1)S(1)} %get-tuple-element.96.own_ref), channel_id=1, source_target_pairs={{0,1},{1,0},{2,3},{3,2},{4,5},{5,4},{6,7},{7,6},{8,9},{9,8},{10,11... | collective-permute-start | bytes 6291464 | tf_op jit(solution)/shard_map/ppermute | solution.py:590
  48.5 4.7 %collective-permute-start.19 = (f32[32,64]{1,0:T(8,128)S(1)}, f32[32,64]{1,0:T(8,128)S(1)}, u32[]{:S(2)}, u32[]{:S(2)}) collective-permute-start(f32[32,64]{1,0:T(8,128)S(1)} %get-tuple-element.101.refs_0_), channel_id=1, source_target_pairs={{0,24},{8,16},{16,8},{24,0},{1,25},{9,17},{17,9},{25,1},{2,26},{10... | collective-permute-start | bytes 24584 | tf_op jit(solution)/shard_map/ppermute | solution.py:456
  50.1 3.7 %collective-permute-start.18 = (f32[32,64]{1,0:T(8,128)S(1)}, f32[32,64]{1,0:T(8,128)S(1)}, u32[]{:S(2)}, u32[]{:S(2)}) collective-permute-start(f32[32,64]{1,0:T(8,128)S(1)} %get-tuple-element.101.refs_0_), channel_id=1, source_target_pairs={{0,16},{8,24},{16,0},{24,8},{1,17},{9,25},{17,1},{25,9},{2,18},{10... | collective-permute-start | bytes 24584 | tf_op jit(solution)/shard_map/ppermute | solution.py:456
  50.7 3.7 %collective-permute-start.17 = (f32[32,64]{1,0:T(8,128)S(1)}, f32[32,64]{1,0:T(8,128)S(1)}, u32[]{:S(2)}, u32[]{:S(2)}) collective-permute-start(f32[32,64]{1,0:T(8,128)S(1)} %get-tuple-element.101.refs_0_), channel_id=1, source_target_pairs={{0,8},{8,0},{16,24},{24,16},{1,9},{9,1},{17,25},{25,17},{2,10},{10... | collective-permute-start | bytes 24584 | tf_op jit(solution)/shard_map/ppermute | solution.py:456
  54.4 6.7 %collective-permute-start.22 = (f32[32,64]{1,0:T(8,128)S(1)}, f32[32,64]{1,0:T(8,128)S(1)}, u32[]{:S(2)}, u32[]{:S(2)}) collective-permute-start(f32[32,64]{1,0:T(8,128)S(1)} %line_sum.1), channel_id=1, source_target_pairs={{0,6},{2,4},{4,2},{6,0},{1,7},{3,5},{5,3},{7,1},{8,14},{10,12},{12... | collective-permute-start | bytes 24584 | tf_op jit(solution)/shard_map/ppermute | solution.py:456
  56.3 4.8 %collective-permute-start.21 = (f32[32,64]{1,0:T(8,128)S(1)}, f32[32,64]{1,0:T(8,128)S(1)}, u32[]{:S(2)}, u32[]{:S(2)}) collective-permute-start(f32[32,64]{1,0:T(8,128)S(1)} %line_sum.1), channel_id=1, source_target_pairs={{0,4},{2,6},{4,0},{6,2},{1,5},{3,7},{5,1},{7,3},{8,12},{10,14},{12... | collective-permute-start | bytes 24584 | tf_op jit(solution)/shard_map/ppermute | solution.py:456
  56.4 4.7 %collective-permute-start.20 = (f32[32,64]{1,0:T(8,128)S(1)}, f32[32,64]{1,0:T(8,128)S(1)}, u32[]{:S(2)}, u32[]{:S(2)}) collective-permute-start(f32[32,64]{1,0:T(8,128)S(1)} %line_sum.1), channel_id=1, source_target_pairs={{0,2},{2,0},{4,6},{6,4},{1,3},{3,1},{5,7},{7,5},{8,10},{10,8},{12,... | collective-permute-start | bytes 24584 | tf_op jit(solution)/shard_map/ppermute | solution.py:456
  58.9 2.2 %copy-start = (f32[64,32]{0,1:T(8,128)S(1)}, f32[64,32]{0,1:T(8,128)}, u32[]{:S(2)}) copy-start(f32[64,32]{0,1:T(8,128)} %param.11) | copy-start | bytes 24580

commit v6 on v5

--- a/solution.py
+++ b/solution.py
@@ -207,11 +207,11 @@
         ux[s] = w_ref[s, nx - 1].astype(BF)
 
     def body(i, carry):
-        for j in range(4):
-            one(i * 4 + j)
+        for j in range(16):
+            one(i * 16 + j)
         return carry
 
-    lax.fori_loop(0, samples // 4, body, 0)
+    lax.fori_loop(0, samples // 16, body, 0)
 
 
 def split_shape(shape):
@@ -362,7 +362,7 @@
 def finish_kernel(w_in, u_ref, cx0, cx1, cy0, cy1, hx0, hx1, hy0, hy1, *refs):
     del w_in
     ends, (main_ref, px, py) = refs[:2], refs[2:5]
-    w_ref, out_ref, snap_ref, xbuf, ybuf = refs[-5:]
+    w_ref, out_ref, xbuf, ybuf = refs[-4:]
     samples, nx, ny, nz = u_ref.shape
     w_rows = flat(w_ref)
 
@@ -379,11 +379,11 @@
             w_rows[line, :] = w_rows[line, :] + flux
 
     def patch(i, carry):
-        for j in range(4):
-            one(i * 4 + j)
+        for j in range(16):
+            one(i * 16 + j)
         return carry
 
-    lax.fori_loop(0, samples // 4, patch, 0)
+    lax.fori_loop(0, samples // 16, patch, 0)
     total = main_ref[...]
     for buf, psi in ((xbuf, px), (ybuf, py)):
         count = buf.shape[2]
@@ -397,11 +397,15 @@
             total = total + contract(jnp.concatenate(left, axis=1), jnp.concatenate(right, axis=1))
     out_ref[...] = total
 
+
+def snapshot_kernel(u_ref, *refs):
+    snap_ref = refs[-1]
+
     def body(x, carry):
-        split_into(snap_ref, x, w_ref[:, x])
+        split_into(snap_ref, x, u_ref[:, x])
         return carry
 
-    lax.fori_loop(0, nx, body, 0)
+    lax.fori_loop(0, u_ref.shape[1], body, 0)
 
 
 def sum_kernel(*refs):
@@ -577,9 +581,9 @@
         flops=2 * ranks * ROWS * cells,
         nbytes=4 * cells,
     )(held_psi, moved, *written)
-    final, partial_sum, snapshot = vmem_call(
+    final, partial_sum = vmem_call(
         finish_kernel,
-        [(block, F32), ((samples, ranks), F32), (split_shape(block), BF)],
+        [(block, F32), ((samples, ranks), F32)],
         "finish",
         scratch=[pltpu.VMEM((2,) + x_face, F32), pltpu.VMEM((2,) + y_face, F32)],
         aliases={0: 0},
@@ -587,6 +591,12 @@
         nbytes=2 * cells,
     )(moved, state, *face_coefs, *halos, *lines, main, psi_x, psi_y, prev, weights)
     first_sums = received(partial_sum, "sx")
+    line_sum = vmem_call(
+        sum_kernel, [((samples, ranks), F32)], "line_sum", flops=SUM_COST, nbytes=SUM_COST
+    )(partial_sum, *first_sums)[0]
+    snapshot = vmem_call(
+        snapshot_kernel, [(split_shape(block), BF)], "snapshot", flops=cells, nbytes=2 * cells
+    )(final, prev, weights)[0]
     other = lax.ppermute(snapshot, "par", [(i, (i + 1) % par_size) for i in range(par_size)])
     range_sketch, final_state, done = vmem_call(
         range_kernel,
@@ -600,9 +610,6 @@
         flops=2 * ranks * ROWS * cells,
         nbytes=4 * cells,
     )(weights, snapshot, other, prev, final, written)
-    line_sum = vmem_call(
-        sum_kernel, [((samples, ranks), F32)], "line_sum", flops=SUM_COST, nbytes=SUM_COST
-    )(partial_sum, *first_sums)[0]
     corange = sum(received(line_sum, "sy"), corange_prev.T + line_sum) + done
     return final_state, range_sketch, corange.T
 

time: 61.9 us -> 61.7 us (level)
    pallas_call x14 -> x15, Pallas kernels: 29.5 us -> 29.3 us  [call(): pl.pallas_call(kernel, out_shape=out_shape, in_specs=in_specs, out_specs=...]
where the time goes in v6:
time: 61.7 us; the launch traced here: 61.6 us
  Pallas kernels  29.3 us (47%)
  starting transfers between devices  26.1 us (42%)
  waiting for transfers between devices  3.56 us (6%)
  other arithmetic  1.21 us (2%)
  between operations  1.09 us (2%)
    pallas_call x15, Pallas kernels, call(): pl.pallas_call(kernel, out_shape=out_shape, in_specs=in_specs, out_specs=...  29.3 us
    ppermute x16, starting transfers between devices, exchange(): got[axis, parity] = lax.ppermute(mine, (axis, 'par'), pairs)  18 us
    ppermute x6, starting transfers between devices, received(): lax.ppermute(value, axis, [(i, i ^ shift) for i in range(count)])  8 us
    ppermute x6, waiting for transfers between devices, received(): lax.ppermute(value, axis, [(i, i ^ shift) for i in range(count)])  2.36 us
  transfers between devices with their start and end apart: 23, of which 6 were waited for; matrix products, arithmetic and copies ran while one was open for 1% of the time, Pallas kernels for 40%

profile of v6, /device:TPU:0, one launch (start us, length us, event | category | flops | bytes accessed | tf_op | source)
XLA Modules:
  0.0 61.6 jit_solution(4244040591060381761)
XLA Ops:
  0.7 1.7 %faces.1 = (bf16[2,32,16,128]{3,2,1,0:T(8,128)(2,1)S(1)}, bf16[2,32,16,128]{3,2,1,0:T(8,128)(2,1)S(1)}, bf16[2,32,16,128]{3,2,1,0:T(8,128)(2,1)S(1)}, bf16[2,32,16,128]{3,2,1,0:T(8,128)(2,1)S(1)}) custom-call(f32[32,16,16,128]{3,2,1,0:T(8,128)} %u_ref.1, f32[32,16,16,128]{3,2,1,0:T(8,128)} %k_ref.1), custom_call_target="tpu_custom_call" | custom-call | flops 524288 | bytes 1048576 | tf_op jit(solution)/shard_map/faces/pallas_call | solution.py:35
  2.4 0.5 collective-permute-start.1
  2.9 4.0 %collective-permute-start = (bf16[2,32,16,128]{3,2,1,0:T(8,128)(2,1)S(1)}, bf16[2,32,16,128]{3,2,1,0:T(8,128)(2,1)S(1)}, u32[]{:S(2)}, u32[]{:S(2)}) collective-permute-start(bf16[2,32,16,128]{3,2,1,0:T(8,128)(2,1)S(1)} %get-tuple-element.108), channel_id=1, source_target_pairs={{0,8},{1,9},{8,0},{9,1},{16,24},{17,25},{24,16},{25,17},{2,10},{3,... | collective-permute-start | bytes 786440 | tf_op jit(solution)/shard_map/ppermute | solution.py:446
  6.9 0.1 collective-permute-start.3
  7.0 3.1 %collective-permute-start.2 = (bf16[2,32,16,128]{3,2,1,0:T(8,128)(2,1)S(1)}, bf16[2,32,16,128]{3,2,1,0:T(8,128)(2,1)S(1)}, u32[]{:S(2)}, u32[]{:S(2)}) collective-permute-start(bf16[2,32,16,128]{3,2,1,0:T(8,128)(2,1)S(1)} %get-tuple-element.104), channel_id=1, source_target_pairs={{0,2},{1,3},{2,0},{3,1},{4,6},{5,7},{6,4},{7,5},{8,10},{9,11},{10,... | collective-permute-start | bytes 786440 | tf_op jit(solution)/shard_map/ppermute | solution.py:446
  10.1 0.1 fusion.5
  10.2 0.1 copy.17
  10.3 0.1 copy.18
  10.4 3.0 %psi.1 = (bf16[16,2,512,128]{3,2,1,0:T(8,128)(2,1)S(1)}, bf16[2,16,64,128]{3,2,1,0:T(8,128)(2,1)S(1)}) custom-call(bf16[64,16,16,128]{3,2,1,0:T(8,128)(2,1)} %psi_hbm.3), custom_call_target="tpu_custom_call" | custom-call | flops 4194304 | bytes 4194304 | tf_op jit(solution)/shard_map/psi/pallas_call | solution.py:35
  13.4 6.7 %first.1 = (f32[32,16,16,128]{3,2,1,0:T(8,128)S(1)}, f32[32,16,16,128]{3,2,1,0:T(8,128)S(1)}, f32[32,16,16,128]{3,2,1,0:T(8,128)S(1)}, f32[32,16,16,128]{3,2,1,0...) custom-call(f32[32,16,16,128]{3,2,1,0:T(8,128)} %u_ref.1, ...), custom_call_target="tpu_custom_call" | custom-call | flops 37748736 | bytes 16777216 | tf_op jit(solution)/shard_map/first/pallas_call | solution.py:35
  20.3 0.1 bitcast_add_fusion.2
  20.4 0.7 %edge.3 = (f32[32,16,16,128]{3,2,1,0:T(8,128)S(1)}, bf16[32,16,128]{2,1,0:T(8,128)(2,1)S(1)}, bf16[32,16,128]{2,1,0:T(8,128)(2,1)S(1)}, bf16[32,16,128]{2,1,0:T(...) custom-call(f32[32,16,16,128]{3,2,1,0:T(8,128)S(1)} %get-tuple-eleme, ...), custom_call_target="tpu_custom_call", output_to_operand_aliasing={{0}: (0, {})} | custom-call | flops 1048576 | bytes 1048576 | tf_op jit(solution)/shard_map/edge/pallas_call | solution.py:35
  21.2 0.1 collective-permute-start.5
  21.3 1.6 %collective-permute-start.4 = (bf16[32,16,128]{2,1,0:T(8,128)(2,1)S(1)}, bf16[32,16,128]{2,1,0:T(8,128)(2,1)S(1)}, u32[]{:S(2)}, u32[]{:S(2)}) collective-permute-start(bf16[32,16,128]{2,1,0:T(8,128)(2,1)S(1)} %get-tuple-element.132), channel_id=1, source_target_pairs={{0,8},{1,9},{8,0},{9,1},{16,24},{17,25},{24,16},{25,17},{2,10},{3,... | collective-permute-start | bytes 393224 | tf_op jit(solution)/shard_map/ppermute | solution.py:446
  22.8 0.1 collective-permute-start.7
  22.9 1.7 %collective-permute-start.6 = (bf16[32,16,128]{2,1,0:T(8,128)(2,1)S(1)}, bf16[32,16,128]{2,1,0:T(8,128)(2,1)S(1)}, u32[]{:S(2)}, u32[]{:S(2)}) collective-permute-start(bf16[32,16,128]{2,1,0:T(8,128)(2,1)S(1)} %get-tuple-element.128), channel_id=1, source_target_pairs={{0,2},{1,3},{2,0},{3,1},{4,6},{5,7},{6,4},{7,5},{8,10},{9,11},{10,... | collective-permute-start | bytes 393224 | tf_op jit(solution)/shard_map/ppermute | solution.py:446
  24.7 3.0 %step.3.w_in = f32[32,16,16,128]{3,2,1,0:T(8,128)S(1)} custom-call(f32[32,16,16,128]{3,2,1,0:T(8,128)S(1)} %get-tuple-element.64.u_ref, f32[32,16,16,128]{3,2,1,0:T(8,128)S(1)} %get-tuple-element.65.cx_ref, f32[32,16,16,128]{3,2,1,0:T(8,128)S(1)} %get-tuple-element.66.cy_ref, f32[32,16,16,128]{3,2,1,0:T(8,128)S(1)} %get-tuple-element.67.cup_ref, ...), custom_call_target="tpu_custom_call" | custom-call | flops 25165824 | bytes 8388608 | tf_op jit(solution)/shard_map/step/pallas_call | solution.py:35
  27.7 0.9 %collective-permute-done.4 = bf16[32,16,128]{2,1,0:T(8,128)(2,1)S(1)} collective-permute-done((bf16[32,16,128]{2,1,0:T(8,128)(2,1)S(1)}, bf16[32,16,128]{2,1,0:T(8,128)(2,1)S(1)}, u32[]{:S(2)}, u32[]{:S(2)}) %collective-permute-start.4) | collective-permute-done | bytes 131104 | tf_op jit(solution)/shard_map/ppermute | solution.py:446
  28.6 0.2 collective-permute-done.6
  28.9 0.6 edge.4
  29.5 0.1 collective-permute-start.9
  29.6 1.9 %collective-permute-start.8 = (bf16[32,16,128]{2,1,0:T(8,128)(2,1)S(1)}, bf16[32,16,128]{2,1,0:T(8,128)(2,1)S(1)}, u32[]{:S(2)}, u32[]{:S(2)}) collective-permute-start(bf16[32,16,128]{2,1,0:T(8,128)(2,1)S(1)} %get-tuple-element.124), channel_id=1, source_target_pairs={{0,8},{1,9},{8,0},{9,1},{16,24},{17,25},{24,16},{25,17},{2,10},{3,... | collective-permute-start | bytes 393224 | tf_op jit(solution)/shard_map/ppermute | solution.py:446
  31.6 0.1 collective-permute-start.11
  31.6 1.4 %collective-permute-start.10 = (bf16[32,16,128]{2,1,0:T(8,128)(2,1)S(1)}, bf16[32,16,128]{2,1,0:T(8,128)(2,1)S(1)}, u32[]{:S(2)}, u32[]{:S(2)}) collective-permute-start(bf16[32,16,128]{2,1,0:T(8,128)(2,1)S(1)} %get-tuple-element.120), channel_id=1, source_target_pairs={{0,2},{1,3},{2,0},{3,1},{4,6},{5,7},{6,4},{7,5},{8,10},{9,11},{10,... | collective-permute-start | bytes 393224 | tf_op jit(solution)/shard_map/ppermute | solution.py:446
  33.0 3.0 %step.4.after.w_in = f32[32,16,16,128]{3,2,1,0:T(8,128)S(1)} custom-call(f32[32,16,16,128]{3,2,1,0:T(8,128)S(1)} %get-tuple-element.75.u_ref, f32[32,16,16,128]{3,2,1,0:T(8,128)S(1)} %get-tuple-element.65.cx_ref, f32[32,16,16,128]{3,2,1,0:T(8,128)S(1)} %get-tuple-element.66.cy_ref, f32[32,16,16,128]{3,2,1,0:T(8,128)S(1)} %get-tuple-element.67.cup_ref, ...), custom_call_target="tpu_custom_call" | custom-call | flops 25165824 | bytes 8388608 | tf_op jit(solution)/shard_map/step/pallas_call | solution.py:35
  36.1 1.8 %lines.1 = (bf16[2,16,64,128]{3,2,1,0:T(8,128)(2,1)S(1)}, bf16[2,256,256]{2,1,0:T(8,128)(2,1)S(1)}, bf16[32,16,16,128]{3,2,1,0:T(8,128)(2,1)S(1)}) custom-call(bf16[64,16,16,128]{3,2,1,0:T(8,128)(2,1)} %psi_hbm.3, bf16[32,16,16,128]{3,2,1,0:T(8,128)(2,1)} %prev_hbm.1, bf16[2,32,32]{2,1,0:T(8,128)(2,1)S(1)} %pad_maximum_fusion.omega_ref, ...), custom_call_target="tpu_custom_call" | custom-call | flops 1048576 | bytes 1048576 | tf_op jit(solution)/shard_map/lines/pallas_call | solution.py:35
  38.0 0.6 edge.5
  38.6 0.1 collective-permute-start.13
  38.7 2.2 %collective-permute-start.12 = (bf16[32,16,128]{2,1,0:T(8,128)(2,1)S(1)}, bf16[32,16,128]{2,1,0:T(8,128)(2,1)S(1)}, u32[]{:S(2)}, u32[]{:S(2)}) collective-permute-start(bf16[32,16,128]{2,1,0:T(8,128)(2,1)S(1)} %get-tuple-element.116), channel_id=1, source_target_pairs={{0,8},{1,9},{8,0},{9,1},{16,24},{17,25},{24,16},{25,17},{2,10},{3,... | collective-permute-start | bytes 393224 | tf_op jit(solution)/shard_map/ppermute | solution.py:446
  40.9 0.1 collective-permute-start.15
  41.0 1.1 %collective-permute-start.14 = (bf16[32,16,128]{2,1,0:T(8,128)(2,1)S(1)}, bf16[32,16,128]{2,1,0:T(8,128)(2,1)S(1)}, u32[]{:S(2)}, u32[]{:S(2)}) collective-permute-start(bf16[32,16,128]{2,1,0:T(8,128)(2,1)S(1)} %get-tuple-element.112), channel_id=1, source_target_pairs={{0,2},{1,3},{2,0},{3,1},{4,6},{5,7},{6,4},{7,5},{8,10},{9,11},{10,... | collective-permute-start | bytes 393224 | tf_op jit(solution)/shard_map/ppermute | solution.py:446
  42.1 3.1 %step.5 = (f32[32,16,16,128]{3,2,1,0:T(8,128)S(1)}, f32[32,16,16,128]{3,2,1,0:T(8,128)}) custom-call(f32[32,16,16,128]{3,2,1,0:T(8,128)S(1)} %get-tuple-element.85.u_ref, f32[32,16,16,128]{3,2,1,0:T(8,128)S(1)} %get-tuple-element.65.cx_ref, f32[32,16,16,128]{3,2,1,0:T(8,128)S(1)} %get-tuple-element.66.cy_ref, ...), custom_call_target="tpu_custom_call" | custom-call | flops 25165824 | bytes 8388608 | tf_op jit(solution)/shard_map/step/pallas_call | solution.py:35
  45.1 1.6 %corange.1 = (f32[32,64]{1,0:T(8,128)S(1)}, f32[32,16,16,128]{3,2,1,0:T(8,128)}) custom-call(bf16[16,2,512,128]{3,2,1,0:T(8,128)(2,1)S(1)} %get-tuple-element.62.refs_8_.refs_0_.refs_10_.psi_ref, f32[32,16,16,128]{3,2,1,0:T(8,128)S(1)} %get-tuple-element.86.u_ref.w_in, f32[32,16,16,128]{3,2,1,0:T(8,128)} %get-tuple-element.93.state_in), custom_call_target="tpu_custom_call", output_to_operand_aliasing={{1}: (2, {})} | custom-call | flops 1073741824 | bytes 4194304 | tf_op jit(solution)/shard_map/corange/pallas_call | solution.py:35
  46.8 0.1 collective-permute-done.14
  46.9 1.0 %finish.1 = (f32[32,16,16,128]{3,2,1,0:T(8,128)S(1)}, f32[32,64]{1,0:T(8,128)S(1)}) custom-call(f32[32,16,16,128]{3,2,1,0:T(8,128)S(1)} %get-tuple-element.86.u_ref.w_in, f32[32,16,16,128]{3,2,1,0:T(8,128)S(1)} %get-tuple-element.85.u_ref, f32[32,16,128]{2,1,0:T(8,128)S(1)} %get-tuple-element.138.refs_0_.cx0, ...), custom_call_target="tpu_custom_call", output_to_operand_aliasing={{0}: (0, {})} | custom-call | flops 1048576 | bytes 2097152 | tf_op jit(solution)/shard_map/finish/pallas_call | solution.py:35
  47.9 0.3 snapshot.1.own_ref
  48.2 0.1 collective-permute-start.16
  48.3 1.6 %collective-permute-start.19 = (f32[32,64]{1,0:T(8,128)S(1)}, f32[32,64]{1,0:T(8,128)S(1)}, u32[]{:S(2)}, u32[]{:S(2)}) collective-permute-start(f32[32,64]{1,0:T(8,128)S(1)} %get-tuple-element.99.refs_0_), channel_id=1, source_target_pairs={{0,24},{8,16},{16,8},{24,0},{1,25},{9,17},{17,9},{25,1},{2,26},{10... | collective-permute-start | bytes 24584 | tf_op jit(solution)/shard_map/ppermute | solution.py:460
  49.9 0.6 collective-permute-start.18
  50.5 1.4 %collective-permute-start.17 = (f32[32,64]{1,0:T(8,128)S(1)}, f32[32,64]{1,0:T(8,128)S(1)}, u32[]{:S(2)}, u32[]{:S(2)}) collective-permute-start(f32[32,64]{1,0:T(8,128)S(1)} %get-tuple-element.99.refs_0_), channel_id=1, source_target_pairs={{0,8},{8,0},{16,24},{24,16},{1,9},{9,1},{17,25},{25,17},{2,10},{10... | collective-permute-start | bytes 24584 | tf_op jit(solution)/shard_map/ppermute | solution.py:460
  51.9 1.2 %collective-permute-done.19.refs_3_ = f32[32,64]{1,0:T(8,128)S(1)} collective-permute-done((f32[32,64]{1,0:T(8,128)S(1)}, f32[32,64]{1,0:T(8,128)S(1)}, u32[]{:S(2)}, u32[]{:S(2)}) %collective-permute-start.19) | collective-permute-done | bytes 8224 | tf_op jit(solution)/shard_map/ppermute | solution.py:460
  53.0 0.6 %collective-permute-done.18.refs_2_ = f32[32,64]{1,0:T(8,128)S(1)} collective-permute-done((f32[32,64]{1,0:T(8,128)S(1)}, f32[32,64]{1,0:T(8,128)S(1)}, u32[]{:S(2)}, u32[]{:S(2)}) %collective-permute-start.18) | collective-permute-done | bytes 8224 | tf_op jit(solution)/shard_map/ppermute | solution.py:460
  53.7 0.6 collective-permute-done.17.refs_1_
  54.2 1.9 %collective-permute-start.22 = (f32[32,64]{1,0:T(8,128)S(1)}, f32[32,64]{1,0:T(8,128)S(1)}, u32[]{:S(2)}, u32[]{:S(2)}) collective-permute-start(f32[32,64]{1,0:T(8,128)S(1)} %line_sum.1), channel_id=1, source_target_pairs={{0,6},{2,4},{4,2},{6,0},{1,7},{3,5},{5,3},{7,1},{8,14},{10,12},{12... | collective-permute-start | bytes 24584 | tf_op jit(solution)/shard_map/ppermute | solution.py:460
  56.1 0.1 collective-permute-start.21
  56.2 2.5 %collective-permute-start.20 = (f32[32,64]{1,0:T(8,128)S(1)}, f32[32,64]{1,0:T(8,128)S(1)}, u32[]{:S(2)}, u32[]{:S(2)}) collective-permute-start(f32[32,64]{1,0:T(8,128)S(1)} %line_sum.1), channel_id=1, source_target_pairs={{0,2},{2,0},{4,6},{6,4},{1,3},{3,1},{5,7},{7,5},{8,10},{10,8},{12,... | collective-permute-start | bytes 24584 | tf_op jit(solution)/shard_map/ppermute | solution.py:460
  58.7 2.2 %range.1 = (bf16[32,16,16,128]{3,2,1,0:T(8,128)(2,1)}, f32[32,16,16,128]{3,2,1,0:T(8,128)}, f32[32,64]{1,0:T(8,128)S(1)}) custom-call(bf16[2,256,256]{2,1,0:T(8,128)(2,1)S(1)} %get-tuple-element.76.refs_13_.refs_3_.refs_6_.refs_1_.weight_ref, bf16[16,2,256,128]{3,2,1,0:T(8,128)(2,1)S(1)} %snapshot.1.own_ref, ...), custom_call_target="tpu_custom_call", output_to_operand_aliasing={{1}: (5, {})} | custom-call | flops 1073741824 | bytes 4194304 | tf_op jit(solution)/shard_map/range/pallas_call | solution.py:35
  60.9 0.6 %fusion.4 = f32[64,32]{0,1:T(8,128)} fusion(f32[32,64]{1,0:T(8,128)S(1)} %get-tuple-element.100, f32[32,64]{1,0:T(8,128)S(1)} %collective-permute-done.22, f32[32,64]{1,0:T(8,128)S(1)} %collective-permute-done.21, f32[32,64]{1,0:T(8,128)S(1)} %collective-permute-done.20, f32[32,64]{1,0:T(8,128)S(1)} %line_sum.1, f32[64,32]{0,1:T(8,128)S(1)} %copy-done), kind=kLoop, calls=%fused_computation.46 | loop fusion | flops 10240 | bytes 57344 | tf_op jit(solution)/shard_map/transpose | solution.py:614
  (42 shorter events, 0.6 us)
Async XLA Ops:
  0.6 9.5 %copy-start.1 = (bf16[64,64]{1,0:T(8,128)(2,1)S(1)}, bf16[64,64]{1,0:T(8,128)(2,1)}, u32[]{:S(2)}) copy-start(bf16[64,64]{1,0:T(8,128)(2,1)} %param.8) | copy-start | bytes 24580
  2.4 17.7 %collective-permute-start.1 = (bf16[2,32,16,128]{3,2,1,0:T(8,128)(2,1)S(1)}, bf16[2,32,16,128]{3,2,1,0:T(8,128)(2,1)S(1)}, u32[]{:S(2)}, u32[]{:S(2)}) collective-permute-start(bf16[2,32,16,128]{3,2,1,0:T(8,128)(2,1)S(1)} %get-tuple-element.107), channel_id=1, source_target_pairs={{0,1},{1,0},{8,16},{9,17},{16,8},{17,9},{24,25},{25,24},{2,3},{3,2... | collective-permute-start | bytes 786440 | tf_op jit(solution)/shard_map/ppermute | solution.py:446
  2.9 17.2 %collective-permute-start = (bf16[2,32,16,128]{3,2,1,0:T(8,128)(2,1)S(1)}, bf16[2,32,16,128]{3,2,1,0:T(8,128)(2,1)S(1)}, u32[]{:S(2)}, u32[]{:S(2)}) collective-permute-start(bf16[2,32,16,128]{3,2,1,0:T(8,128)(2,1)S(1)} %get-tuple-element.108), channel_id=1, source_target_pairs={{0,8},{1,9},{8,0},{9,1},{16,24},{17,25},{24,16},{25,17},{2,10},{3,... | collective-permute-start | bytes 786440 | tf_op jit(solution)/shard_map/ppermute | solution.py:446
  6.9 13.3 %collective-permute-start.3 = (bf16[2,32,16,128]{3,2,1,0:T(8,128)(2,1)S(1)}, bf16[2,32,16,128]{3,2,1,0:T(8,128)(2,1)S(1)}, u32[]{:S(2)}, u32[]{:S(2)}) collective-permute-start(bf16[2,32,16,128]{3,2,1,0:T(8,128)(2,1)S(1)} %get-tuple-element.103), channel_id=1, source_target_pairs={{0,1},{1,0},{2,4},{3,5},{4,2},{5,3},{6,7},{7,6},{8,9},{9,8},{10,12... | collective-permute-start | bytes 786440 | tf_op jit(solution)/shard_map/ppermute | solution.py:446
  7.0 13.2 %collective-permute-start.2 = (bf16[2,32,16,128]{3,2,1,0:T(8,128)(2,1)S(1)}, bf16[2,32,16,128]{3,2,1,0:T(8,128)(2,1)S(1)}, u32[]{:S(2)}, u32[]{:S(2)}) collective-permute-start(bf16[2,32,16,128]{3,2,1,0:T(8,128)(2,1)S(1)} %get-tuple-element.104), channel_id=1, source_target_pairs={{0,2},{1,3},{2,0},{3,1},{4,6},{5,7},{6,4},{7,5},{8,10},{9,11},{10,... | collective-permute-start | bytes 786440 | tf_op jit(solution)/shard_map/ppermute | solution.py:446
  21.2 6.5 %collective-permute-start.5 = (bf16[32,16,128]{2,1,0:T(8,128)(2,1)S(1)}, bf16[32,16,128]{2,1,0:T(8,128)(2,1)S(1)}, u32[]{:S(2)}, u32[]{:S(2)}) collective-permute-start(bf16[32,16,128]{2,1,0:T(8,128)(2,1)S(1)} %get-tuple-element.131), channel_id=1, source_target_pairs={{0,1},{1,0},{8,16},{9,17},{16,8},{17,9},{24,25},{25,24},{2,3},{3,2... | collective-permute-start | bytes 393224 | tf_op jit(solution)/shard_map/ppermute | solution.py:446
  21.3 7.3 %collective-permute-start.4 = (bf16[32,16,128]{2,1,0:T(8,128)(2,1)S(1)}, bf16[32,16,128]{2,1,0:T(8,128)(2,1)S(1)}, u32[]{:S(2)}, u32[]{:S(2)}) collective-permute-start(bf16[32,16,128]{2,1,0:T(8,128)(2,1)S(1)} %get-tuple-element.132), channel_id=1, source_target_pairs={{0,8},{1,9},{8,0},{9,1},{16,24},{17,25},{24,16},{25,17},{2,10},{3,... | collective-permute-start | bytes 393224 | tf_op jit(solution)/shard_map/ppermute | solution.py:446
  22.8 5.8 %collective-permute-start.7 = (bf16[32,16,128]{2,1,0:T(8,128)(2,1)S(1)}, bf16[32,16,128]{2,1,0:T(8,128)(2,1)S(1)}, u32[]{:S(2)}, u32[]{:S(2)}) collective-permute-start(bf16[32,16,128]{2,1,0:T(8,128)(2,1)S(1)} %get-tuple-element.127), channel_id=1, source_target_pairs={{0,1},{1,0},{2,4},{3,5},{4,2},{5,3},{6,7},{7,6},{8,9},{9,8},{10,12... | collective-permute-start | bytes 393224 | tf_op jit(solution)/shard_map/ppermute | solution.py:446
  22.9 5.9 %collective-permute-start.6 = (bf16[32,16,128]{2,1,0:T(8,128)(2,1)S(1)}, bf16[32,16,128]{2,1,0:T(8,128)(2,1)S(1)}, u32[]{:S(2)}, u32[]{:S(2)}) collective-permute-start(bf16[32,16,128]{2,1,0:T(8,128)(2,1)S(1)} %get-tuple-element.128), channel_id=1, source_target_pairs={{0,2},{1,3},{2,0},{3,1},{4,6},{5,7},{6,4},{7,5},{8,10},{9,11},{10,... | collective-permute-start | bytes 393224 | tf_op jit(solution)/shard_map/ppermute | solution.py:446
  29.5 8.4 %collective-permute-start.9 = (bf16[32,16,128]{2,1,0:T(8,128)(2,1)S(1)}, bf16[32,16,128]{2,1,0:T(8,128)(2,1)S(1)}, u32[]{:S(2)}, u32[]{:S(2)}) collective-permute-start(bf16[32,16,128]{2,1,0:T(8,128)(2,1)S(1)} %get-tuple-element.123), channel_id=1, source_target_pairs={{0,1},{1,0},{8,16},{9,17},{16,8},{17,9},{24,25},{25,24},{2,3},{3,2... | collective-permute-start | bytes 393224 | tf_op jit(solution)/shard_map/ppermute | solution.py:446
  29.6 8.3 %collective-permute-start.8 = (bf16[32,16,128]{2,1,0:T(8,128)(2,1)S(1)}, bf16[32,16,128]{2,1,0:T(8,128)(2,1)S(1)}, u32[]{:S(2)}, u32[]{:S(2)}) collective-permute-start(bf16[32,16,128]{2,1,0:T(8,128)(2,1)S(1)} %get-tuple-element.124), channel_id=1, source_target_pairs={{0,8},{1,9},{8,0},{9,1},{16,24},{17,25},{24,16},{25,17},{2,10},{3,... | collective-permute-start | bytes 393224 | tf_op jit(solution)/shard_map/ppermute | solution.py:446
  31.6 6.4 %collective-permute-start.11 = (bf16[32,16,128]{2,1,0:T(8,128)(2,1)S(1)}, bf16[32,16,128]{2,1,0:T(8,128)(2,1)S(1)}, u32[]{:S(2)}, u32[]{:S(2)}) collective-permute-start(bf16[32,16,128]{2,1,0:T(8,128)(2,1)S(1)} %get-tuple-element.119), channel_id=1, source_target_pairs={{0,1},{1,0},{2,4},{3,5},{4,2},{5,3},{6,7},{7,6},{8,9},{9,8},{10,12... | collective-permute-start | bytes 393224 | tf_op jit(solution)/shard_map/ppermute | solution.py:446
  31.6 6.3 %collective-permute-start.10 = (bf16[32,16,128]{2,1,0:T(8,128)(2,1)S(1)}, bf16[32,16,128]{2,1,0:T(8,128)(2,1)S(1)}, u32[]{:S(2)}, u32[]{:S(2)}) collective-permute-start(bf16[32,16,128]{2,1,0:T(8,128)(2,1)S(1)} %get-tuple-element.120), channel_id=1, source_target_pairs={{0,2},{1,3},{2,0},{3,1},{4,6},{5,7},{6,4},{7,5},{8,10},{9,11},{10,... | collective-permute-start | bytes 393224 | tf_op jit(solution)/shard_map/ppermute | solution.py:446
  38.6 8.1 %collective-permute-start.13 = (bf16[32,16,128]{2,1,0:T(8,128)(2,1)S(1)}, bf16[32,16,128]{2,1,0:T(8,128)(2,1)S(1)}, u32[]{:S(2)}, u32[]{:S(2)}) collective-permute-start(bf16[32,16,128]{2,1,0:T(8,128)(2,1)S(1)} %get-tuple-element.115), channel_id=1, source_target_pairs={{0,1},{1,0},{8,16},{9,17},{16,8},{17,9},{24,25},{25,24},{2,3},{3,2... | collective-permute-start | bytes 393224 | tf_op jit(solution)/shard_map/ppermute | solution.py:446
  38.7 8.0 %collective-permute-start.12 = (bf16[32,16,128]{2,1,0:T(8,128)(2,1)S(1)}, bf16[32,16,128]{2,1,0:T(8,128)(2,1)S(1)}, u32[]{:S(2)}, u32[]{:S(2)}) collective-permute-start(bf16[32,16,128]{2,1,0:T(8,128)(2,1)S(1)} %get-tuple-element.116), channel_id=1, source_target_pairs={{0,8},{1,9},{8,0},{9,1},{16,24},{17,25},{24,16},{25,17},{2,10},{3,... | collective-permute-start | bytes 393224 | tf_op jit(solution)/shard_map/ppermute | solution.py:446
  40.9 5.9 %collective-permute-start.15 = (bf16[32,16,128]{2,1,0:T(8,128)(2,1)S(1)}, bf16[32,16,128]{2,1,0:T(8,128)(2,1)S(1)}, u32[]{:S(2)}, u32[]{:S(2)}) collective-permute-start(bf16[32,16,128]{2,1,0:T(8,128)(2,1)S(1)} %get-tuple-element.111), channel_id=1, source_target_pairs={{0,1},{1,0},{2,4},{3,5},{4,2},{5,3},{6,7},{7,6},{8,9},{9,8},{10,12... | collective-permute-start | bytes 393224 | tf_op jit(solution)/shard_map/ppermute | solution.py:446
  41.0 5.9 %collective-permute-start.14 = (bf16[32,16,128]{2,1,0:T(8,128)(2,1)S(1)}, bf16[32,16,128]{2,1,0:T(8,128)(2,1)S(1)}, u32[]{:S(2)}, u32[]{:S(2)}) collective-permute-start(bf16[32,16,128]{2,1,0:T(8,128)(2,1)S(1)} %get-tuple-element.112), channel_id=1, source_target_pairs={{0,2},{1,3},{2,0},{3,1},{4,6},{5,7},{6,4},{7,5},{8,10},{9,11},{10,... | collective-permute-start | bytes 393224 | tf_op jit(solution)/shard_map/ppermute | solution.py:446
  48.2 10.4 %collective-permute-start.16 = (bf16[16,2,256,128]{3,2,1,0:T(8,128)(2,1)S(1)}, bf16[16,2,256,128]{3,2,1,0:T(8,128)(2,1)S(1)}, u32[]{:S(2)}, u32[]{:S(2)}) collective-permute-start(bf16[16,2,256,128]{3,2,1,0:T(8,128)(2,1)S(1)} %snapshot.1.own_ref), channel_id=1, source_target_pairs={{0,1},{1,0},{2,3},{3,2},{4,5},{5,4},{6,7},{7,6},{8,9},{9,8},{10,11... | collective-permute-start | bytes 6291464 | tf_op jit(solution)/shard_map/ppermute | solution.py:600
  48.3 4.7 %collective-permute-start.19 = (f32[32,64]{1,0:T(8,128)S(1)}, f32[32,64]{1,0:T(8,128)S(1)}, u32[]{:S(2)}, u32[]{:S(2)}) collective-permute-start(f32[32,64]{1,0:T(8,128)S(1)} %get-tuple-element.99.refs_0_), channel_id=1, source_target_pairs={{0,24},{8,16},{16,8},{24,0},{1,25},{9,17},{17,9},{25,1},{2,26},{10... | collective-permute-start | bytes 24584 | tf_op jit(solution)/shard_map/ppermute | solution.py:460
  49.9 3.7 %collective-permute-start.18 = (f32[32,64]{1,0:T(8,128)S(1)}, f32[32,64]{1,0:T(8,128)S(1)}, u32[]{:S(2)}, u32[]{:S(2)}) collective-permute-start(f32[32,64]{1,0:T(8,128)S(1)} %get-tuple-element.99.refs_0_), channel_id=1, source_target_pairs={{0,16},{8,24},{16,0},{24,8},{1,17},{9,25},{17,1},{25,9},{2,18},{10... | collective-permute-start | bytes 24584 | tf_op jit(solution)/shard_map/ppermute | solution.py:460
  50.5 3.7 %collective-permute-start.17 = (f32[32,64]{1,0:T(8,128)S(1)}, f32[32,64]{1,0:T(8,128)S(1)}, u32[]{:S(2)}, u32[]{:S(2)}) collective-permute-start(f32[32,64]{1,0:T(8,128)S(1)} %get-tuple-element.99.refs_0_), channel_id=1, source_target_pairs={{0,8},{8,0},{16,24},{24,16},{1,9},{9,1},{17,25},{25,17},{2,10},{10... | collective-permute-start | bytes 24584 | tf_op jit(solution)/shard_map/ppermute | solution.py:460
  54.2 6.7 %collective-permute-start.22 = (f32[32,64]{1,0:T(8,128)S(1)}, f32[32,64]{1,0:T(8,128)S(1)}, u32[]{:S(2)}, u32[]{:S(2)}) collective-permute-start(f32[32,64]{1,0:T(8,128)S(1)} %line_sum.1), channel_id=1, source_target_pairs={{0,6},{2,4},{4,2},{6,0},{1,7},{3,5},{5,3},{7,1},{8,14},{10,12},{12... | collective-permute-start | bytes 24584 | tf_op jit(solution)/shard_map/ppermute | solution.py:460
  56.1 4.8 %collective-permute-start.21 = (f32[32,64]{1,0:T(8,128)S(1)}, f32[32,64]{1,0:T(8,128)S(1)}, u32[]{:S(2)}, u32[]{:S(2)}) collective-permute-start(f32[32,64]{1,0:T(8,128)S(1)} %line_sum.1), channel_id=1, source_target_pairs={{0,4},{2,6},{4,0},{6,2},{1,5},{3,7},{5,1},{7,3},{8,12},{10,14},{12... | collective-permute-start | bytes 24584 | tf_op jit(solution)/shard_map/ppermute | solution.py:460
  56.2 4.7 %collective-permute-start.20 = (f32[32,64]{1,0:T(8,128)S(1)}, f32[32,64]{1,0:T(8,128)S(1)}, u32[]{:S(2)}, u32[]{:S(2)}) collective-permute-start(f32[32,64]{1,0:T(8,128)S(1)} %line_sum.1), channel_id=1, source_target_pairs={{0,2},{2,0},{4,6},{6,4},{1,3},{3,1},{5,7},{7,5},{8,10},{10,8},{12,... | collective-permute-start | bytes 24584 | tf_op jit(solution)/shard_map/ppermute | solution.py:460
  58.7 2.2 %copy-start = (f32[64,32]{0,1:T(8,128)S(1)}, f32[64,32]{0,1:T(8,128)}, u32[]{:S(2)}) copy-start(f32[64,32]{0,1:T(8,128)} %param.11) | copy-start | bytes 24580

commit v7 on v6

--- a/solution.py
+++ b/solution.py
@@ -186,20 +186,28 @@
     lax.fori_loop(0, samples // BLOCK, body, 0)
 
 
-def edge_kernel(lined, w_in, u_ref, *refs):
+def edge_kernel(first, w_in, u_ref, *refs):
     del w_in
-    cx0, cx1, cy0, cy1, hx0, hx1, hy0, hy1 = refs[:8]
-    w_ref, lx, ux, ly, uy, *lines = refs[-7:]
+    coefs, halos = refs[:4], refs[4:8]
+    made = refs[-4:] if first else ()
+    w_ref, lx, ux, ly, uy, *lines = refs[-11:-4] if first else refs[-7:]
     samples, nx, ny, nz = u_ref.shape
     w_rows, u_rows = flat(w_ref), flat(u_ref)
 
+    def flux(i, s, state):
+        if first:
+            coef = coefs[i][s] + HALF * halos[i][0, s].astype(F32)
+            made[i][s] = coef
+            return coef * (halos[i][1, s].astype(F32) - state)
+        return coefs[i][s] * (halos[i][s].astype(F32) - state)
+
     def one(s):
-        for x, coef, halo in ((0, cx0, hx0), (nx - 1, cx1, hx1)):
-            w_ref[s, x] = w_ref[s, x] + coef[s] * (halo[s].astype(F32) - u_ref[s, x])
-        for end, (coef, halo, out) in enumerate(((cy0, hy0, ly), (cy1, hy1, uy))):
+        for i, x in enumerate((0, nx - 1)):
+            w_ref[s, x] = w_ref[s, x] + flux(i, s, u_ref[s, x])
+        for end, out in enumerate((ly, uy)):
             line = y_line(u_ref, s, end * (ny - 1))
-            state = refs[8 + end][s] if lined else u_rows[line, :]
-            value = w_rows[line, :] + coef[s] * (halo[s].astype(F32) - state)
+            state = u_rows[line, :] if first else refs[8 + end][s]
+            value = w_rows[line, :] + flux(2 + end, s, state)
             w_rows[line, :] = value
             out[s] = value.astype(BF)
             lines[end][s] = value
@@ -226,16 +234,16 @@
         out_ref[x, h] = part.reshape(count * ROWS, nz).astype(BF)
 
 
-def one_hot(rows, cols, row_width, col_width):
-    row = lax.broadcasted_iota(jnp.int32, (rows, cols), 0) // row_width
-    col = lax.broadcasted_iota(jnp.int32, (rows, cols), 1) // col_width
-    return (row == col).astype(BF)
-
-
-def spread(block):
-    rows, cols = block.shape
-    tall = jnp.dot(one_hot(rows * ROWS, rows, ROWS, 1), block, preferred_element_type=F32).astype(BF)
-    full = jnp.dot(tall, one_hot(cols, cols * ROWS, 1, ROWS), preferred_element_type=F32)
+def spread(omega, ranks, samples, rank_group, sample_group):
+    rows, cols = ranks * ROWS, samples * ROWS
+
+    def pick(count, axis, group, width):
+        shape = (count, omega.shape[axis])
+        row = lax.broadcasted_iota(jnp.int32, shape, 0) // ROWS + group * width
+        return (row == lax.broadcasted_iota(jnp.int32, shape, 1)).astype(BF)
+
+    tall = contract(pick(rows, 1, rank_group, ranks), omega).astype(BF)
+    full = contract(tall, pick(cols, 0, sample_group, samples))
     row = lax.broadcasted_iota(jnp.int32, full.shape, 0) % ROWS
     col = lax.broadcasted_iota(jnp.int32, full.shape, 1) % ROWS
     return jnp.where(row == col, full, 0.0).astype(BF)
@@ -253,8 +261,11 @@
     copies.append(pltpu.make_async_copy(prev_hbm, prev_ref, sem.at[2]))
     for copy in copies:
         copy.start()
-    for i in range(omega_ref.shape[0]):
-        weight_ref[i] = spread(omega_ref[i])
+    group, groups = lax.axis_index("par"), lax.axis_size("par")
+    for i in range(2):
+        source = (group + i * (groups - 1)) % groups
+        shape = [n // ROWS for n in weight_ref.shape[1:]]
+        weight_ref[i] = spread(omega_ref[...], *shape, group, source)
     for end in range(2):
         copies[end].wait()
         wide[...] = xbuf[end].astype(F32)
@@ -482,7 +493,7 @@
         nbytes=cells,
     )(initial_state, conductivity)
     got = exchange(sent)
-    halos = [g[1] for g in got]
+    halos = got
 
     groups = samples // BLOCK
     state, moved, *made = vmem_call(
@@ -496,14 +507,9 @@
         nbytes=16 * cells,
     )(initial_state, conductivity)
     coefs, kfaces = made[:4], made[4:]
-    face_coefs = [k + HALF * g[0].astype(F32) for k, g in zip(kfaces, got)]
+    face_coefs = kfaces
 
     own_ranks = range_prev.shape[0]
-    own_cols = lax.dynamic_slice_in_dim(omega, par * own_ranks, own_ranks, 1).T
-    source = (par + par_size - 1) % par_size
-    omega_blocks = jnp.stack(
-        [lax.dynamic_slice_in_dim(own_cols, p * samples, samples, 1) for p in (par, source)]
-    )
     held_psi, psi_y = vmem_call(
         psi_kernel,
         [(split_shape(psi.shape), BF), ((2, nx, ranks, nz), BF)],
@@ -551,19 +557,23 @@
                 hbm_in=(0, 1),
                 flops=cells,
                 nbytes=cells,
-            )(psi, range_prev, omega_blocks, moved)
+            )(psi, range_prev, omega, moved)
             kept += (psi_x, weights, prev)
         if step < STEPS - 1:
             outs = [(block, F32)] + [(x_face, BF)] * 2 + [(y_face, BF)] * 2 + [(y_face, F32)] * 2
+            if step == 0:
+                outs += [(x_face, F32)] * 2 + [(y_face, F32)] * 2
             state, *edges = vmem_call(
-                functools.partial(edge_kernel, step > 0),
+                functools.partial(edge_kernel, step == 0),
                 outs,
                 "edge",
                 aliases={0: 0},
                 flops=cells,
                 nbytes=cells,
             )(moved, state, *face_coefs, *halos, *lines, *kept)
-            edges, lines = edges[:4], edges[4:]
+            if step == 0:
+                face_coefs = edges[6:]
+            edges, lines = edges[:4], edges[4:6]
 
     main, written = vmem_call(
         corange_kernel,

time: 61.7 us -> 61.7 us (level)
  transfers between devices with their start and end apart: 23 -> 23, of which waited for: 6 -> 5; matrix products, arithmetic and copies ran while one was open for 1% -> 0% of each run, Pallas kernels for 40% -> 40%
where the time goes in v7:
time: 61.7 us; the launch traced here: 61.5 us
  Pallas kernels  29.6 us (48%)
  starting transfers between devices  26.2 us (42%)
  waiting for transfers between devices  3.56 us (6%)
  other arithmetic  1.07 us (2%)
  between operations  1.07 us (2%)
    pallas_call x15, Pallas kernels, call(): pl.pallas_call(kernel, out_shape=out_shape, in_specs=in_specs, out_specs=...  29.6 us
    ppermute x16, starting transfers between devices, exchange(): got[axis, parity] = lax.ppermute(mine, (axis, 'par'), pairs)  18.1 us
    ppermute x6, starting transfers between devices, received(): lax.ppermute(value, axis, [(i, i ^ shift) for i in range(count)])  8 us
    ppermute x6, waiting for transfers between devices, received(): lax.ppermute(value, axis, [(i, i ^ shift) for i in range(count)])  2.42 us
  transfers between devices with their start and end apart: 23, of which 5 were waited for; matrix products, arithmetic and copies ran while one was open for 0% of the time, Pallas kernels for 40%

profile of v7, /device:TPU:0, one launch (start us, length us, event | category | flops | bytes accessed | tf_op | source)
XLA Modules:
  0.0 61.5 jit_solution(738195512070459143)
XLA Ops:
  0.6 1.7 %faces.1 = (bf16[2,32,16,128]{3,2,1,0:T(8,128)(2,1)S(1)}, bf16[2,32,16,128]{3,2,1,0:T(8,128)(2,1)S(1)}, bf16[2,32,16,128]{3,2,1,0:T(8,128)(2,1)S(1)}, bf16[2,32,16,128]{3,2,1,0:T(8,128)(2,1)S(1)}) custom-call(f32[32,16,16,128]{3,2,1,0:T(8,128)} %u_ref.1, f32[32,16,16,128]{3,2,1,0:T(8,128)} %k_ref.1), custom_call_target="tpu_custom_call" | custom-call | flops 524288 | bytes 1048576 | tf_op jit(solution)/shard_map/faces/pallas_call | solution.py:35
  2.4 0.5 collective-permute-start.1
  2.9 4.0 %collective-permute-start = (bf16[2,32,16,128]{3,2,1,0:T(8,128)(2,1)S(1)}, bf16[2,32,16,128]{3,2,1,0:T(8,128)(2,1)S(1)}, u32[]{:S(2)}, u32[]{:S(2)}) collective-permute-start(bf16[2,32,16,128]{3,2,1,0:T(8,128)(2,1)S(1)} %get-tuple-element.116), channel_id=1, source_target_pairs={{0,8},{1,9},{8,0},{9,1},{16,24},{17,25},{24,16},{25,17},{2,10},{3,... | collective-permute-start | bytes 786440 | tf_op jit(solution)/shard_map/ppermute | solution.py:457
  6.9 0.1 collective-permute-start.3
  7.0 3.1 %collective-permute-start.2 = (bf16[2,32,16,128]{3,2,1,0:T(8,128)(2,1)S(1)}, bf16[2,32,16,128]{3,2,1,0:T(8,128)(2,1)S(1)}, u32[]{:S(2)}, u32[]{:S(2)}) collective-permute-start(bf16[2,32,16,128]{3,2,1,0:T(8,128)(2,1)S(1)} %get-tuple-element.112), channel_id=1, source_target_pairs={{0,2},{1,3},{2,0},{3,1},{4,6},{5,7},{6,4},{7,5},{8,10},{9,11},{10,... | collective-permute-start | bytes 786440 | tf_op jit(solution)/shard_map/ppermute | solution.py:457
  10.1 3.0 %psi.1 = (bf16[16,2,512,128]{3,2,1,0:T(8,128)(2,1)S(1)}, bf16[2,16,64,128]{3,2,1,0:T(8,128)(2,1)S(1)}) custom-call(bf16[64,16,16,128]{3,2,1,0:T(8,128)(2,1)} %psi_hbm.3), custom_call_target="tpu_custom_call" | custom-call | flops 4194304 | bytes 4194304 | tf_op jit(solution)/shard_map/psi/pallas_call | solution.py:35
  13.1 6.9 %first.1 = (f32[32,16,16,128]{3,2,1,0:T(8,128)S(1)}, f32[32,16,16,128]{3,2,1,0:T(8,128)S(1)}, f32[32,16,16,128]{3,2,1,0:T(8,128)S(1)}, f32[32,16,16,128]{3,2,1,0...) custom-call(f32[32,16,16,128]{3,2,1,0:T(8,128)} %u_ref.1, ...), custom_call_target="tpu_custom_call" | custom-call | flops 37748736 | bytes 16777216 | tf_op jit(solution)/shard_map/first/pallas_call | solution.py:35
  20.0 0.0 collective-permute-done.1
  20.0 0.0 collective-permute-done
  20.1 0.9 %edge.3 = (f32[32,16,16,128]{3,2,1,0:T(8,128)S(1)}, bf16[32,16,128]{2,1,0:T(8,128)(2,1)S(1)}, bf16[32,16,128]{2,1,0:T(8,128)(2,1)S(1)}, bf16[32,16,128]{2,1,0:T(...) custom-call(f32[32,16,16,128]{3,2,1,0:T(8,128)S(1)} %get-tuple-eleme, ...), custom_call_target="tpu_custom_call", output_to_operand_aliasing={{0}: (0, {})} | custom-call | flops 1048576 | bytes 1048576 | tf_op jit(solution)/shard_map/edge/pallas_call | solution.py:35
  21.1 0.1 collective-permute-start.5
  21.1 1.6 %collective-permute-start.4 = (bf16[32,16,128]{2,1,0:T(8,128)(2,1)S(1)}, bf16[32,16,128]{2,1,0:T(8,128)(2,1)S(1)}, u32[]{:S(2)}, u32[]{:S(2)}) collective-permute-start(bf16[32,16,128]{2,1,0:T(8,128)(2,1)S(1)} %get-tuple-element.140), channel_id=1, source_target_pairs={{0,8},{1,9},{8,0},{9,1},{16,24},{17,25},{24,16},{25,17},{2,10},{3,... | collective-permute-start | bytes 393224 | tf_op jit(solution)/shard_map/ppermute | solution.py:457
  22.7 0.1 collective-permute-start.7
  22.8 1.7 %collective-permute-start.6 = (bf16[32,16,128]{2,1,0:T(8,128)(2,1)S(1)}, bf16[32,16,128]{2,1,0:T(8,128)(2,1)S(1)}, u32[]{:S(2)}, u32[]{:S(2)}) collective-permute-start(bf16[32,16,128]{2,1,0:T(8,128)(2,1)S(1)} %get-tuple-element.136), channel_id=1, source_target_pairs={{0,2},{1,3},{2,0},{3,1},{4,6},{5,7},{6,4},{7,5},{8,10},{9,11},{10,... | collective-permute-start | bytes 393224 | tf_op jit(solution)/shard_map/ppermute | solution.py:457
  24.5 3.0 %step.3.w_in = f32[32,16,16,128]{3,2,1,0:T(8,128)S(1)} custom-call(f32[32,16,16,128]{3,2,1,0:T(8,128)S(1)} %get-tuple-element.68.u_ref, f32[32,16,16,128]{3,2,1,0:T(8,128)S(1)} %get-tuple-element.69.cx_ref, f32[32,16,16,128]{3,2,1,0:T(8,128)S(1)} %get-tuple-element.70.cy_ref, f32[32,16,16,128]{3,2,1,0:T(8,128)S(1)} %get-tuple-element.71.cup_ref, ...), custom_call_target="tpu_custom_call" | custom-call | flops 25165824 | bytes 8388608 | tf_op jit(solution)/shard_map/step/pallas_call | solution.py:35
  27.6 0.9 %collective-permute-done.4 = bf16[32,16,128]{2,1,0:T(8,128)(2,1)S(1)} collective-permute-done((bf16[32,16,128]{2,1,0:T(8,128)(2,1)S(1)}, bf16[32,16,128]{2,1,0:T(8,128)(2,1)S(1)}, u32[]{:S(2)}, u32[]{:S(2)}) %collective-permute-start.4) | collective-permute-done | bytes 131104 | tf_op jit(solution)/shard_map/ppermute | solution.py:457
  28.5 0.0 collective-permute-done.7
  28.5 0.2 collective-permute-done.6
  28.7 0.6 edge.4
  29.4 0.1 collective-permute-start.9
  29.5 1.9 %collective-permute-start.8 = (bf16[32,16,128]{2,1,0:T(8,128)(2,1)S(1)}, bf16[32,16,128]{2,1,0:T(8,128)(2,1)S(1)}, u32[]{:S(2)}, u32[]{:S(2)}) collective-permute-start(bf16[32,16,128]{2,1,0:T(8,128)(2,1)S(1)} %get-tuple-element.132), channel_id=1, source_target_pairs={{0,8},{1,9},{8,0},{9,1},{16,24},{17,25},{24,16},{25,17},{2,10},{3,... | collective-permute-start | bytes 393224 | tf_op jit(solution)/shard_map/ppermute | solution.py:457
  31.4 0.1 collective-permute-start.11
  31.5 1.4 %collective-permute-start.10 = (bf16[32,16,128]{2,1,0:T(8,128)(2,1)S(1)}, bf16[32,16,128]{2,1,0:T(8,128)(2,1)S(1)}, u32[]{:S(2)}, u32[]{:S(2)}) collective-permute-start(bf16[32,16,128]{2,1,0:T(8,128)(2,1)S(1)} %get-tuple-element.128), channel_id=1, source_target_pairs={{0,2},{1,3},{2,0},{3,1},{4,6},{5,7},{6,4},{7,5},{8,10},{9,11},{10,... | collective-permute-start | bytes 393224 | tf_op jit(solution)/shard_map/ppermute | solution.py:457
  33.0 3.0 %step.4.after.w_in = f32[32,16,16,128]{3,2,1,0:T(8,128)S(1)} custom-call(f32[32,16,16,128]{3,2,1,0:T(8,128)S(1)} %get-tuple-element.83.u_ref, f32[32,16,16,128]{3,2,1,0:T(8,128)S(1)} %get-tuple-element.69.cx_ref, f32[32,16,16,128]{3,2,1,0:T(8,128)S(1)} %get-tuple-element.70.cy_ref, f32[32,16,16,128]{3,2,1,0:T(8,128)S(1)} %get-tuple-element.71.cup_ref, ...), custom_call_target="tpu_custom_call" | custom-call | flops 25165824 | bytes 8388608 | tf_op jit(solution)/shard_map/step/pallas_call | solution.py:35
  36.0 1.8 %lines.1 = (bf16[2,16,64,128]{3,2,1,0:T(8,128)(2,1)S(1)}, bf16[2,256,256]{2,1,0:T(8,128)(2,1)S(1)}, bf16[32,16,16,128]{3,2,1,0:T(8,128)(2,1)S(1)}) custom-call(bf16[64,16,16,128]{3,2,1,0:T(8,128)(2,1)} %psi_hbm.3, bf16[32,16,16,128]{3,2,1,0:T(8,128)(2,1)} %prev_hbm.1, bf16[64,64]{1,0:T(8,128)(2,1)S(1)} %copy-done, f32[32,16,16,128]{3,2,1,0:T(8,128)S(1)} %step.4.after.w_in), custom_call_target="tpu_custom_call" | custom-call | flops 1048576 | bytes 1048576 | tf_op jit(solution)/shard_map/lines/pallas_call | solution.py:35
  37.8 0.0 collective-permute-done.9
  37.8 0.0 collective-permute-done.8
  37.9 0.6 edge.5
  38.6 0.1 collective-permute-start.13
  38.6 2.1 %collective-permute-start.12 = (bf16[32,16,128]{2,1,0:T(8,128)(2,1)S(1)}, bf16[32,16,128]{2,1,0:T(8,128)(2,1)S(1)}, u32[]{:S(2)}, u32[]{:S(2)}) collective-permute-start(bf16[32,16,128]{2,1,0:T(8,128)(2,1)S(1)} %get-tuple-element.124), channel_id=1, source_target_pairs={{0,8},{1,9},{8,0},{9,1},{16,24},{17,25},{24,16},{25,17},{2,10},{3,... | collective-permute-start | bytes 393224 | tf_op jit(solution)/shard_map/ppermute | solution.py:457
  40.7 0.1 collective-permute-start.15
  40.8 1.2 %collective-permute-start.14 = (bf16[32,16,128]{2,1,0:T(8,128)(2,1)S(1)}, bf16[32,16,128]{2,1,0:T(8,128)(2,1)S(1)}, u32[]{:S(2)}, u32[]{:S(2)}) collective-permute-start(bf16[32,16,128]{2,1,0:T(8,128)(2,1)S(1)} %get-tuple-element.120), channel_id=1, source_target_pairs={{0,2},{1,3},{2,0},{3,1},{4,6},{5,7},{6,4},{7,5},{8,10},{9,11},{10,... | collective-permute-start | bytes 393224 | tf_op jit(solution)/shard_map/ppermute | solution.py:457
  42.0 3.1 %step.5 = (f32[32,16,16,128]{3,2,1,0:T(8,128)S(1)}, f32[32,16,16,128]{3,2,1,0:T(8,128)}) custom-call(f32[32,16,16,128]{3,2,1,0:T(8,128)S(1)} %get-tuple-element.93.u_ref, f32[32,16,16,128]{3,2,1,0:T(8,128)S(1)} %get-tuple-element.69.cx_ref, f32[32,16,16,128]{3,2,1,0:T(8,128)S(1)} %get-tuple-element.70.cy_ref, ...), custom_call_target="tpu_custom_call" | custom-call | flops 25165824 | bytes 8388608 | tf_op jit(solution)/shard_map/step/pallas_call | solution.py:35
  45.1 1.6 %corange.1 = (f32[32,64]{1,0:T(8,128)S(1)}, f32[32,16,16,128]{3,2,1,0:T(8,128)}) custom-call(bf16[16,2,512,128]{3,2,1,0:T(8,128)(2,1)S(1)} %get-tuple-element.66.refs_8_.refs_0_.refs_10_.psi_ref, f32[32,16,16,128]{3,2,1,0:T(8,128)S(1)} %get-tuple-element.94.u_ref.w_in, f32[32,16,16,128]{3,2,1,0:T(8,128)} %get-tuple-element.101.state_in), custom_call_target="tpu_custom_call", output_to_operand_aliasing={{1}: (2, {})} | custom-call | flops 1073741824 | bytes 4194304 | tf_op jit(solution)/shard_map/corange/pallas_call | solution.py:35
  46.8 1.0 %finish.1 = (f32[32,16,16,128]{3,2,1,0:T(8,128)S(1)}, f32[32,64]{1,0:T(8,128)S(1)}) custom-call(f32[32,16,16,128]{3,2,1,0:T(8,128)S(1)} %get-tuple-element.94.u_ref.w_in, f32[32,16,16,128]{3,2,1,0:T(8,128)S(1)} %get-tuple-element.93.u_ref, f32[32,16,128]{2,1,0:T(8,128)S(1)} %get-tuple-element.73.refs_0_.cx0, ...), custom_call_target="tpu_custom_call", output_to_operand_aliasing={{0}: (0, {})} | custom-call | flops 1048576 | bytes 2097152 | tf_op jit(solution)/shard_map/finish/pallas_call | solution.py:35
  47.9 0.3 snapshot.1.own_ref
  48.2 0.1 collective-permute-start.16
  48.3 1.6 %collective-permute-start.19 = (f32[32,64]{1,0:T(8,128)S(1)}, f32[32,64]{1,0:T(8,128)S(1)}, u32[]{:S(2)}, u32[]{:S(2)}) collective-permute-start(f32[32,64]{1,0:T(8,128)S(1)} %get-tuple-element.107.refs_0_), channel_id=1, source_target_pairs={{0,24},{8,16},{16,8},{24,0},{1,25},{9,17},{17,9},{25,1},{2,26},{10... | collective-permute-start | bytes 24584 | tf_op jit(solution)/shard_map/ppermute | solution.py:471
  49.8 0.7 %collective-permute-start.18 = (f32[32,64]{1,0:T(8,128)S(1)}, f32[32,64]{1,0:T(8,128)S(1)}, u32[]{:S(2)}, u32[]{:S(2)}) collective-permute-start(f32[32,64]{1,0:T(8,128)S(1)} %get-tuple-element.107.refs_0_), channel_id=1, source_target_pairs={{0,16},{8,24},{16,0},{24,8},{1,17},{9,25},{17,1},{25,9},{2,18},{10... | collective-permute-start | bytes 24584 | tf_op jit(solution)/shard_map/ppermute | solution.py:471
  50.5 1.3 %collective-permute-start.17 = (f32[32,64]{1,0:T(8,128)S(1)}, f32[32,64]{1,0:T(8,128)S(1)}, u32[]{:S(2)}, u32[]{:S(2)}) collective-permute-start(f32[32,64]{1,0:T(8,128)S(1)} %get-tuple-element.107.refs_0_), channel_id=1, source_target_pairs={{0,8},{8,0},{16,24},{24,16},{1,9},{9,1},{17,25},{25,17},{2,10},{10... | collective-permute-start | bytes 24584 | tf_op jit(solution)/shard_map/ppermute | solution.py:471
  51.8 1.1 %collective-permute-done.19.refs_3_ = f32[32,64]{1,0:T(8,128)S(1)} collective-permute-done((f32[32,64]{1,0:T(8,128)S(1)}, f32[32,64]{1,0:T(8,128)S(1)}, u32[]{:S(2)}, u32[]{:S(2)}) %collective-permute-start.19) | collective-permute-done | bytes 8224 | tf_op jit(solution)/shard_map/ppermute | solution.py:471
  53.0 0.6 collective-permute-done.18.refs_2_
  53.6 0.7 %collective-permute-done.17.refs_1_ = f32[32,64]{1,0:T(8,128)S(1)} collective-permute-done((f32[32,64]{1,0:T(8,128)S(1)}, f32[32,64]{1,0:T(8,128)S(1)}, u32[]{:S(2)}, u32[]{:S(2)}) %collective-permute-start.17) | collective-permute-done | bytes 8224 | tf_op jit(solution)/shard_map/ppermute | solution.py:471
  54.2 1.8 %collective-permute-start.22 = (f32[32,64]{1,0:T(8,128)S(1)}, f32[32,64]{1,0:T(8,128)S(1)}, u32[]{:S(2)}, u32[]{:S(2)}) collective-permute-start(f32[32,64]{1,0:T(8,128)S(1)} %line_sum.1), channel_id=1, source_target_pairs={{0,6},{2,4},{4,2},{6,0},{1,7},{3,5},{5,3},{7,1},{8,14},{10,12},{12... | collective-permute-start | bytes 24584 | tf_op jit(solution)/shard_map/ppermute | solution.py:471
  56.0 0.1 collective-permute-start.21
  56.2 2.5 %collective-permute-start.20 = (f32[32,64]{1,0:T(8,128)S(1)}, f32[32,64]{1,0:T(8,128)S(1)}, u32[]{:S(2)}, u32[]{:S(2)}) collective-permute-start(f32[32,64]{1,0:T(8,128)S(1)} %line_sum.1), channel_id=1, source_target_pairs={{0,2},{2,0},{4,6},{6,4},{1,3},{3,1},{5,7},{7,5},{8,10},{10,8},{12,... | collective-permute-start | bytes 24584 | tf_op jit(solution)/shard_map/ppermute | solution.py:471
  58.7 2.1 %range.1 = (bf16[32,16,16,128]{3,2,1,0:T(8,128)(2,1)}, f32[32,16,16,128]{3,2,1,0:T(8,128)}, f32[32,64]{1,0:T(8,128)S(1)}) custom-call(bf16[2,256,256]{2,1,0:T(8,128)(2,1)S(1)} %get-tuple-element.84.refs_13_.refs_3_.refs_6_.refs_1_.weight_ref, bf16[16,2,256,128]{3,2,1,0:T(8,128)(2,1)S(1)} %snapshot.1.own_ref, ...), custom_call_target="tpu_custom_call", output_to_operand_aliasing={{1}: (5, {})} | custom-call | flops 1073741824 | bytes 4194304 | tf_op jit(solution)/shard_map/range/pallas_call | solution.py:35
  60.9 0.6 %fusion.4 = f32[64,32]{0,1:T(8,128)} fusion(f32[32,64]{1,0:T(8,128)S(1)} %get-tuple-element.108, f32[32,64]{1,0:T(8,128)S(1)} %collective-permute-done.22, f32[32,64]{1,0:T(8,128)S(1)} %collective-permute-done.21, f32[32,64]{1,0:T(8,128)S(1)} %collective-permute-done.20, f32[32,64]{1,0:T(8,128)S(1)} %line_sum.1, f32[64,32]{0,1:T(8,128)S(1)} %copy-done.1), kind=kLoop, calls=%fused_computation.37 | loop fusion | flops 10240 | bytes 57344 | tf_op jit(solution)/shard_map/transpose | solution.py:624
  (34 shorter events, 0.5 us)
Async XLA Ops:
  2.4 17.6 %collective-permute-start.1 = (bf16[2,32,16,128]{3,2,1,0:T(8,128)(2,1)S(1)}, bf16[2,32,16,128]{3,2,1,0:T(8,128)(2,1)S(1)}, u32[]{:S(2)}, u32[]{:S(2)}) collective-permute-start(bf16[2,32,16,128]{3,2,1,0:T(8,128)(2,1)S(1)} %get-tuple-element.115), channel_id=1, source_target_pairs={{0,1},{1,0},{8,16},{9,17},{16,8},{17,9},{24,25},{25,24},{2,3},{3,2... | collective-permute-start | bytes 786440 | tf_op jit(solution)/shard_map/ppermute | solution.py:457
  2.9 17.1 %collective-permute-start = (bf16[2,32,16,128]{3,2,1,0:T(8,128)(2,1)S(1)}, bf16[2,32,16,128]{3,2,1,0:T(8,128)(2,1)S(1)}, u32[]{:S(2)}, u32[]{:S(2)}) collective-permute-start(bf16[2,32,16,128]{3,2,1,0:T(8,128)(2,1)S(1)} %get-tuple-element.116), channel_id=1, source_target_pairs={{0,8},{1,9},{8,0},{9,1},{16,24},{17,25},{24,16},{25,17},{2,10},{3,... | collective-permute-start | bytes 786440 | tf_op jit(solution)/shard_map/ppermute | solution.py:457
  6.9 13.2 %collective-permute-start.3 = (bf16[2,32,16,128]{3,2,1,0:T(8,128)(2,1)S(1)}, bf16[2,32,16,128]{3,2,1,0:T(8,128)(2,1)S(1)}, u32[]{:S(2)}, u32[]{:S(2)}) collective-permute-start(bf16[2,32,16,128]{3,2,1,0:T(8,128)(2,1)S(1)} %get-tuple-element.111), channel_id=1, source_target_pairs={{0,1},{1,0},{2,4},{3,5},{4,2},{5,3},{6,7},{7,6},{8,9},{9,8},{10,12... | collective-permute-start | bytes 786440 | tf_op jit(solution)/shard_map/ppermute | solution.py:457
  7.0 13.1 %collective-permute-start.2 = (bf16[2,32,16,128]{3,2,1,0:T(8,128)(2,1)S(1)}, bf16[2,32,16,128]{3,2,1,0:T(8,128)(2,1)S(1)}, u32[]{:S(2)}, u32[]{:S(2)}) collective-permute-start(bf16[2,32,16,128]{3,2,1,0:T(8,128)(2,1)S(1)} %get-tuple-element.112), channel_id=1, source_target_pairs={{0,2},{1,3},{2,0},{3,1},{4,6},{5,7},{6,4},{7,5},{8,10},{9,11},{10,... | collective-permute-start | bytes 786440 | tf_op jit(solution)/shard_map/ppermute | solution.py:457
  21.1 6.5 %collective-permute-start.5 = (bf16[32,16,128]{2,1,0:T(8,128)(2,1)S(1)}, bf16[32,16,128]{2,1,0:T(8,128)(2,1)S(1)}, u32[]{:S(2)}, u32[]{:S(2)}) collective-permute-start(bf16[32,16,128]{2,1,0:T(8,128)(2,1)S(1)} %get-tuple-element.139), channel_id=1, source_target_pairs={{0,1},{1,0},{8,16},{9,17},{16,8},{17,9},{24,25},{25,24},{2,3},{3,2... | collective-permute-start | bytes 393224 | tf_op jit(solution)/shard_map/ppermute | solution.py:457
  21.1 7.3 %collective-permute-start.4 = (bf16[32,16,128]{2,1,0:T(8,128)(2,1)S(1)}, bf16[32,16,128]{2,1,0:T(8,128)(2,1)S(1)}, u32[]{:S(2)}, u32[]{:S(2)}) collective-permute-start(bf16[32,16,128]{2,1,0:T(8,128)(2,1)S(1)} %get-tuple-element.140), channel_id=1, source_target_pairs={{0,8},{1,9},{8,0},{9,1},{16,24},{17,25},{24,16},{25,17},{2,10},{3,... | collective-permute-start | bytes 393224 | tf_op jit(solution)/shard_map/ppermute | solution.py:457
  22.7 5.8 %collective-permute-start.7 = (bf16[32,16,128]{2,1,0:T(8,128)(2,1)S(1)}, bf16[32,16,128]{2,1,0:T(8,128)(2,1)S(1)}, u32[]{:S(2)}, u32[]{:S(2)}) collective-permute-start(bf16[32,16,128]{2,1,0:T(8,128)(2,1)S(1)} %get-tuple-element.135), channel_id=1, source_target_pairs={{0,1},{1,0},{2,4},{3,5},{4,2},{5,3},{6,7},{7,6},{8,9},{9,8},{10,12... | collective-permute-start | bytes 393224 | tf_op jit(solution)/shard_map/ppermute | solution.py:457
  22.8 5.9 %collective-permute-start.6 = (bf16[32,16,128]{2,1,0:T(8,128)(2,1)S(1)}, bf16[32,16,128]{2,1,0:T(8,128)(2,1)S(1)}, u32[]{:S(2)}, u32[]{:S(2)}) collective-permute-start(bf16[32,16,128]{2,1,0:T(8,128)(2,1)S(1)} %get-tuple-element.136), channel_id=1, source_target_pairs={{0,2},{1,3},{2,0},{3,1},{4,6},{5,7},{6,4},{7,5},{8,10},{9,11},{10,... | collective-permute-start | bytes 393224 | tf_op jit(solution)/shard_map/ppermute | solution.py:457
  29.4 8.4 %collective-permute-start.9 = (bf16[32,16,128]{2,1,0:T(8,128)(2,1)S(1)}, bf16[32,16,128]{2,1,0:T(8,128)(2,1)S(1)}, u32[]{:S(2)}, u32[]{:S(2)}) collective-permute-start(bf16[32,16,128]{2,1,0:T(8,128)(2,1)S(1)} %get-tuple-element.131), channel_id=1, source_target_pairs={{0,1},{1,0},{8,16},{9,17},{16,8},{17,9},{24,25},{25,24},{2,3},{3,2... | collective-permute-start | bytes 393224 | tf_op jit(solution)/shard_map/ppermute | solution.py:457
  29.5 8.4 %collective-permute-start.8 = (bf16[32,16,128]{2,1,0:T(8,128)(2,1)S(1)}, bf16[32,16,128]{2,1,0:T(8,128)(2,1)S(1)}, u32[]{:S(2)}, u32[]{:S(2)}) collective-permute-start(bf16[32,16,128]{2,1,0:T(8,128)(2,1)S(1)} %get-tuple-element.132), channel_id=1, source_target_pairs={{0,8},{1,9},{8,0},{9,1},{16,24},{17,25},{24,16},{25,17},{2,10},{3,... | collective-permute-start | bytes 393224 | tf_op jit(solution)/shard_map/ppermute | solution.py:457
  31.4 6.4 %collective-permute-start.11 = (bf16[32,16,128]{2,1,0:T(8,128)(2,1)S(1)}, bf16[32,16,128]{2,1,0:T(8,128)(2,1)S(1)}, u32[]{:S(2)}, u32[]{:S(2)}) collective-permute-start(bf16[32,16,128]{2,1,0:T(8,128)(2,1)S(1)} %get-tuple-element.127), channel_id=1, source_target_pairs={{0,1},{1,0},{2,4},{3,5},{4,2},{5,3},{6,7},{7,6},{8,9},{9,8},{10,12... | collective-permute-start | bytes 393224 | tf_op jit(solution)/shard_map/ppermute | solution.py:457
  31.5 6.4 %collective-permute-start.10 = (bf16[32,16,128]{2,1,0:T(8,128)(2,1)S(1)}, bf16[32,16,128]{2,1,0:T(8,128)(2,1)S(1)}, u32[]{:S(2)}, u32[]{:S(2)}) collective-permute-start(bf16[32,16,128]{2,1,0:T(8,128)(2,1)S(1)} %get-tuple-element.128), channel_id=1, source_target_pairs={{0,2},{1,3},{2,0},{3,1},{4,6},{5,7},{6,4},{7,5},{8,10},{9,11},{10,... | collective-permute-start | bytes 393224 | tf_op jit(solution)/shard_map/ppermute | solution.py:457
  33.0 3.0 %copy-start = (bf16[64,64]{1,0:T(8,128)(2,1)S(1)}, bf16[64,64]{1,0:T(8,128)(2,1)}, u32[]{:S(2)}) copy-start(bf16[64,64]{1,0:T(8,128)(2,1)} %omega_ref.1) | copy-start | bytes 24580
  38.6 8.2 %collective-permute-start.13 = (bf16[32,16,128]{2,1,0:T(8,128)(2,1)S(1)}, bf16[32,16,128]{2,1,0:T(8,128)(2,1)S(1)}, u32[]{:S(2)}, u32[]{:S(2)}) collective-permute-start(bf16[32,16,128]{2,1,0:T(8,128)(2,1)S(1)} %get-tuple-element.123), channel_id=1, source_target_pairs={{0,1},{1,0},{8,16},{9,17},{16,8},{17,9},{24,25},{25,24},{2,3},{3,2... | collective-permute-start | bytes 393224 | tf_op jit(solution)/shard_map/ppermute | solution.py:457
  38.6 8.1 %collective-permute-start.12 = (bf16[32,16,128]{2,1,0:T(8,128)(2,1)S(1)}, bf16[32,16,128]{2,1,0:T(8,128)(2,1)S(1)}, u32[]{:S(2)}, u32[]{:S(2)}) collective-permute-start(bf16[32,16,128]{2,1,0:T(8,128)(2,1)S(1)} %get-tuple-element.124), channel_id=1, source_target_pairs={{0,8},{1,9},{8,0},{9,1},{16,24},{17,25},{24,16},{25,17},{2,10},{3,... | collective-permute-start | bytes 393224 | tf_op jit(solution)/shard_map/ppermute | solution.py:457
  40.7 6.0 %collective-permute-start.15 = (bf16[32,16,128]{2,1,0:T(8,128)(2,1)S(1)}, bf16[32,16,128]{2,1,0:T(8,128)(2,1)S(1)}, u32[]{:S(2)}, u32[]{:S(2)}) collective-permute-start(bf16[32,16,128]{2,1,0:T(8,128)(2,1)S(1)} %get-tuple-element.119), channel_id=1, source_target_pairs={{0,1},{1,0},{2,4},{3,5},{4,2},{5,3},{6,7},{7,6},{8,9},{9,8},{10,12... | collective-permute-start | bytes 393224 | tf_op jit(solution)/shard_map/ppermute | solution.py:457
  40.8 6.0 %collective-permute-start.14 = (bf16[32,16,128]{2,1,0:T(8,128)(2,1)S(1)}, bf16[32,16,128]{2,1,0:T(8,128)(2,1)S(1)}, u32[]{:S(2)}, u32[]{:S(2)}) collective-permute-start(bf16[32,16,128]{2,1,0:T(8,128)(2,1)S(1)} %get-tuple-element.120), channel_id=1, source_target_pairs={{0,2},{1,3},{2,0},{3,1},{4,6},{5,7},{6,4},{7,5},{8,10},{9,11},{10,... | collective-permute-start | bytes 393224 | tf_op jit(solution)/shard_map/ppermute | solution.py:457
  48.2 10.5 %collective-permute-start.16 = (bf16[16,2,256,128]{3,2,1,0:T(8,128)(2,1)S(1)}, bf16[16,2,256,128]{3,2,1,0:T(8,128)(2,1)S(1)}, u32[]{:S(2)}, u32[]{:S(2)}) collective-permute-start(bf16[16,2,256,128]{3,2,1,0:T(8,128)(2,1)S(1)} %snapshot.1.own_ref), channel_id=1, source_target_pairs={{0,1},{1,0},{2,3},{3,2},{4,5},{5,4},{6,7},{7,6},{8,9},{9,8},{10,11... | collective-permute-start | bytes 6291464 | tf_op jit(solution)/shard_map/ppermute | solution.py:610
  48.3 4.7 %collective-permute-start.19 = (f32[32,64]{1,0:T(8,128)S(1)}, f32[32,64]{1,0:T(8,128)S(1)}, u32[]{:S(2)}, u32[]{:S(2)}) collective-permute-start(f32[32,64]{1,0:T(8,128)S(1)} %get-tuple-element.107.refs_0_), channel_id=1, source_target_pairs={{0,24},{8,16},{16,8},{24,0},{1,25},{9,17},{17,9},{25,1},{2,26},{10... | collective-permute-start | bytes 24584 | tf_op jit(solution)/shard_map/ppermute | solution.py:471
  49.8 3.7 %collective-permute-start.18 = (f32[32,64]{1,0:T(8,128)S(1)}, f32[32,64]{1,0:T(8,128)S(1)}, u32[]{:S(2)}, u32[]{:S(2)}) collective-permute-start(f32[32,64]{1,0:T(8,128)S(1)} %get-tuple-element.107.refs_0_), channel_id=1, source_target_pairs={{0,16},{8,24},{16,0},{24,8},{1,17},{9,25},{17,1},{25,9},{2,18},{10... | collective-permute-start | bytes 24584 | tf_op jit(solution)/shard_map/ppermute | solution.py:471
  50.5 3.7 %collective-permute-start.17 = (f32[32,64]{1,0:T(8,128)S(1)}, f32[32,64]{1,0:T(8,128)S(1)}, u32[]{:S(2)}, u32[]{:S(2)}) collective-permute-start(f32[32,64]{1,0:T(8,128)S(1)} %get-tuple-element.107.refs_0_), channel_id=1, source_target_pairs={{0,8},{8,0},{16,24},{24,16},{1,9},{9,1},{17,25},{25,17},{2,10},{10... | collective-permute-start | bytes 24584 | tf_op jit(solution)/shard_map/ppermute | solution.py:471
  54.2 6.6 %collective-permute-start.22 = (f32[32,64]{1,0:T(8,128)S(1)}, f32[32,64]{1,0:T(8,128)S(1)}, u32[]{:S(2)}, u32[]{:S(2)}) collective-permute-start(f32[32,64]{1,0:T(8,128)S(1)} %line_sum.1), channel_id=1, source_target_pairs={{0,6},{2,4},{4,2},{6,0},{1,7},{3,5},{5,3},{7,1},{8,14},{10,12},{12... | collective-permute-start | bytes 24584 | tf_op jit(solution)/shard_map/ppermute | solution.py:471
  56.0 4.8 %collective-permute-start.21 = (f32[32,64]{1,0:T(8,128)S(1)}, f32[32,64]{1,0:T(8,128)S(1)}, u32[]{:S(2)}, u32[]{:S(2)}) collective-permute-start(f32[32,64]{1,0:T(8,128)S(1)} %line_sum.1), channel_id=1, source_target_pairs={{0,4},{2,6},{4,0},{6,2},{1,5},{3,7},{5,1},{7,3},{8,12},{10,14},{12... | collective-permute-start | bytes 24584 | tf_op jit(solution)/shard_map/ppermute | solution.py:471
  56.2 4.7 %collective-permute-start.20 = (f32[32,64]{1,0:T(8,128)S(1)}, f32[32,64]{1,0:T(8,128)S(1)}, u32[]{:S(2)}, u32[]{:S(2)}) collective-permute-start(f32[32,64]{1,0:T(8,128)S(1)} %line_sum.1), channel_id=1, source_target_pairs={{0,2},{2,0},{4,6},{6,4},{1,3},{3,1},{5,7},{7,5},{8,10},{10,8},{12,... | collective-permute-start | bytes 24584 | tf_op jit(solution)/shard_map/ppermute | solution.py:471
  58.7 2.2 %copy-start.1 = (f32[64,32]{0,1:T(8,128)S(1)}, f32[64,32]{0,1:T(8,128)}, u32[]{:S(2)}) copy-start(f32[64,32]{0,1:T(8,128)} %param.11) | copy-start | bytes 24580
